TPU v7x, 32 devices: a whole 2x2x4 slice. The times are simulated.
32 devices in a mesh: dp: 8 (over z, y), bal: 4 (over x, core).
Axes of the slice: x: 2, y: 2, z: 4, core: 2. Of those that a mesh axis runs over, the one named last changes fastest.
Arguments:
- tokens: bfloat16 [4, 128, 225, 768], P(None, ('dp', 'bal')), may hold values from -6 to 6
- cotangent: bfloat16 [4, 128, 225, 768], P(None, ('dp', 'bal')), may hold values from -6 to 6
- counts: int32 [4, 128], P(None, ('dp', 'bal')), may hold values from 56 to 225, as said below
- rows: int32 [4, 128, 225], P(None, ('dp', 'bal')), may hold values from 0 to 14, as said below
- cols: int32 [4, 128, 225], P(None, ('dp', 'bal')), may hold values from 0 to 14, as said below
- present: int32 [4, 128], P(None, ('dp', 'bal')), may hold values 0 or 1
- slots: int32 [4, 128], P(None, ('dp', 'bal')), may hold values from 0 to 15, as said below
- first_gain: float32 [768], replicated, may hold values from 0.25 to 1.75
- first_shift: float32 [768], replicated, may hold values from -1.75 to 1.75
- qkv_weight: bfloat16 [768, 2304], replicated, may hold values from -0.21875 to 0.21875
- query_bias: float32 [768], replicated, may hold values from -1.75 to 1.75
- value_bias: float32 [768], replicated, may hold values from -1.75 to 1.75
- out_weight: bfloat16 [768, 768], replicated, may hold values from -0.625 to 0.625
- out_bias: float32 [768], replicated, may hold values from -1.75 to 1.75
- second_gain: float32 [768], replicated, may hold values from 0.25 to 1.75
- second_shift: float32 [768], replicated, may hold values from -1.75 to 1.75
- up_weight: bfloat16 [768, 3072], replicated, may hold values from -0.21875 to 0.21875
- up_bias: float32 [3072], replicated, may hold values from -1.75 to 1.75
- down_weight: bfloat16 [3072, 768], replicated, may hold values from -0.109375 to 0.109375
- down_bias: float32 [768], replicated, may hold values from -1.75 to 1.75
Outputs:
- block_output: bfloat16 [4, 128, 225, 768], P(None, ('dp', 'bal'))
- tokens_grad: float32 [4, 128, 225, 768], P(None, ('dp', 'bal'))
- first_gain_grad: float32 [768], replicated
- first_shift_grad: float32 [768], replicated
- qkv_weight_grad: float32 [768, 2304], P('dp')
- query_bias_grad: float32 [768], replicated
- value_bias_grad: float32 [768], replicated
- out_weight_grad: float32 [768, 768], P('dp')
- out_bias_grad: float32 [768], replicated
- second_gain_grad: float32 [768], replicated
- second_shift_grad: float32 [768], replicated
- up_weight_grad: float32 [768, 3072], P('dp')
- up_bias_grad: float32 [3072], replicated
- down_weight_grad: float32 [3072, 768], P('dp')
- down_bias_grad: float32 [768], replicated
Inputs may be any that keep to these rules, and one draw needn't show every extreme that they name: `counts`: every image has at least 56 visible patches; in every draw some image has all 225. In each image the pairs (rows, cols) over the 225 slots are the cells of a 15 x 15 grid, each once. `cols`: paired with rows as stated there. Within each aligned block of 16 images of a micro-batch the slots are a permutation of 0 to 15. Split such a block into runs of 4 images in order. For every pair of runs a and b, exactly one image of run a has a slot in [b * 4, (b + 1) * 4).
All inputs are finite; a program needn't handle non-finite values. No bound on the sum of `present` on one device may be relied on, other than what follows from the above.
Results may differ from a plain program's by a relative error of at most 0.014.
Values may be sent and summed in bfloat16 or wider, within the bound.
A program may use at most 512 MiB of HBM per device.

v0:
```python
import math

import jax
import jax.numpy as jnp
from jax import lax
from jax.sharding import PartitionSpec as P

HEADS = 12


norm_eps = 1e-06
masked_score = -1000000000.0
matrix_spots = (2, 5, 9, 11)
vector_spots = (0, 1, 3, 4, 6, 7, 8, 10, 12)


def normalize(values, norm_gain, norm_shift):
    average = jnp.mean(values, axis=-1, keepdims=True)
    centred = values - average
    spread = jnp.mean(centred * centred, axis=-1, keepdims=True)
    return centred * lax.rsqrt(spread + norm_eps) * norm_gain + norm_shift


def gelu_exact(values):
    return jax.nn.gelu(values, approximate=False)


def alibi_term(row_pos, col_pos, heads):
    row_f = row_pos.astype(jnp.float32)
    col_f = col_pos.astype(jnp.float32)
    row_gap = row_f[:, :, None] - row_f[:, None, :]
    col_gap = col_f[:, :, None] - col_f[:, None, :]
    distance = jnp.sqrt(row_gap * row_gap + col_gap * col_gap)
    slopes = jnp.exp2(-8.0 * (jnp.arange(heads, dtype=jnp.float32) + 1.0) / heads)
    return -slopes[None, :, None, None] * distance[:, None, :, :]


def matmul(left, right):
    return jnp.dot(left, right, preferred_element_type=jnp.float32)


def matmul_back(left, right):
    return lax.dot_general(
        left, right, (((1,), (1,)), ((), ())), preferred_element_type=jnp.float32
    )


def token_sum(left, right):
    return lax.dot_general(
        left, right, (((0,), (0,)), ((), ())), preferred_element_type=jnp.float32
    )


def scores_of(query_heads, key_heads, alibi, visible, scale):
    raw = (
        jnp.einsum("bqhd,bkhd->bhqk", query_heads, key_heads, preferred_element_type=jnp.float32)
        * scale
    )
    return jnp.where(visible[:, None, None, :] > 0, raw + alibi, masked_score)


def forward(images, alibi, visible, weights):
    (
        first_gain,
        first_shift,
        qkv_weight,
        query_bias,
        value_bias,
        out_weight,
        out_bias,
        second_gain,
        second_shift,
        up_weight,
        up_bias,
        down_weight,
        down_bias,
    ) = weights
    count, length, width = images.shape
    heads = alibi.shape[1]
    head_dim = width // heads
    flat_rows = count * length
    scale = 1.0 / math.sqrt(head_dim)
    inputs = images.astype(jnp.float32).reshape(flat_rows, width)
    normed_one, first_pull = jax.vjp(normalize, inputs, first_gain, first_shift)
    hidden_one = normed_one.astype(jnp.bfloat16)
    shift_all = jnp.concatenate([query_bias, jnp.zeros_like(query_bias), value_bias])
    projected = (matmul(hidden_one, qkv_weight) + shift_all).astype(jnp.bfloat16)
    split = projected.reshape(count, length, 3, heads, head_dim)
    query_heads = split[:, :, 0]
    key_heads = split[:, :, 1]
    value_heads = split[:, :, 2]
    scores = scores_of(query_heads, key_heads, alibi, visible, scale)
    row_max = jnp.max(scores, axis=-1, keepdims=True)
    exp_terms = jnp.exp(scores - row_max)
    row_total = jnp.sum(exp_terms, axis=-1, keepdims=True)
    probs = exp_terms / row_total
    log_total = row_max + jnp.log(row_total)
    probs_low = probs.astype(jnp.bfloat16)
    attended = (
        jnp.einsum("bhqk,bkhd->bqhd", probs_low, value_heads, preferred_element_type=jnp.float32)
        .astype(jnp.bfloat16)
        .reshape(flat_rows, width)
    )
    middle = inputs + (matmul(attended, out_weight) + out_bias)
    normed_two, second_pull = jax.vjp(normalize, middle, second_gain, second_shift)
    hidden_two = normed_two.astype(jnp.bfloat16)
    pre_act = matmul(hidden_two, up_weight) + up_bias
    activated, gelu_pull = jax.vjp(gelu_exact, pre_act)
    act_low = activated.astype(jnp.bfloat16)
    result = (middle + (matmul(act_low, down_weight) + down_bias)) * visible.reshape(flat_rows, 1)
    kept = (
        first_pull,
        hidden_one,
        query_heads,
        key_heads,
        value_heads,
        log_total,
        attended,
        second_pull,
        hidden_two,
        gelu_pull,
        act_low,
    )
    return (result.reshape(count, length, width), kept)


def backward(out_grad, kept, alibi, visible, weights):
    (
        first_gain,
        first_shift,
        qkv_weight,
        query_bias,
        value_bias,
        out_weight,
        out_bias,
        second_gain,
        second_shift,
        up_weight,
        up_bias,
        down_weight,
        down_bias,
    ) = weights
    (
        first_pull,
        hidden_one,
        query_heads,
        key_heads,
        value_heads,
        log_total,
        attended,
        second_pull,
        hidden_two,
        gelu_pull,
        act_low,
    ) = kept
    count, length, width = out_grad.shape
    heads = alibi.shape[1]
    head_dim = width // heads
    flat_rows = count * length
    scale = 1.0 / math.sqrt(head_dim)
    flat_grad = out_grad.reshape(flat_rows, width)
    down_low = flat_grad.astype(jnp.bfloat16)
    down_weight_grad = token_sum(act_low, down_low)
    down_bias_grad = jnp.sum(down_low, axis=0, dtype=jnp.float32)
    act_grad = matmul_back(down_low, down_weight)
    (pre_grad,) = gelu_pull(act_grad)
    pre_low = pre_grad.astype(jnp.bfloat16)
    up_weight_grad = token_sum(hidden_two, pre_low)
    up_bias_grad = jnp.sum(pre_low, axis=0, dtype=jnp.float32)
    hidden_two_grad = matmul_back(pre_low, up_weight)
    middle_part, second_gain_grad, second_shift_grad = second_pull(hidden_two_grad)
    middle_grad = flat_grad + middle_part
    branch_low = middle_grad.astype(jnp.bfloat16)
    out_weight_grad = token_sum(attended, branch_low)
    out_bias_grad = jnp.sum(branch_low, axis=0, dtype=jnp.float32)
    attended_grad = (
        matmul_back(branch_low, out_weight)
        .astype(jnp.bfloat16)
        .reshape(count, length, heads, head_dim)
    )
    scores = scores_of(query_heads, key_heads, alibi, visible, scale)
    probs = jnp.exp(scores - log_total)
    probs_low = probs.astype(jnp.bfloat16)
    prob_grad = jnp.einsum(
        "bqhd,bkhd->bhqk", attended_grad, value_heads, preferred_element_type=jnp.float32
    )
    value_grad = jnp.einsum(
        "bhqk,bqhd->bkhd", probs_low, attended_grad, preferred_element_type=jnp.float32
    )
    inner = jnp.sum(probs * prob_grad, axis=-1, keepdims=True)
    score_low = (probs * (prob_grad - inner)).astype(jnp.bfloat16)
    query_grad = (
        jnp.einsum("bhqk,bkhd->bqhd", score_low, key_heads, preferred_element_type=jnp.float32)
        * scale
    )
    key_grad = (
        jnp.einsum("bhqk,bqhd->bkhd", score_low, query_heads, preferred_element_type=jnp.float32)
        * scale
    )
    projected_grad = (
        jnp.stack([query_grad, key_grad, value_grad], axis=2)
        .astype(jnp.bfloat16)
        .reshape(flat_rows, 3 * width)
    )
    qkv_weight_grad = token_sum(hidden_one, projected_grad)
    shift_grad = jnp.sum(projected_grad, axis=0, dtype=jnp.float32)
    query_bias_grad = shift_grad[:width]
    value_bias_grad = shift_grad[2 * width :]
    hidden_one_grad = matmul_back(projected_grad, qkv_weight)
    input_part, first_gain_grad, first_shift_grad = first_pull(hidden_one_grad)
    input_grad = middle_grad + input_part
    grads = (
        first_gain_grad,
        first_shift_grad,
        qkv_weight_grad,
        query_bias_grad,
        value_bias_grad,
        out_weight_grad,
        out_bias_grad,
        second_gain_grad,
        second_shift_grad,
        up_weight_grad,
        up_bias_grad,
        down_weight_grad,
        down_bias_grad,
    )
    return (input_grad.reshape(count, length, width), grads)


def packing_table(slot_row, images):
    target_peer = slot_row // images
    ordinal = jnp.arange(images, dtype=jnp.int32)
    earlier = (target_peer[None, :] == target_peer[:, None]) & (ordinal[None, :] < ordinal[:, None])
    rank = jnp.sum(earlier.astype(jnp.int32), axis=1)
    group = images // (images // lax.axis_size("bal"))
    per_peer = images // group
    packed = target_peer * per_peer + rank
    return (packed[:, None] == ordinal[None, :]).astype(jnp.float32)


def placing_table(arrived_place, images):
    ordinal = jnp.arange(images, dtype=jnp.float32)
    return (arrived_place[:, None] == ordinal[None, :]).astype(jnp.float32)


def per_device(
    tokens,
    cotangent,
    counts,
    rows,
    cols,
    present,
    slots,
    first_gain,
    first_shift,
    qkv_weight,
    query_bias,
    value_bias,
    out_weight,
    out_bias,
    second_gain,
    second_shift,
    up_weight,
    up_bias,
    down_weight,
    down_bias,
):
    weights = (
        first_gain,
        first_shift,
        qkv_weight,
        query_bias,
        value_bias,
        out_weight,
        out_bias,
        second_gain,
        second_shift,
        up_weight,
        up_bias,
        down_weight,
        down_bias,
    )
    micro_count, images, length, width = tokens.shape
    group = lax.axis_size("bal")
    per_peer = images // group
    position = jnp.arange(length, dtype=jnp.int32)
    running_vectors = tuple((jnp.zeros(weights[spot].shape, jnp.float32) for spot in vector_spots))
    running_matrices = tuple((jnp.zeros(weights[spot].shape, jnp.float32) for spot in matrix_spots))
    row_shares = None
    outputs = []
    input_grads = []
    for micro_step in range(micro_count):
        visible_home = (position[None, :] < counts[micro_step][:, None]).astype(jnp.float32)
        live_home = visible_home * present[micro_step][:, None].astype(jnp.float32)
        slot_row = slots[micro_step]
        packing = packing_table(slot_row, images)
        packing_low = packing.astype(jnp.bfloat16)
        place_rows = jnp.broadcast_to(
            (slot_row % images).astype(jnp.float32)[:, None], (images, length)
        )
        alibi = alibi_term(rows[micro_step], cols[micro_step], HEADS)
        result, kept = forward(tokens[micro_step], alibi, visible_home, weights)
        result_low = result.astype(jnp.bfloat16)
        send_result = (
            jnp.einsum("ie,isd->esd", packing_low, result_low, preferred_element_type=jnp.float32)
            .astype(jnp.bfloat16)
            .reshape(group, per_peer, length, width)
        )
        send_places = (
            jnp.einsum(
                "ie,is->es",
                packing_low,
                place_rows.astype(jnp.bfloat16),
                preferred_element_type=jnp.float32,
            )
            .astype(jnp.bfloat16)
            .reshape(group, per_peer, length)
        )
        got_result, got_places = (
            lax.all_to_all(send_result, "bal", split_axis=0, concat_axis=0, tiled=True),
            lax.all_to_all(send_places, "bal", split_axis=0, concat_axis=0, tiled=True),
        )
        placing = placing_table(
            got_places.reshape(images, length)[:, 0].astype(jnp.float32), images
        )
        placing_low = placing.astype(jnp.bfloat16)
        outputs.append(
            jnp.einsum(
                "pl,psd->lsd",
                placing_low,
                got_result.reshape(images, length, width),
                preferred_element_type=jnp.float32,
            ).astype(jnp.bfloat16)
        )
        send_cot = (
            jnp.einsum(
                "pl,lsd->psd",
                placing_low,
                cotangent[micro_step],
                preferred_element_type=jnp.float32,
            )
            .astype(jnp.bfloat16)
            .reshape(group, per_peer, length, width)
        )
        got_cot = lax.all_to_all(send_cot, "bal", split_axis=0, concat_axis=0, tiled=True)
        home_cot = jnp.einsum(
            "ie,esd->isd",
            packing_low,
            got_cot.reshape(images, length, width),
            preferred_element_type=jnp.float32,
        )
        out_grad = home_cot * live_home[:, :, None]
        local_grad, grads = backward(out_grad, kept, alibi, visible_home, weights)
        input_grads.append(local_grad)
        running_vectors = tuple(
            (acc + grads[spot] for acc, spot in zip(running_vectors, vector_spots))
        )
        running_matrices = tuple(
            (acc + grads[spot] for acc, spot in zip(running_matrices, matrix_spots))
        )
    row_shares = (
        lax.psum_scatter(running_matrices[0], "dp", scatter_dimension=0, tiled=True),
        lax.psum_scatter(running_matrices[1], "dp", scatter_dimension=0, tiled=True),
        lax.psum_scatter(running_matrices[2], "dp", scatter_dimension=0, tiled=True),
        lax.psum_scatter(running_matrices[3], "dp", scatter_dimension=0, tiled=True),
    )
    qkv_rows, out_rows, up_rows, down_rows = (
        lax.psum(row_shares[0].astype(jnp.bfloat16), "bal").astype(jnp.float32),
        lax.psum(row_shares[1].astype(jnp.bfloat16), "bal").astype(jnp.float32),
        lax.psum(row_shares[2].astype(jnp.bfloat16), "bal").astype(jnp.float32),
        lax.psum(row_shares[3].astype(jnp.bfloat16), "bal").astype(jnp.float32),
    )
    vector_sums = lax.psum(
        (
            running_vectors[0],
            running_vectors[1],
            running_vectors[2],
            running_vectors[3],
            running_vectors[4],
            running_vectors[5],
            running_vectors[6],
            running_vectors[7],
            running_vectors[8],
        ),
        ("dp", "bal"),
    )
    return (
        jnp.stack(outputs),
        jnp.stack(input_grads),
        vector_sums[0],
        vector_sums[1],
        qkv_rows,
        vector_sums[2],
        vector_sums[3],
        out_rows,
        vector_sums[4],
        vector_sums[5],
        vector_sums[6],
        up_rows,
        vector_sums[7],
        down_rows,
        vector_sums[8],
    )


def solution(mesh):
    return jax.shard_map(
        per_device,
        mesh=mesh,
        in_specs=(
            P(None, ("dp", "bal"), None, None),
            P(None, ("dp", "bal"), None, None),
            P(None, ("dp", "bal")),
            P(None, ("dp", "bal"), None),
            P(None, ("dp", "bal"), None),
            P(None, ("dp", "bal")),
            P(None, ("dp", "bal")),
            P(),
            P(),
            P(),
            P(),
            P(),
            P(),
            P(),
            P(),
            P(),
            P(),
            P(),
            P(),
            P(),
        ),
        out_specs=(
            P(None, ("dp", "bal"), None, None),
            P(None, ("dp", "bal"), None, None),
            P(),
            P(),
            P("dp", None),
            P(),
            P(),
            P("dp", None),
            P(),
            P(),
            P(),
            P("dp", None),
            P(),
            P("dp", None),
            P(),
        ),
        check_vma=False,
    )
```

profile of v0, /device:TPU:0, one launch (start us, length us, event | category | flops | bytes accessed | tf_op | source)
XLA Modules:
  0.0 1524.1 jit_solution(5559305753679215103)
XLA Ops:
  77.0 9.3 reshape.1436
  142.4 9.3 reshape.1430
  179.4 10.3 fusion.253
  224.3 9.3 reshape.1424
  262.1 10.4 fusion.250
  296.9 9.3 reshape.1418
  345.3 8.8 add_convert_fusion.16
  354.3 108.0 %multiply_convert_fusion.7 = (bf16[900,3072]{1,0:T(8,128)(2,1)}, f32[900,3072]{1,0:T(8,128)}, bf16[900,3072]{1,0:T(8,128)(2,1)}, f32[900,3072]{1,0:T(8,128)}, bf...) fusion(f32[3072]{0:T(1024)S(1)} %copy-done.235, ...), kind=kOutput, calls=%fused_computation.80 | convolution fusion | flops 4980096000 | bytes 118101024 | tf_op jit(solution)/shard_map/dot_general | solution.py:39
  542.7 17.6 %convert_reduce_fusion = (f32[3072]{0:T(1024)}, bf16[900,3072]{1,0:T(8,128)(2,1)}) fusion(f32[900,3072]{1,0:T(8,128)} %get-tuple-element.214, bf16[3072,768]{1,0:T(8,128)(2,1)} %param.38, f32[900,768]{1,0:T(8,128)} %reshape.1454, f32[900,3072]{1,0:T(8,128)} %fusion.253, f32[3072]{0:T(1024)S(1)} %copy-done.236), kind=kOutput, calls=%fused_computation.33 | convolution fusion | flops 4294422528 | bytes 35155968 | tf_op jit(solution)/shard_map/dot_general | solution.py:43
  560.3 10.9 multiply_reduce_fusion.4
  585.1 15.9 %convert_reduce_fusion.1 = (f32[3072]{0:T(1024)}, bf16[900,3072]{1,0:T(8,128)(2,1)S(1)}) fusion(f32[900,3072]{1,0:T(8,128)} %get-tuple-element.216, bf16[3072,768]{1,0:T(8,128)(2,1)} %param.38, f32[900,768]{1,0:T(8,128)} %reshape.1450, f32[900,3072]{1,0:T(8,128)} %fusion.252, f32[3072]{0:T(1024)S(1)} %copy-done.237), kind=kOutput, calls=%fused_computation.34 | convolution fusion | flops 4294422528 | bytes 35155968 | tf_op jit(solution)/shard_map/dot_general | solution.py:43
  603.5 8.4 fusion.284
  625.1 16.1 %convert_reduce_fusion.2 = (f32[3072]{0:T(1024)}, bf16[900,3072]{1,0:T(8,128)(2,1)S(1)}) fusion(f32[900,3072]{1,0:T(8,128)} %get-tuple-element.218, bf16[3072,768]{1,0:T(8,128)(2,1)} %param.38, f32[900,768]{1,0:T(8,128)} %reshape.1446, f32[900,3072]{1,0:T(8,128)} %fusion.250, f32[3072]{0:T(1024)S(1)} %copy-done.238), kind=kOutput, calls=%fused_computation.35 | convolution fusion | flops 4294422528 | bytes 35155968 | tf_op jit(solution)/shard_map/dot_general | solution.py:43
  643.6 8.5 fusion.282
  660.9 16.3 %convert_reduce_fusion.3 = (f32[3072]{0:T(1024)}, bf16[900,3072]{1,0:T(8,128)(2,1)}) fusion(f32[900,3072]{1,0:T(8,128)} %get-tuple-element.170, bf16[3072,768]{1,0:T(8,128)(2,1)} %param.38, f32[900,768]{1,0:T(8,128)} %reshape.1442, f32[900,3072]{1,0:T(8,128)} %get-tuple-element.297, f32[3072]{0:T(1024)} %param.37), kind=kOutput, calls=%fused_computation.36 | convolution fusion | flops 4294422528 | bytes 35155968 | tf_op jit(solution)/shard_map/dot_general | solution.py:43
  677.2 17.0 %multiply_reduce_fusion.7 = (f32[768]{0:T(1024)}, f32[900]{0:T(1024)}, f32[768]{0:T(1024)}, f32[900]{0:T(1024)}, f32[900,768]{1,0:T(8,128)}, /*index=5*/f32[768]...) fusion(f32[900,768]{1,0:T(8,128)} %copy-done.13, ...), kind=kOutput, calls=%fused_computation.152 | convolution fusion | flops 4268151296 | bytes 35199696 | tf_op jit(solution)/shard_map/dot_general | solution.py:43
  716.5 9.2 multiply_reduce_fusion
  766.5 9.3 multiply_reduce_fusion.1
  799.7 7.9 fusion.51
  807.7 9.3 multiply_reduce_fusion.2
  849.0 9.3 multiply_reduce_fusion.3
  896.1 9.2 convert_element_type.939
  905.3 9.1 copy.611
  914.3 9.4 convert_element_type.928
  923.7 9.0 copy.600
  932.7 9.1 convert_element_type.917
  952.1 9.6 convert_element_type.906
  961.7 9.8 fusion.288
  983.9 11.1 add_add_fusion.2
  995.7 11.1 fusion.251
  1006.9 10.6 fusion.247
  1017.6 8.1 fusion.249
  1025.8 18.5 %add_add_fusion.1 = f32[768,3072]{1,0:T(8,128)} fusion(f32[768,3072]{1,0:T(8,128)} %fusion.251, f32[768,3072]{1,0:T(8,128)} %fusion.247, f32[768,3072]{1,0:T(8,128)} %fusion.249, bf16[900,3072]{1,0:T(8,128)(2,1)} %get-tuple-element.311, f32[900,768]{1,0:T(8,128)S(1)} %copy-done.78, f32[900]{0:T(1024)S(1)} %copy-done.196, f32[900]{0:T(1024)S(1)} %copy-done.161, ...), kind=kOutput, calls=%fused_computation.106 | convolution fusion | flops 4257266688 | bytes 46056480 | tf_op jit(solution)/shard_map/dot_general | solution.py:49
  1044.3 10.6 fusion.145
  1055.0 10.6 fusion.157
  1065.6 8.0 fusion.151
  1073.6 19.1 %add_add_fusion = f32[3072,768]{1,0:T(8,128)} fusion(f32[3072,768]{1,0:T(8,128)} %fusion.145, f32[3072,768]{1,0:T(8,128)} %fusion.157, f32[3072,768]{1,0:T(8,128)} %fusion.151, bf16[900,3072]{1,0:T(8,128)(2,1)} %get-tuple-element.213, f32[900,768]{1,0:T(8,128)S(1)} %copy-done.6), kind=kOutput, calls=%fused_computation.105 | convolution fusion | flops 4254501888 | bytes 46043136 | tf_op jit(solution)/shard_map/dot_general | solution.py:49
  1093.5 10.7 multiply_convert_fusion.8
  1115.2 10.5 multiply_convert_fusion.9
  1138.2 10.4 multiply_convert_fusion.10
  1161.1 10.5 multiply_convert_fusion.11
  1194.4 8.1 all-to-all-done.1
  1205.3 8.6 pad_maximum_fusion.1
  1214.0 9.2 multiply_reduce_fusion.8
  1234.6 15.6 %multiply_reduce_fusion.11 = (f32[768]{0:T(1024)}, f32[900]{0:T(1024)}, f32[768]{0:T(1024)}, f32[900]{0:T(1024)S(1)}, f32[900,768]{1,0:T(8,128)}, /*index=5*/f32...) fusion(f32[900,768]{1,0:T(8,128)} %reshape.1457, ...), kind=kOutput, calls=%fused_computation.160 | convolution fusion | flops 3206468096 | bytes 32637648 | tf_op jit(solution)/shard_map/dot_general | solution.py:43
  1261.0 10.0 fusion.258
  1319.0 140.6 %reduce-scatter.11.cloned.1.call-done = f32[384,768]{1,0:T(8,128)} async-done(((f32[3072,768]{1,0:T(8,128)}), f32[384,768]{1,0:T(8,128)}) %reduce-scatter.11.cloned.1.call-update) | async-done | bytes 1179664 | tf_op jit(solution)/shard_map/reduce_scatter | solution.py:365
  1466.4 41.9 %all-reduce = (f32[768]{0:T(1024)}, f32[768]{0:T(1024)}, f32[768]{0:T(1024)}, f32[768]{0:T(1024)}, f32[768]{0:T(1024)}, /*index=5*/f32[768]{0:T(1024)}, f32[768]{0:T(1024)}, f32[3072]{0:T(1024)}, f32[768]{0:T(1024)}) all-reduce(f32[768]{0:T(1024)} %add_add_fusion.30, ...), channel_id=1, replica_groups=mesh['dp'=8,'bal'=4] {'dp','bal'}, use_global_device_ids=true, to_apply=%region_52.53 | all-reduce | flops 9216 | bytes 73728 | tf_op jit(solution)/shard_map/psum | solution.py:373
  (872 shorter events, 728.1 us)
Async XLA Ops:
  7.2 55.6 %copy-start = (bf16[768,2304]{1,0:T(8,128)(2,1)S(1)}, bf16[768,2304]{1,0:T(8,128)(2,1)}, u32[]{:S(2)}) copy-start(bf16[768,2304]{1,0:T(8,128)(2,1)} %param.29) | copy-start | bytes 10616836
  13.5 449.7 %all-to-all-start.6 = ((bf16[4,1,225]{2,1,0:T(2,128)(2,1)}), bf16[4,1,225]{2,1,0:T(2,128)(2,1)}, u32[]{:S(2)}, u32[]{:S(2)}) async-start(bf16[4,1,225]{2,1,0:T(2,128)(2,1)} %copy.563), calls=%async_computation.6 | async-start | bytes 8192 | tf_op jit(solution)/shard_map/all_to_all | solution.py:321
  172.3 17.4 %slice-start.22 = ((s8[4718592]{0:T(1024)(128)(4,1)}), s8[4194304]{0:T(1024)(128)(4,1)S(1)}, s32[]{:S(2)}) async-start(s8[4718592]{0:T(1024)(128)(4,1)} %bitcast.491), calls=%async_computation.43 | async-start | bytes 8388608
  331.2 23.0 %copy-start.108 = (f32[900]{0:T(1024)}, f32[900]{0:T(1024)S(1)}, u32[]{:S(2)}) copy-start(f32[900]{0:T(1024)S(1)} %broadcast_multiply_fusion.7) | copy-start | bytes 10804
  333.7 20.6 %copy-start.116 = (f32[900]{0:T(1024)}, f32[900]{0:T(1024)S(1)}, u32[]{:S(2)}) copy-start(f32[900]{0:T(1024)S(1)} %fusion.175) | copy-start | bytes 10804
  354.2 108.1 %copy-start.220 = (s32[4]{0:T(128)S(1)}, s32[4]{0:T(128)}, u32[]{:S(2)}) copy-start(s32[4]{0:T(128)} %add.687) | copy-start | bytes 52
  354.2 108.1 %copy-start.228 = (bf16[4]{0:T(256)(128)(2,1)S(1)}, bf16[4]{0:T(256)(128)(2,1)}, u32[]{:S(2)}) copy-start(bf16[4]{0:T(256)(128)(2,1)} %get-tuple-element.263) | copy-start | bytes 28
  354.3 108.3 %copy-start.205 = (bf16[4,1,225]{2,0,1:T(4,128)(2,1)S(1)}, bf16[4,1,225]{2,0,1:T(4,128)(2,1)}, u32[]{:S(2)}) copy-start(bf16[4,1,225]{2,0,1:T(4,128)(2,1)} %fusion.138) | copy-start | bytes 5404
  354.3 108.9 %copy-start.209 = (s32[4]{0:T(128)S(1)}, s32[4]{0:T(128)}, u32[]{:S(2)}) copy-start(s32[4]{0:T(128)} %get-tuple-element.259) | copy-start | bytes 52
  354.3 108.9 %copy-start.230 = (s32[4]{0:T(128)S(1)}, s32[4]{0:T(128)}, u32[]{:S(2)}) copy-start(s32[4]{0:T(128)} %get-tuple-element.341) | copy-start | bytes 52
  463.2 7.6 all-to-all-start.4
  470.8 7.0 all-to-all-start.2
  477.8 7.7 all-to-all-start
  485.5 44.0 %all-to-all-start.11 = ((bf16[4,1,225,768]{3,2,1,0:T(8,128)(2,1)}), bf16[4,1,225,768]{3,2,1,0:T(8,128)(2,1)}, u32[]{:S(2)}, u32[]{:S(2)}) async-start(bf16[4,1,225,768]{3,2,1,0:T(8,128)(2,1)} %copy.612), calls=%async_computation.11 | async-start | bytes 2850816 | tf_op jit(solution)/shard_map/all_to_all | solution.py:345
  529.5 42.3 %all-to-all-start.10 = ((bf16[4,1,225,768]{3,2,1,0:T(8,128)(2,1)}), bf16[4,1,225,768]{3,2,1,0:T(8,128)(2,1)}, u32[]{:S(2)}, u32[]{:S(2)}) async-start(bf16[4,1,225,768]{3,2,1,0:T(8,128)(2,1)} %copy.601), calls=%async_computation.10 | async-start | bytes 2850816 | tf_op jit(solution)/shard_map/all_to_all | solution.py:345
  542.7 17.6 %copy-start.77 = (f32[900,768]{1,0:T(8,128)S(1)}, f32[900,768]{1,0:T(8,128)}, u32[]{:S(2)}) copy-start(f32[900,768]{1,0:T(8,128)} %copy-done.75) | copy-start | bytes 8294404
  542.7 17.6 %copy-start.160 = (f32[900]{0:T(1024)S(1)}, f32[900]{0:T(1024)}, u32[]{:S(2)}) copy-start(f32[900]{0:T(1024)} %copy-done.158) | copy-start | bytes 10804
  542.7 17.6 %copy-start.195 = (f32[900]{0:T(1024)S(1)}, f32[900]{0:T(1024)}, u32[]{:S(2)}) copy-start(f32[900]{0:T(1024)} %fusion.178) | copy-start | bytes 10804
  571.8 40.1 %all-to-all-start.9 = ((bf16[4,1,225,768]{3,2,1,0:T(8,128)(2,1)}), bf16[4,1,225,768]{3,2,1,0:T(8,128)(2,1)}, u32[]{:S(2)}, u32[]{:S(2)}) async-start(bf16[4,1,225,768]{3,2,1,0:T(8,128)(2,1)} %copy.590), calls=%async_computation.9 | async-start | bytes 2850816 | tf_op jit(solution)/shard_map/all_to_all | solution.py:345
  611.9 40.2 %all-to-all-start.8 = ((bf16[4,1,225,768]{3,2,1,0:T(8,128)(2,1)}), bf16[4,1,225,768]{3,2,1,0:T(8,128)(2,1)}, u32[]{:S(2)}, u32[]{:S(2)}) async-start(bf16[4,1,225,768]{3,2,1,0:T(8,128)(2,1)} %copy.579), calls=%async_computation.8 | async-start | bytes 2850816 | tf_op jit(solution)/shard_map/all_to_all | solution.py:345
  616.3 696.9 %reduce-scatter.7.cloned.1.call-start = ((), (), s32[]{:S(2)}) async-start(), calls=%async_computation.17 | async-start | bytes 2654208 | tf_op jit(solution)/shard_map/reduce_scatter | solution.py:363
  660.9 16.3 %copy-start.103 = (f32[900]{0:T(1024)S(1)}, f32[900]{0:T(1024)}, u32[]{:S(2)}) copy-start(f32[900]{0:T(1024)} %copy-done.102) | copy-start | bytes 10804
  660.9 16.3 %copy-start.106 = (f32[900]{0:T(1024)S(1)}, f32[900]{0:T(1024)}, u32[]{:S(2)}) copy-start(f32[900]{0:T(1024)} %copy-done.105) | copy-start | bytes 10804
  660.9 16.3 %copy-start.109 = (f32[900]{0:T(1024)S(1)}, f32[900]{0:T(1024)}, u32[]{:S(2)}) copy-start(f32[900]{0:T(1024)} %copy-done.108) | copy-start | bytes 10804
  708.7 17.1 %slice-start = ((s8[11403264]{0:T(1024)(128)(4,1)}), s8[4194304]{0:T(1024)(128)(4,1)S(1)}, s32[]{:S(2)}) async-start(s8[11403264]{0:T(1024)(128)(4,1)} %bitcast.469), calls=%async_computation.21 | async-start | bytes 8388608
  758.6 17.1 %slice-start.3 = ((s8[11403264]{0:T(1024)(128)(4,1)}), s8[4194304]{0:T(1024)(128)(4,1)S(1)}, s32[]{:S(2)}) async-start(s8[11403264]{0:T(1024)(128)(4,1)} %bitcast.471), calls=%async_computation.24 | async-start | bytes 8388608
  799.7 17.2 %slice-start.6 = ((s8[11403264]{0:T(1024)(128)(4,1)}), s8[4194304]{0:T(1024)(128)(4,1)S(1)}, s32[]{:S(2)}) async-start(s8[11403264]{0:T(1024)(128)(4,1)} %bitcast.473), calls=%async_computation.27 | async-start | bytes 8388608
  841.1 17.1 %slice-start.9 = ((s8[11403264]{0:T(1024)(128)(4,1)}), s8[4194304]{0:T(1024)(128)(4,1)S(1)}, s32[]{:S(2)}) async-start(s8[11403264]{0:T(1024)(128)(4,1)} %bitcast.475), calls=%async_computation.30 | async-start | bytes 8388608
  878.0 436.8 %reduce-scatter.5.cloned.1.call-start = ((), (), s32[]{:S(2)}) async-start(), calls=%async_computation.16 | async-start | bytes 7962624 | tf_op jit(solution)/shard_map/reduce_scatter | solution.py:362
  961.7 16.0 %slice-start.18 = ((s8[4718592]{0:T(1024)(128)(4,1)}), s8[4194304]{0:T(1024)(128)(4,1)S(1)}, s32[]{:S(2)}) async-start(s8[4718592]{0:T(1024)(128)(4,1)} %bitcast.483), calls=%async_computation.39 | async-start | bytes 8388608
  995.0 321.8 %reduce-scatter.9.cloned.1.call-start = ((), (), s32[]{:S(2)}) async-start(), calls=%async_computation.18 | async-start | bytes 10616832 | tf_op jit(solution)/shard_map/reduce_scatter | solution.py:364
  995.7 21.8 %slice-start.14 = ((s8[5554176]{0:T(1024)(128)(4,1)}), s8[4194304]{0:T(1024)(128)(4,1)S(1)}, s32[]{:S(2)}) async-start(s8[5554176]{0:T(1024)(128)(4,1)} %bitcast.479), calls=%async_computation.35 | async-start | bytes 8388608
  1044.3 415.3 %reduce-scatter.11.cloned.1.call-start = ((), (), s32[]{:S(2)}) async-start(), calls=%async_computation.19 | async-start | bytes 10616832 | tf_op jit(solution)/shard_map/reduce_scatter | solution.py:365
  1044.3 21.3 %slice-start.24 = ((s8[5554176]{0:T(1024)(128)(4,1)}), s8[4194304]{0:T(1024)(128)(4,1)S(1)}, s32[]{:S(2)}) async-start(s8[5554176]{0:T(1024)(128)(4,1)} %bitcast.493), calls=%async_computation.45 | async-start | bytes 8388608
  1110.8 22.9 %all-to-all-start.7 = ((bf16[4,1,225,768]{3,2,1,0:T(8,128)(2,1)}), bf16[4,1,225,768]{3,2,1,0:T(8,128)(2,1)}, u32[]{:S(2)}, u32[]{:S(2)}) async-start(bf16[4,1,225,768]{3,2,1,0:T(8,128)(2,1)} %copy.576), calls=%async_computation.7 | async-start | bytes 2850816 | tf_op jit(solution)/shard_map/all_to_all | solution.py:320
  1133.7 23.1 %all-to-all-start.5 = ((bf16[4,1,225,768]{3,2,1,0:T(8,128)(2,1)}), bf16[4,1,225,768]{3,2,1,0:T(8,128)(2,1)}, u32[]{:S(2)}, u32[]{:S(2)}) async-start(bf16[4,1,225,768]{3,2,1,0:T(8,128)(2,1)} %copy.560), calls=%async_computation.5 | async-start | bytes 2850816 | tf_op jit(solution)/shard_map/all_to_all | solution.py:320
  1156.8 22.9 %all-to-all-start.3 = ((bf16[4,1,225,768]{3,2,1,0:T(8,128)(2,1)}), bf16[4,1,225,768]{3,2,1,0:T(8,128)(2,1)}, u32[]{:S(2)}, u32[]{:S(2)}) async-start(bf16[4,1,225,768]{3,2,1,0:T(8,128)(2,1)} %copy.544), calls=%async_computation.3 | async-start | bytes 2850816 | tf_op jit(solution)/shard_map/all_to_all | solution.py:320
  1179.7 22.9 %all-to-all-start.1 = ((bf16[4,1,225,768]{3,2,1,0:T(8,128)(2,1)}), bf16[4,1,225,768]{3,2,1,0:T(8,128)(2,1)}, u32[]{:S(2)}, u32[]{:S(2)}) async-start(bf16[4,1,225,768]{3,2,1,0:T(8,128)(2,1)} %copy.528), calls=%async_computation.1 | async-start | bytes 2850816 | tf_op jit(solution)/shard_map/all_to_all | solution.py:320
  1184.0 326.5 %all-reduce.4.cloned.1.call-start = ((), (), s32[]{:S(2)}) async-start(), calls=%async_computation.20 | async-start | bytes 3538944 | tf_op jit(solution)/shard_map/psum | solution.py:368
  1190.9 23.0 %copy-start.151 = (f32[768]{0:T(1024)S(1)}, f32[768]{0:T(1024)}, u32[]{:S(2)}) copy-start(f32[768]{0:T(1024)} %param.27) | copy-start | bytes 9220
  1190.9 23.0 %copy-start.192 = (f32[900]{0:T(1024)S(1)}, f32[900]{0:T(1024)}, u32[]{:S(2)}) copy-start(f32[900]{0:T(1024)} %rsqrt.98) | copy-start | bytes 10804
  1190.9 23.0 %copy-start.193 = (f32[900]{0:T(1024)S(1)}, f32[900]{0:T(1024)}, u32[]{:S(2)}) copy-start(f32[900]{0:T(1024)} %div.298) | copy-start | bytes 10804
  1205.3 17.9 %slice-start.16 = ((s8[4718592]{0:T(1024)(128)(4,1)}), s8[4194304]{0:T(1024)(128)(4,1)S(1)}, s32[]{:S(2)}) async-start(s8[4718592]{0:T(1024)(128)(4,1)} %bitcast.481), calls=%async_computation.37 | async-start | bytes 8388608
  1205.3 23.5 %slice-start.20 = ((s8[4718592]{0:T(1024)(128)(4,1)}), s8[4194304]{0:T(1024)(128)(4,1)S(1)}, s32[]{:S(2)}) async-start(s8[4718592]{0:T(1024)(128)(4,1)} %bitcast.485), calls=%async_computation.41 | async-start | bytes 8388608
  1316.8 145.0 %copy-start.188 = (f32[768]{0:T(1024)S(1)}, f32[768]{0:T(1024)}, u32[]{:S(2)}) copy-start(f32[768]{0:T(1024)} %get-tuple-element.96) | copy-start | bytes 9220
  1316.8 146.2 %copy-start.187 = (f32[768]{0:T(1024)S(1)}, f32[768]{0:T(1024)}, u32[]{:S(2)}) copy-start(f32[768]{0:T(1024)} %get-tuple-element.117) | copy-start | bytes 9220
  1316.8 147.5 %copy-start.186 = (f32[768]{0:T(1024)S(1)}, f32[768]{0:T(1024)}, u32[]{:S(2)}) copy-start(f32[768]{0:T(1024)} %get-tuple-element.318) | copy-start | bytes 9220
  1316.8 149.6 %copy-start.177 = (f32[768]{0:T(1024)S(1)}, f32[768]{0:T(1024)}, u32[]{:S(2)}) copy-start(f32[768]{0:T(1024)} %add.761) | copy-start | bytes 9220
  (243 other events, 1360.6 us)
Sparse Core Ops, SparseCore 0:
  878.1 71.3 reduce-scatter.6
  995.2 131.4 reduce-scatter.4
  1130.6 162.4 reduce-scatter.8
  1297.0 162.5 reduce-scatter.10
  1463.4 47.0 all-reduce.3
where the time goes:
time: 1540 us; the launch traced here: 1520 us
  matrix products  680 us (44%)
  local copies, waits for them, and re-layouts  384 us (25%)
  other arithmetic  193 us (13%)
  waiting for transfers between devices  159 us (10%)
  starting transfers between devices  50.6 us (3%)
  blocking collectives  41.9 us (3%)
  between operations  16.5 us (1%)
    dot_general x16, matrix products, matmul(): return jnp.dot(left, right, preferred_element_type=jnp.float32)  226 us
    dot_general x16, matrix products, matmul_back(): lax.dot_general(left, right, (((1,), (1,)), ((), ())), preferred_element_...  156 us
    reduce_scatter x1, waiting for transfers between devices, per_device(): lax.psum_scatter(running_matrices[3], 'dp', scatter_dimension=0, tiled=True)  141 us
    dot_general x16, matrix products, token_sum(): lax.dot_general(left, right, (((0,), (0,)), ((), ())), preferred_element_...  137 us
    convert_element_type x8, local copies, waits for them, and re-layouts, backward(): projected_grad = jnp.stack([query_grad, key_grad, value_grad], axis=2).as...  68.7 us
    unnamed x557, local copies, waits for them, and re-layouts  44.2 us
    psum x1, blocking collectives, per_device(): lax.psum((running_vectors[0], running_vectors[1], running_vectors[2], run...  41.9 us
    reshape x4, local copies, waits for them, and re-layouts, forward(): split = projected.reshape(count, length, 3, heads, head_dim)  37.3 us
  transfers between devices with their start and end apart: 17, of which 9 were waited for; matrix products, arithmetic and copies ran while one was open for 65% of the time, Pallas kernels for 0%

commit v1 on v0

v1 whole, which is shorter than its diff:
```python
import functools
import math

import jax
import jax.numpy as jnp
from jax import lax
from jax.experimental import pallas as pl
from jax.experimental.pallas import tpu as pltpu
from jax.sharding import PartitionSpec as P

HEADS = 12
TILE = 256
WINDOW = 256
FAR = 1e12
EPS = 1e-06
VMEM_LIMIT = 60 * 1024 * 1024

F32 = jnp.float32
BF16 = jnp.bfloat16

OFF, CNT, IMG, LIVE, PEER, MISC = 0, 16, 32, 48, 64, 80
N_FWD, N_BWD, ROWS_FWD, ROWS_BWD, N_LIVE = MISC, MISC + 1, MISC + 2, MISC + 3, MISC + 4


def dot(a, b):
    return jnp.dot(a, b, preferred_element_type=F32)


def dot_bt(a, b):
    return lax.dot_general(a, b, (((1,), (1,)), ((), ())), preferred_element_type=F32)


def turned(block):
    size = 256 if block.shape[1] % 256 == 0 else 128
    row = lax.broadcasted_iota(jnp.int32, (size, size), 0)
    col = lax.broadcasted_iota(jnp.int32, (size, size), 1)
    eye = jnp.where(row == col, 1.0, 0.0).astype(BF16)
    parts = [
        dot_bt(eye, block[:, start : start + size]).astype(BF16)
        for start in range(0, block.shape[1], size)
    ]
    return parts[0] if len(parts) == 1 else jnp.concatenate(parts, axis=0)


def layer_norm(values):
    average = jnp.mean(values, axis=-1, keepdims=True)
    centred = values - average
    spread = jnp.mean(centred * centred, axis=-1, keepdims=True)
    inverse = lax.rsqrt(spread + EPS)
    return centred * inverse, inverse


def norm_back(out_grad, gain, unit, inverse):
    e = out_grad * gain
    mean_e = jnp.mean(e, axis=-1, keepdims=True)
    mean_eu = jnp.mean(e * unit, axis=-1, keepdims=True)
    return inverse * (e - mean_e - unit * mean_eu)


def gelu_parts(u):
    size = jnp.abs(u)
    t = 1.0 / (1.0 + (0.3275911 * math.sqrt(0.5)) * size)
    bell = jnp.exp(-0.5 * (u * u))
    poly = t * (
        0.5 * 0.254829592
        + t
        * (
            0.5 * -0.284496736
            + t * (0.5 * 1.421413741 + t * (0.5 * -1.453152027 + t * (0.5 * 1.061405429)))
        )
    )
    tail = poly * bell
    phi_sum = jnp.where(u >= 0, 1.0 - tail, tail)
    return phi_sum, u * bell * (1.0 / math.sqrt(2.0 * math.pi))


def row_ids(start, rows):
    return start + lax.broadcasted_iota(jnp.int32, (rows, 1), 0)


def aligned(value, step=16):
    return pl.multiple_of(value, step)


def by_count(count, run):
    @pl.when(count <= 128)
    def _():
        run(128, 128)

    @pl.when(jnp.logical_and(count > 128, count <= 192))
    def _():
        run(192, 256)

    @pl.when(count > 192)
    def _():
        run(256, 256)


def distances(spot_rows, spot_cols, count, keys, queries):
    down = spot_cols[:keys, 0:1] - spot_rows[0:1, :queries]
    across = spot_cols[:keys, 1:2] - spot_rows[1:2, :queries]
    far = row_ids(0, keys) >= count
    return jnp.where(far, FAR, jnp.sqrt(down * down + across * across))


def attend_kernel(
    meta, slopes, tokens, spot_rows, spot_cols, gain, shift, weight, bias,
    packed_out, qkv_out, att_out, total_out,
    packed, qkv, att, gaps, sem_packed, sem_qkv, sem_att,
):
    step = pl.program_id(0)
    images = pl.num_programs(0) // 2
    length, width = tokens.shape[1], tokens.shape[2]

    def tile_copy(which, t):
        src, dst, sem = (
            (packed, packed_out, sem_packed),
            (qkv, qkv_out, sem_qkv),
            (att, att_out, sem_att),
        )[which]
        rows = pl.ds(aligned(t * TILE, TILE), TILE)
        return pltpu.make_async_copy(src.at[rows], dst.at[rows], sem.at[t])

    @pl.when(step == 0)
    def _():
        packed[...] = jnp.zeros_like(packed)

    @pl.when(step < images)
    def _():
        off = aligned(meta[OFF + step])
        packed[pl.ds(off, length), :] = tokens[0]
        begin = off // TILE
        after = aligned(meta[OFF + jnp.minimum(step + 1, images - 1)])
        end = jnp.where(step == images - 1, meta[N_FWD], after // TILE)

        def project(t, carry):
            rows = pl.ds(aligned(t * TILE, TILE), TILE)
            unit, _ = layer_norm(packed[rows, :].astype(F32))
            hidden = (unit * gain[...] + shift[...]).astype(BF16)
            for part in range(3):
                cols = slice(part * width, (part + 1) * width)
                qkv[rows, cols] = (dot(hidden, weight[:, cols]) + bias[:, cols]).astype(BF16)
            tile_copy(0, t).start()
            tile_copy(1, t).start()
            return carry

        lax.fori_loop(begin, end, project, 0)

    @pl.when(step >= images)
    def _():
        spot = step - images
        off = aligned(meta[OFF + spot])
        count = meta[CNT + spot]

        def run(keys, queries):
            gaps[:keys, :queries] = distances(spot_rows[0], spot_cols[0], count, keys, queries)
            key_seen = row_ids(0, keys) < count
            query_seen = row_ids(0, queries) < count
            left = lax.broadcasted_iota(jnp.int32, (queries, 128), 1) < 64

            def pair(p, carry):
                lanes = aligned(p * 128, 128)
                q2 = qkv[pl.ds(off, queries), pl.ds(lanes, 128)] * 0.125
                k2 = qkv[pl.ds(off, keys), pl.ds(width + lanes, 128)]
                v2 = qkv[pl.ds(off, keys), pl.ds(2 * width + lanes, 128)]
                q2 = jnp.where(query_seen, q2, jnp.zeros_like(q2))
                k2 = jnp.where(key_seen, k2, jnp.zeros_like(k2))
                v2 = jnp.where(key_seen, v2, jnp.zeros_like(v2))
                v2t = turned(v2)
                outs = []
                for half in range(2):
                    head = 2 * p + half
                    mine = left if half == 0 else jnp.logical_not(left)
                    qh = jnp.where(mine, q2, jnp.zeros_like(q2))
                    scores = dot_bt(k2, qh) - slopes[head] * gaps[:keys, :queries]
                    top = jnp.max(scores, axis=0, keepdims=True)
                    terms = jnp.exp(scores - top)
                    total = jnp.sum(terms, axis=0, keepdims=True)
                    heads_out = dot(v2t[half * 64 : half * 64 + 64], terms.astype(BF16))
                    outs.append((heads_out * (1.0 / total)).astype(BF16))
                    total_out[0, p, half : half + 1, :queries] = top + jnp.log(total)
                both = jnp.concatenate(outs, axis=0)
                att[pl.ds(off, queries), pl.ds(lanes, 128)] = turned_back(both)
                return carry

            lax.fori_loop(0, HEADS // 2, pair, 0)

        by_count(count, run)
        after = meta[OFF + jnp.minimum(spot + 1, images - 1)]
        end = jnp.where(spot == images - 1, meta[N_FWD], after // TILE)

        def send(t, carry):
            tile_copy(2, t).start()
            return carry

        lax.fori_loop(off // TILE, end, send, 0)

    @pl.when(step == 2 * images - 1)
    def _():
        def finish(t, carry):
            for which in range(3):
                tile_copy(which, t).wait()
            return carry

        lax.fori_loop(0, meta[N_FWD], finish, 0)


def turned_back(block):
    size = block.shape[1]
    parts = []
    for start in range(0, size, 128):
        row = lax.broadcasted_iota(jnp.int32, (128, size), 0)
        col = lax.broadcasted_iota(jnp.int32, (128, size), 1)
        eye = jnp.where(row + start == col, 1.0, 0.0).astype(BF16)
        parts.append(dot_bt(eye, block).astype(BF16))
    return parts[0] if len(parts) == 1 else jnp.concatenate(parts, axis=0)


def mlp_kernel(
    chunk, meta, cot_in, att_in, tokens_in,
    out_w, out_b, gain, shift, up_w, up_b, down_w, down_b,
    y_send, mid_grad, att_grad, up_g, down_g, out_g, vec_g, upb_g,
    cot, y_all, up_acc, down_acc, out_acc, h2_s, h2t_s, dzt_s, z_s, g_s, stage, sem,
):
    step = pl.program_id(0)
    images = 16
    tiles = pl.num_programs(0) - 2 * images
    length, width = cot_in.shape[1], cot_in.shape[2]
    hidden = up_w.shape[1]

    @pl.when(step == 0)
    def _():
        up_acc[...] = jnp.zeros_like(up_acc)
        down_acc[...] = jnp.zeros_like(down_acc)
        out_acc[...] = jnp.zeros_like(out_acc)
        vec_g[...] = jnp.zeros_like(vec_g)
        upb_g[...] = jnp.zeros_like(upb_g)

    @pl.when(jnp.logical_and(step < images, step < meta[N_LIVE]))
    def _():
        spot = step
        off = aligned(meta[OFF + spot])
        seen = row_ids(0, length) < meta[CNT + spot]
        block = cot_in[0]
        edge = length // 16 * 16
        cot[pl.ds(aligned(off + edge), 16), :] = jnp.zeros((16, width), BF16)
        cot[pl.ds(off, length), :] = jnp.where(seen, block, jnp.zeros_like(block))

    def run_tile(t, both):
        rows = aligned(t * TILE, TILE)
        ids = row_ids(rows, TILE)
        att = att_in[...]
        att = jnp.where(ids < meta[ROWS_FWD], att, jnp.zeros_like(att))
        mid = tokens_in[...].astype(F32) + (dot(att, out_w[...]) + out_b[...])
        unit, inverse = layer_norm(mid)
        h2 = (unit * gain[...] + shift[...]).astype(BF16)
        h2_s[...] = h2
        z_s[...] = mid + down_b[...]
        if both:
            dz = cot[pl.ds(rows, TILE), :]
            dz = jnp.where(ids < meta[ROWS_BWD], dz, jnp.zeros_like(dz))
            h2t_s[...] = turned(h2)
            dzt_s[...] = turned(dz)
            g_s[...] = jnp.zeros_like(g_s)

        def part(c, carry):
            cols = pl.ds(aligned(c * chunk, chunk), chunk)
            pre = dot(h2_s[...], up_w[:, cols]) + up_b[:, cols]
            share, slope = gelu_parts(pre)
            act = (pre * share).astype(BF16)
            z_s[...] += dot(act, down_w[cols, :])
            if both:
                pre_g = (dot_bt(dz, down_w[cols, :]) * (share + slope)).astype(BF16)
                up_acc[:, cols] += dot(h2t_s[...], pre_g)
                down_acc[:, cols] += dot(dzt_s[...], act)
                upb_g[0:1, cols] += jnp.sum(pre_g.astype(F32), axis=0, keepdims=True)
                g_s[...] += dot_bt(pre_g, up_w[:, cols])
            return carry

        lax.fori_loop(0, hidden // chunk, part, 0)
        y_all[pl.ds(rows, TILE), :] = z_s[...].astype(BF16)
        if both:
            dzf = dz.astype(F32)
            g2 = g_s[...]
            dmid = dzf + norm_back(g2, gain[...], unit, inverse)
            branch = dmid.astype(BF16)
            mid_grad[...] = dmid
            att_grad[...] = dot_bt(branch, out_w[...]).astype(BF16)
            out_acc[...] += dot(turned(att), branch)
            vec_g[0:1, :] += jnp.sum(g2 * unit, axis=0, keepdims=True)
            vec_g[1:2, :] += jnp.sum(g2, axis=0, keepdims=True)
            vec_g[2:3, :] += jnp.sum(branch.astype(F32), axis=0, keepdims=True)
            vec_g[3:4, :] += jnp.sum(dzf, axis=0, keepdims=True)

    tile = step - images

    @pl.when(jnp.logical_and(tile >= 0, tile < meta[N_BWD]))
    def _():
        run_tile(tile, True)

    @pl.when(
        jnp.logical_and(
            jnp.logical_and(tile >= meta[N_BWD], tile >= 0),
            jnp.logical_and(tile < meta[N_FWD], tile < tiles),
        )
    )
    def _():
        run_tile(tile, False)

    @pl.when(step == images + tiles)
    def _():
        size = stage.shape[1]
        jobs = []
        for start in range(0, width, size):
            jobs.append((up_acc, start, up_g, False))
            jobs.append((out_acc, start, out_g, False))
        for start in range(0, hidden, size):
            jobs.append((down_acc, start, down_g, True))

        def copy(n):
            source, start, target, _ = jobs[n]
            columns = target.shape[1]
            return pltpu.make_async_copy(
                stage.at[n % 2, :, pl.ds(0, columns)], target.at[pl.ds(start, size)], sem.at[n % 2]
            )

        for n, (source, start, target, flip) in enumerate(jobs):
            if n >= 2:
                copy(n - 2).wait()
            if flip:
                for low in range(0, width, 256):
                    block = source[pl.ds(low, 256), pl.ds(start, size)].astype(BF16)
                    stage[n % 2, :, pl.ds(low, 256)] = turned(block)
            else:
                columns = target.shape[1]
                stage[n % 2, :, pl.ds(0, columns)] = source[pl.ds(start, size), :].astype(BF16)
            copy(n).start()
        copy(len(jobs) - 2).wait()
        copy(len(jobs) - 1).wait()

    spot = step - images - tiles

    @pl.when(spot >= 0)
    def _():
        off = aligned(meta[OFF + spot])
        seen = row_ids(0, length) < meta[CNT + spot]
        block = y_all[pl.ds(off, length), :]
        y_send[0] = jnp.where(seen, block, jnp.zeros_like(block))


def attend_back_kernel(
    meta, slopes, qkv, att_grad, totals, spot_rows, spot_cols, tokens, gain, shift,
    packed_grad, weight_g, bias_g,
    grads, gaps, acc, stage, sem,
):
    step = pl.program_id(0)
    images = 16
    width = tokens.shape[1]
    length = 225

    @pl.when(step == 0)
    def _():
        acc[...] = jnp.zeros_like(acc)
        bias_g[...] = jnp.zeros_like(bias_g)

    @pl.when(jnp.logical_and(step < images, step < meta[N_LIVE]))
    def _():
        spot = step
        off = aligned(meta[OFF + spot])
        count = meta[CNT + spot]

        def run(keys, queries):
            gaps[:keys, :queries] = distances(spot_rows[0], spot_cols[0], count, keys, queries)
            key_seen = row_ids(0, keys) < count
            query_seen = row_ids(0, queries) < count
            left = lax.broadcasted_iota(jnp.int32, (queries, 128), 1) < 64

            def pair(p, carry):
                lanes = aligned(p * 128, 128)
                q2 = qkv[:queries, pl.ds(lanes, 128)] * 0.125
                k2 = qkv[:keys, pl.ds(width + lanes, 128)]
                v2 = qkv[:keys, pl.ds(2 * width + lanes, 128)]
                o2 = att_grad[:queries, pl.ds(lanes, 128)]
                q2 = jnp.where(query_seen, q2, jnp.zeros_like(q2))
                o2 = jnp.where(query_seen, o2, jnp.zeros_like(o2))
                k2 = jnp.where(key_seen, k2, jnp.zeros_like(k2))
                v2 = jnp.where(key_seen, v2, jnp.zeros_like(v2))
                k2t = turned(k2)
                dq_parts = []
                dk = dv = None
                for half in range(2):
                    head = 2 * p + half
                    mine = left if half == 0 else jnp.logical_not(left)
                    qh = jnp.where(mine, q2, jnp.zeros_like(q2))
                    oh = jnp.where(mine, o2, jnp.zeros_like(o2))
                    scores = dot_bt(k2, qh) - slopes[head] * gaps[:keys, :queries]
                    probs = jnp.exp(scores - totals[0, p, half : half + 1, :queries])
                    prob_g = dot_bt(v2, oh)
                    inner = jnp.sum(probs * prob_g, axis=0, keepdims=True)
                    score_g = (probs * (prob_g - inner)).astype(BF16)
                    dv_part = dot(probs.astype(BF16), oh)
                    dk_part = dot(score_g, qh)
                    dq_parts.append(
                        (dot(k2t[half * 64 : half * 64 + 64], score_g) * 0.125).astype(BF16)
                    )
                    dk = dk_part if dk is None else dk + dk_part
                    dv = dv_part if dv is None else dv + dv_part
                dq = turned_back(jnp.concatenate(dq_parts, axis=0))
                grads[pl.ds(off, queries), pl.ds(lanes, 128)] = dq
                grads[pl.ds(off, keys), pl.ds(width + lanes, 128)] = dk.astype(BF16)
                grads[pl.ds(off, keys), pl.ds(2 * width + lanes, 128)] = dv.astype(BF16)
                return carry

            lax.fori_loop(0, HEADS // 2, pair, 0)

        by_count(count, run)

    tile = step - images

    @pl.when(jnp.logical_and(tile >= 0, tile < meta[N_BWD]))
    def _():
        rows = aligned(tile * TILE, TILE)
        ids = row_ids(rows, TILE)
        unit, _ = layer_norm(tokens[...].astype(F32))
        hidden = (unit * gain[...] + shift[...]).astype(BF16)
        hidden_t = turned(hidden)
        for part in range(3):
            cols = slice(part * width, (part + 1) * width)
            block = grads[pl.ds(rows, TILE), cols]
            block = jnp.where(ids < meta[ROWS_BWD], block, jnp.zeros_like(block))
            packed_grad[:, cols] = block
            acc[:, cols] += dot(hidden_t, block)
            bias_g[0:1, cols] += jnp.sum(block.astype(F32), axis=0, keepdims=True)

    @pl.when(step == pl.num_programs(0) - 1)
    def _():
        size = stage.shape[1]
        count = width // size

        def copy(n):
            return pltpu.make_async_copy(
                stage.at[n % 2], weight_g.at[pl.ds(n * size, size)], sem.at[n % 2]
            )

        for n in range(count):
            if n >= 2:
                copy(n - 2).wait()
            stage[n % 2] = acc[pl.ds(n * size, size), :].astype(BF16)
            copy(n).start()
        copy(count - 2).wait()
        copy(count - 1).wait()


def token_grad_kernel(
    meta, packed_grad, tokens, mid_grad, gain, weight, out, vec_g, held,
):
    step = pl.program_id(0)
    images = 16
    tiles = pl.num_programs(0) - images
    length = out.shape[1]

    @pl.when(step == 0)
    def _():
        vec_g[...] = jnp.zeros_like(vec_g)

    @pl.when(jnp.logical_and(step < tiles, step < meta[N_BWD]))
    def _():
        rows = aligned(step * TILE, TILE)
        unit, inverse = layer_norm(tokens[...].astype(F32))
        g1 = dot_bt(packed_grad[...], weight[...])
        held[pl.ds(rows, TILE), :] = mid_grad[...] + norm_back(g1, gain[...], unit, inverse)
        vec_g[0:1, :] += jnp.sum(g1 * unit, axis=0, keepdims=True)
        vec_g[1:2, :] += jnp.sum(g1, axis=0, keepdims=True)

    @pl.when(step >= tiles)
    def _():
        spot = step - tiles
        off = aligned(meta[OFF + spot])
        limit = meta[CNT + spot] * meta[LIVE + spot]
        block = held[pl.ds(off, length), :]
        out[0] = jnp.where(row_ids(0, length) < limit, block, 0.0)


def move_kernel(table, source, target):
    del table
    target[...] = source[...]


def move_images(source, table):
    count, length, width = source.shape
    return pl.pallas_call(
        move_kernel,
        out_shape=jax.ShapeDtypeStruct(source.shape, source.dtype),
        grid_spec=pltpu.PrefetchScalarGridSpec(
            num_scalar_prefetch=1,
            grid=(count,),
            in_specs=[pl.BlockSpec((1, length, width), lambda s, table: (table[s], 0, 0))],
            out_specs=pl.BlockSpec((1, length, width), lambda s, table: (s, 0, 0)),
        ),
    )(table, source)


def whole(*shape):
    return pl.BlockSpec(shape, lambda *_: (0,) * len(shape), pipeline_mode=pl.Buffered(1))


def params():
    return pltpu.CompilerParams(vmem_limit_bytes=VMEM_LIMIT)


def make_meta(counts, present, peer):
    images = counts.shape[0]
    ordinal = jnp.arange(images, dtype=jnp.int32)
    padded = (counts + 15) // 16 * 16
    key = (1 - present) * images + ordinal
    before = (key[None, :] < key[:, None]).astype(jnp.int32)
    place = jnp.sum(before, axis=1)
    start = jnp.sum(before * padded[None, :], axis=1)
    pick = (place[None, :] == ordinal[:, None]).astype(jnp.int32)

    def ordered(values):
        return jnp.sum(pick * values[None, :], axis=1)

    rows_fwd = jnp.sum(padded)
    rows_bwd = jnp.sum(padded * present)
    misc = jnp.stack(
        [
            (rows_fwd + TILE - 1) // TILE,
            (rows_bwd + TILE - 1) // TILE,
            rows_fwd,
            rows_bwd,
            jnp.sum(present),
        ]
    )
    return jnp.concatenate(
        [
            ordered(start),
            ordered(counts),
            ordered(ordinal),
            ordered(present),
            ordered(peer),
            jnp.pad(misc, (0, 11)),
        ]
    ).astype(jnp.int32)


def first_half(meta, slopes, tokens, spot_rows, spot_cols, gain, shift, weight, bias):
    images, length, width = tokens.shape
    full = images * ((length + 15) // 16 * 16)
    tiles = -(-full // TILE)
    rows = tiles * TILE + WINDOW
    last = images - 1

    def by_spot(step, meta, slopes):
        return (meta[IMG + jnp.maximum(step - images, 0)], 0, 0)

    return pl.pallas_call(
        attend_kernel,
        out_shape=(
            jax.ShapeDtypeStruct((rows, width), BF16),
            jax.ShapeDtypeStruct((rows, 3 * width), BF16),
            jax.ShapeDtypeStruct((rows, width), BF16),
            jax.ShapeDtypeStruct((images, HEADS // 2, 8, WINDOW), F32),
        ),
        grid_spec=pltpu.PrefetchScalarGridSpec(
            num_scalar_prefetch=2,
            grid=(2 * images,),
            in_specs=[
                pl.BlockSpec(
                    (1, length, width), lambda s, meta, sl: (meta[IMG + jnp.minimum(s, last)], 0, 0)
                ),
                pl.BlockSpec((1, 8, WINDOW), by_spot),
                pl.BlockSpec((1, WINDOW, 128), by_spot),
                whole(1, width),
                whole(1, width),
                whole(width, 3 * width),
                whole(1, 3 * width),
            ],
            out_specs=[
                pl.BlockSpec(memory_space=pl.ANY),
                pl.BlockSpec(memory_space=pl.ANY),
                pl.BlockSpec(memory_space=pl.ANY),
                pl.BlockSpec(
                    (1, HEADS // 2, 8, WINDOW),
                    lambda s, meta, sl: (jnp.maximum(s - images, 0), 0, 0, 0),
                ),
            ],
            scratch_shapes=[
                pltpu.VMEM((rows, width), BF16),
                pltpu.VMEM((rows, 3 * width), BF16),
                pltpu.VMEM((rows, width), BF16),
                pltpu.VMEM((WINDOW, WINDOW), F32),
                pltpu.SemaphoreType.DMA((tiles,)),
                pltpu.SemaphoreType.DMA((tiles,)),
                pltpu.SemaphoreType.DMA((tiles,)),
            ],
        ),
        compiler_params=params(),
    )(meta, slopes, tokens, spot_rows, spot_cols, gain, shift, weight, bias)


def mlp(meta, cot, att, packed, out_w, out_b, gain, shift, up_w, up_b, down_w, down_b):
    images, length, width = cot.shape
    rows = packed.shape[0]
    tiles = (rows - WINDOW) // TILE
    hidden = up_w.shape[1]
    stage_rows = 256
    last = images - 1

    def fwd_tile(s, meta):
        return (jnp.clip(s - images, 0, meta[N_FWD] - 1), 0)

    def bwd_tile(s, meta):
        return (jnp.clip(s - images, 0, jnp.maximum(meta[N_BWD] - 1, 0)), 0)

    return pl.pallas_call(
        functools.partial(mlp_kernel, 512),
        out_shape=(
            jax.ShapeDtypeStruct((images, length, width), BF16),
            jax.ShapeDtypeStruct((rows, width), F32),
            jax.ShapeDtypeStruct((rows, width), BF16),
            jax.ShapeDtypeStruct((width, hidden), BF16),
            jax.ShapeDtypeStruct((hidden, width), BF16),
            jax.ShapeDtypeStruct((width, width), BF16),
            jax.ShapeDtypeStruct((8, width), F32),
            jax.ShapeDtypeStruct((8, hidden), F32),
        ),
        grid_spec=pltpu.PrefetchScalarGridSpec(
            num_scalar_prefetch=1,
            grid=(2 * images + tiles,),
            in_specs=[
                pl.BlockSpec(
                    (1, length, width), lambda s, meta: (meta[PEER + jnp.minimum(s, last)], 0, 0)
                ),
                pl.BlockSpec((TILE, width), fwd_tile),
                pl.BlockSpec((TILE, width), fwd_tile),
                whole(width, width),
                whole(1, width),
                whole(1, width),
                whole(1, width),
                whole(width, hidden),
                whole(1, hidden),
                whole(hidden, width),
                whole(1, width),
            ],
            out_specs=[
                pl.BlockSpec(
                    (1, length, width),
                    lambda s, meta: (meta[PEER + jnp.clip(s - images - tiles, 0, last)], 0, 0),
                ),
                pl.BlockSpec((TILE, width), bwd_tile),
                pl.BlockSpec((TILE, width), bwd_tile),
                pl.BlockSpec(memory_space=pl.ANY),
                pl.BlockSpec(memory_space=pl.ANY),
                pl.BlockSpec(memory_space=pl.ANY),
                whole(8, width),
                whole(8, hidden),
            ],
            scratch_shapes=[
                pltpu.VMEM((rows, width), BF16),
                pltpu.VMEM((rows, width), BF16),
                pltpu.VMEM((width, hidden), F32),
                pltpu.VMEM((width, hidden), F32),
                pltpu.VMEM((width, width), F32),
                pltpu.VMEM((TILE, width), BF16),
                pltpu.VMEM((width, TILE), BF16),
                pltpu.VMEM((width, TILE), BF16),
                pltpu.VMEM((TILE, width), F32),
                pltpu.VMEM((TILE, width), F32),
                pltpu.VMEM((2, stage_rows, hidden), BF16),
                pltpu.SemaphoreType.DMA((2,)),
            ],
        ),
        compiler_params=params(),
    )(meta, cot, att, packed, out_w, out_b, gain, shift, up_w, up_b, down_w, down_b)


def attend_back(meta, slopes, qkv, att_grad, totals, spot_rows, spot_cols, packed, gain, shift):
    images = totals.shape[0]
    rows, width = packed.shape
    tiles = (rows - WINDOW) // TILE
    last = images - 1

    def spot_of(s, meta):
        return jnp.clip(s, 0, jnp.maximum(jnp.minimum(last, meta[N_LIVE] - 1), 0))

    def by_offset(s, meta, slopes):
        return (aligned(meta[OFF + spot_of(s, meta)]), 0)

    def by_spot(s, meta, slopes):
        return (spot_of(s, meta), 0, 0, 0)

    def by_image(s, meta, slopes):
        return (meta[IMG + spot_of(s, meta)], 0, 0)

    def bwd_tile(s, meta, slopes):
        return (jnp.clip(s - images, 0, jnp.maximum(meta[N_BWD] - 1, 0)), 0)

    return pl.pallas_call(
        attend_back_kernel,
        out_shape=(
            jax.ShapeDtypeStruct((rows, 3 * width), BF16),
            jax.ShapeDtypeStruct((width, 3 * width), BF16),
            jax.ShapeDtypeStruct((8, 3 * width), F32),
        ),
        grid_spec=pltpu.PrefetchScalarGridSpec(
            num_scalar_prefetch=2,
            grid=(images + tiles,),
            in_specs=[
                pl.BlockSpec((pl.Element(WINDOW), pl.Element(3 * width)), by_offset),
                pl.BlockSpec((pl.Element(WINDOW), pl.Element(width)), by_offset),
                pl.BlockSpec((1, HEADS // 2, 8, WINDOW), by_spot),
                pl.BlockSpec((1, 8, WINDOW), by_image),
                pl.BlockSpec((1, WINDOW, 128), by_image),
                pl.BlockSpec((TILE, width), bwd_tile),
                whole(1, width),
                whole(1, width),
            ],
            out_specs=[
                pl.BlockSpec((TILE, 3 * width), bwd_tile),
                pl.BlockSpec(memory_space=pl.ANY),
                whole(8, 3 * width),
            ],
            scratch_shapes=[
                pltpu.VMEM((rows, 3 * width), BF16),
                pltpu.VMEM((WINDOW, WINDOW), F32),
                pltpu.VMEM((width, 3 * width), F32),
                pltpu.VMEM((2, 256, 3 * width), BF16),
                pltpu.SemaphoreType.DMA((2,)),
            ],
        ),
        compiler_params=params(),
    )(meta, slopes, qkv, att_grad, totals, spot_rows, spot_cols, packed, gain, shift)


def token_grad(meta, packed_grad, packed, mid_grad, gain, weight, images, length):
    rows, width = packed.shape
    tiles = (rows - WINDOW) // TILE
    last = images - 1

    def bwd_tile(s, meta):
        return (jnp.clip(s, 0, jnp.maximum(meta[N_BWD] - 1, 0)), 0)

    return pl.pallas_call(
        token_grad_kernel,
        out_shape=(
            jax.ShapeDtypeStruct((images, length, width), F32),
            jax.ShapeDtypeStruct((8, width), F32),
        ),
        grid_spec=pltpu.PrefetchScalarGridSpec(
            num_scalar_prefetch=1,
            grid=(images + tiles,),
            in_specs=[
                pl.BlockSpec((TILE, 3 * width), bwd_tile),
                pl.BlockSpec((TILE, width), bwd_tile),
                pl.BlockSpec((TILE, width), bwd_tile),
                whole(1, width),
                whole(width, 3 * width),
            ],
            out_specs=[
                pl.BlockSpec(
                    (1, length, width),
                    lambda s, meta: (meta[IMG + jnp.clip(s - tiles, 0, last)], 0, 0),
                ),
                whole(8, width),
            ],
            scratch_shapes=[pltpu.VMEM((rows, width), F32)],
        ),
        compiler_params=params(),
    )(meta, packed_grad, packed, mid_grad, gain, weight)


def prepare(counts, rows, cols, present, peer):
    images, length = rows.shape
    meta = make_meta(counts, present, peer)
    spots = jnp.stack([rows, cols], axis=1).astype(F32)
    spot_rows = jnp.pad(spots, ((0, 0), (0, 6), (0, WINDOW - length)))
    spot_cols = jnp.pad(
        jnp.swapaxes(spots, 1, 2), ((0, 0), (0, WINDOW - length), (0, 126))
    )
    slopes = jnp.exp2(-8.0 * (jnp.arange(HEADS, dtype=F32) + 1.0) / HEADS)
    return meta, spot_rows, spot_cols, jnp.pad(slopes, (0, 4))


def line(vector):
    return vector.reshape(1, -1)


def per_device(
    tokens,
    cotangent,
    counts,
    rows,
    cols,
    present,
    slots,
    first_gain,
    first_shift,
    qkv_weight,
    query_bias,
    value_bias,
    out_weight,
    out_bias,
    second_gain,
    second_shift,
    up_weight,
    up_bias,
    down_weight,
    down_bias,
):
    steps, images, length, width = tokens.shape
    hidden = up_weight.shape[1]
    group = lax.axis_size("bal")
    total = steps * images
    step_ids = jnp.arange(steps, dtype=jnp.int32)

    peer = slots // images * steps + step_ids[:, None]
    every = lax.all_gather(slots, "bal")
    here = (every // images == lax.axis_index("bal")).astype(jnp.int32)
    place = jnp.sum(here * (every % images), axis=2)
    send_cot_from = (step_ids[None, :] * images + place).reshape(total)
    source = jnp.arange(group, dtype=jnp.int32)[:, None] * steps + step_ids[None, :]
    lands = (place.T[:, None, :] == jnp.arange(images, dtype=jnp.int32)[None, :, None]).astype(jnp.int32)
    take_from = jnp.sum(lands * source.T[:, None, :], axis=2).reshape(total)

    meta, spot_rows, spot_cols, slopes = prepare(
        counts.reshape(total),
        rows.reshape(total, length),
        cols.reshape(total, length),
        present.reshape(total),
        peer.reshape(total),
    )

    def exchange(blocks):
        return lax.all_to_all(blocks, "bal", split_axis=0, concat_axis=0, tiled=True)

    cot_send = move_images(cotangent.reshape(total, length, width), send_cot_from)
    cot_home = exchange(cot_send.reshape(group, steps, length, width)).reshape(total, length, width)
    shift_all = jnp.concatenate([query_bias, jnp.zeros_like(query_bias), value_bias])
    packed, qkv, att, totals = first_half(
        meta, slopes, tokens.reshape(total, length, width), spot_rows, spot_cols,
        line(first_gain), line(first_shift), qkv_weight, line(shift_all),
    )
    y_send, mid_grad, att_grad, up_g, down_g, out_g, vec_two, upb_g = mlp(
        meta, cot_home, att, packed, out_weight, line(out_bias), line(second_gain),
        line(second_shift), up_weight, line(up_bias), down_weight, line(down_bias),
    )
    y_got = exchange(y_send.reshape(group, steps, length, width)).reshape(total, length, width)

    def over_dp(matrix):
        return lax.psum_scatter(matrix, "dp", scatter_dimension=0, tiled=True)

    up_rows, down_rows, out_rows = over_dp(up_g), over_dp(down_g), over_dp(out_g)
    packed_grad, qkv_g, bias_g = attend_back(
        meta, slopes, qkv, att_grad, totals, spot_rows, spot_cols, packed,
        line(first_gain), line(first_shift),
    )
    qkv_rows = over_dp(qkv_g)
    input_grad, vec_one = token_grad(
        meta, packed_grad, packed, mid_grad, line(first_gain), qkv_weight, total, length
    )
    qkv_rows, out_rows, up_rows, down_rows = [
        lax.psum(share, "bal").astype(F32) for share in (qkv_rows, out_rows, up_rows, down_rows)
    ]
    vectors = lax.psum(
        jnp.concatenate(
            [vec_one[0], vec_one[1], bias_g[0], vec_two[0], vec_two[1], vec_two[2], vec_two[3], upb_g[0]]
        ),
        ("dp", "bal"),
    )

    def vector(n):
        return vectors[n * width : (n + 1) * width]

    output = move_images(y_got, take_from)
    return (
        output.reshape(steps, images, length, width),
        input_grad.reshape(steps, images, length, width),
        vector(0),
        vector(1),
        qkv_rows,
        vector(2),
        vector(4),
        out_rows,
        vector(7),
        vector(5),
        vector(6),
        up_rows,
        vectors[9 * width : 9 * width + hidden],
        down_rows,
        vector(8),
    )


def solution(mesh):
    images = P(None, ("dp", "bal"), None, None)
    spots = P(None, ("dp", "bal"), None)
    flags = P(None, ("dp", "bal"))
    matrix = P("dp", None)
    return jax.shard_map(
        per_device,
        mesh=mesh,
        in_specs=(images, images, flags, spots, spots, flags, flags) + (P(),) * 13,
        out_specs=(
            images, images, P(), P(), matrix, P(), P(), matrix, P(), P(), P(), matrix, P(), matrix, P(),
        ),
        check_vma=False,
    )
```

time: 1540 us -> 831 us (0.54)
  matrix products: 680 us -> 0 us
  Pallas kernels: 0 us -> 403 us
  local copies, waits for them, and re-layouts: 384 us -> 77.4 us
  other arithmetic: 193 us -> 12.4 us
  waiting for transfers between devices: 159 us -> 241 us
  starting transfers between devices: 50.6 us -> 23.3 us
    dot_general x92 -> x0, matrix products: 680 us -> none  [the longest x16 226 us: matmul(): return jnp.dot(left, right, preferred_element_type=jnp.float32)]
    pallas_call x0 -> x6, Pallas kernels: none -> 403 us  [the longest x1 166 us: mlp(): pl.pallas_call(functools.partial(mlp_kernel, 512), out_shape=(jax.ShapeDt...]
    convert_element_type x44 -> x0, local copies, waits for them, and re-layouts: 173 us -> none  [the longest x8 68.7 us: backward(): projected_grad = jnp.stack([query_grad, key_grad, value_grad], axis=2).as...]
    reduce_scatter x4, waiting for transfers between devices: 141 us -> 239 us  [over_dp(): return lax.psum_scatter(matrix, 'dp', scatter_dimension=0, tiled=True)]
    reshape x28 -> x12, local copies, waits for them, and re-layouts: 97.8 us -> 19.3 us  [the longest x1 7.2 us: per_device(): y_send.reshape(group, steps, length, width)]
    reduce_sum x22 -> x5, other arithmetic: 62.7 us -> 1.34 us  [the longest x1 0.67 us: make_meta(): jnp.sum(present)]
    convert_element_type x20 -> x4, other arithmetic: 61.5 us -> 7.95 us  [per_device(): lax.psum(share, 'bal').astype(F32)]
    add x20 -> x2, other arithmetic: 33.2 us -> 0.02 us  [the longest x1 0.01 us: per_device(): peer = slots // images * steps + step_ids[:, None]]
  transfers between devices with their start and end apart: 17 -> 7, of which waited for: 9 -> 3; matrix products, arithmetic and copies ran while one was open for 65% -> 8% of each run, Pallas kernels for 0% -> 27%
where the time goes in v1:
time: 831 us; the launch traced here: 820 us
  Pallas kernels  403 us (48%)
  waiting for transfers between devices  241 us (29%)
  local copies, waits for them, and re-layouts  77.4 us (9%)
  blocking collectives  47.6 us (6%)
  starting transfers between devices  23.3 us (3%)
  between operations  15.4 us (2%)
  other arithmetic  12.4 us (1%)
    reduce_scatter x4, waiting for transfers between devices, over_dp(): return lax.psum_scatter(matrix, 'dp', scatter_dimension=0, tiled=True)  239 us
    pallas_call x1, Pallas kernels, mlp(): pl.pallas_call(functools.partial(mlp_kernel, 512), out_shape=(jax.ShapeDt...  166 us
    pallas_call x1, Pallas kernels, first_half(): pl.pallas_call(attend_kernel, out_shape=(jax.ShapeDtypeStruct((rows, widt...  103 us
    pallas_call x1, Pallas kernels, attend_back(): pl.pallas_call(attend_back_kernel, out_shape=(jax.ShapeDtypeStruct((rows,...  87 us
    psum x1, blocking collectives, per_device(): lax.psum(jnp.concatenate([vec_one[0], vec_one[1], bias_g[0], vec_two[0],...  41.3 us
    unnamed x40, local copies, waits for them, and re-layouts  34.4 us
    pallas_call x1, Pallas kernels, token_grad(): pl.pallas_call(token_grad_kernel, out_shape=(jax.ShapeDtypeStruct((images...  23.9 us
    all_to_all x2, starting transfers between devices, exchange(): lax.all_to_all(blocks, 'bal', split_axis=0, concat_axis=0, tiled=True)  23.2 us
  transfers between devices with their start and end apart: 7, of which 3 were waited for; matrix products, arithmetic and copies ran while one was open for 8% of the time, Pallas kernels for 27%

profile of v1, /device:TPU:0, one launch (start us, length us, event | category | flops | bytes accessed | tf_op | source)
XLA Modules:
  0.0 819.8 jit_solution(15308661055603296193)
XLA Ops:
  7.2 6.3 all-gather.1
  13.6 0.6 add.124.table
  14.2 5.8 copy.64
  20.1 11.4 %shard_map.307 = bf16[16,225,768]{2,1,0:T(8,128)(2,1)} custom-call(s32[16]{0:T(128)} %add.124.table, bf16[16,225,768]{2,1,0:T(8,128)(2,1)} %bitcast.23), custom_call_target="tpu_custom_call" | custom-call | tf_op jit(solution)/shard_map/pallas_call | solution.py:491
  31.5 7.2 copy.65
  38.8 5.3 all-to-all-start
  44.3 0.7 fusion.14
  46.3 2.0 stack.26
  48.4 0.6 reshape.176.gain
  49.0 0.6 reshape.177.shift
  49.6 0.6 reshape.179.out_b
  50.2 0.6 reshape.180.gain
  50.7 0.6 reshape.181.shift
  51.3 0.6 reshape.183.down_b
  52.5 0.6 reshape.178.bias
  53.1 1.9 copy.68
  55.0 3.0 convert_bitcast_fusion
  58.0 2.1 copy.75
  60.1 0.7 pad.18.clone.spot_rows
  60.8 1.6 pad.19.spot_cols
  62.4 5.9 copy.67
  68.7 0.6 concatenate.9.meta
  69.3 102.9 %shard_map.308 = (bf16[4096,768]{1,0:T(8,128)(2,1)}, bf16[4096,2304]{1,0:T(8,128)(2,1)}, bf16[4096,768]{1,0:T(8,128)(2,1)}, f32[16,6,8,256]{3,2,1,0:T(8,128)}) custom-call(s32[96]{0:T(128)} %concatenate.9.meta, f32[16]{0:T(128)} %pad.17.slopes, bf16[16,225,768]{2,1,0:T(8,128)(2,1)} %bitcast.19, f32[16,8,256]{2,1,0:T(8,128)} %pad.18.clone.spot_rows, ...), custom_call_target="tpu_custom_call" | custom-call | tf_op jit(solution)/shard_map/pallas_call | solution.py:557
  172.2 5.9 copy.66
  178.1 166.2 %shard_map.309 = (bf16[16,225,768]{2,1,0:T(8,128)(2,1)}, f32[4096,768]{1,0:T(8,128)}, bf16[4096,768]{1,0:T(8,128)(2,1)}, bf16[768,3072]{1,0:T(8,128)(2,1)}, bf16...) custom-call(s32[96]{0:T(128)} %concatenate.9.meta, ...), custom_call_target="tpu_custom_call" | custom-call | tf_op jit(solution)/shard_map/pallas_call | solution.py:616
  344.4 87.0 %shard_map.311 = (bf16[4096,2304]{1,0:T(8,128)(2,1)}, bf16[768,2304]{1,0:T(8,128)(2,1)}, f32[8,2304]{1,0:T(8,128)}) custom-call(s32[96]{0:T(128)} %concatenate.9.meta, f32[16]{0:T(128)} %pad.17.slopes, bf16[4096,2304]{1,0:T(8,128)(2,1)} %get-tuple-element.35.qkv, bf16[4096,768]{1,0:T(8,128)(2,1)} %get-tuple-element.36.att_grad, ...), custom_call_target="tpu_custom_call" | custom-call | tf_op jit(solution)/shard_map/pallas_call | solution.py:699
  431.5 0.7 reduce-scatter.9.cloned.1.call-update
  432.8 7.2 copy.70
  440.0 17.9 %all-to-all-start.1 = ((bf16[4,4,225,768]{3,1,2,0:T(4,128)(2,1)}), bf16[4,4,225,768]{3,1,2,0:T(4,128)(2,1)}, u32[]{:S(2)}, u32[]{:S(2)}) async-start(bf16[4,4,225,768]{3,1,2,0:T(4,128)(2,1)} %copy.70), calls=%async_computation.1 | async-start | bytes 11059200 | tf_op jit(solution)/shard_map/all_to_all | solution.py:835
  458.1 0.6 reshape.169.table
  458.8 0.9 slice.58
  459.7 23.9 %shard_map.312 = (f32[16,225,768]{2,1,0:T(8,128)}, f32[8,768]{1,0:T(8,128)}) custom-call(s32[96]{0:T(128)} %concatenate.9.meta, bf16[4096,2304]{1,0:T(8,128)(2,1)} %get-tuple-element.38.packed_grad, bf16[4096,768]{1,0:T(8,128)(2,1)} %get-tuple-element.33.tokens_in.tokens, f32[4096,768]{1,0:T(8,128)} %get-tuple-element.39.mid_grad, f32[1,768]{1,0:T(1,128)} %reshape.176.gain, ...), custom_call_target="tpu_custom_call" | custom-call | tf_op jit(solution)/shard_map/pallas_call | solution.py:744
  483.6 13.2 %copy.74 = f32[4,4,225,768]{3,1,2,0:T(4,128)} copy(f32[4,4,225,768]{3,2,1,0:T(8,128)} %bitcast.25) | data formatting | bytes 22118400
  496.8 0.8 slice_reduce_fusion.5
  497.8 0.9 slice_reduce_fusion
  498.7 42.4 %reduce-scatter.5.cloned.1.call-done = bf16[96,2304]{1,0:T(8,128)(2,1)} async-done(((bf16[768,2304]{1,0:T(8,128)(2,1)}), bf16[96,2304]{1,0:T(8,128)(2,1)}) %reduce-scatter.5.cloned.1.call-update) | async-done | bytes 442384 | tf_op jit(solution)/shard_map/reduce_scatter | solution.py:851
  541.1 98.5 %reduce-scatter.9.cloned.1.call-done = bf16[96,3072]{1,0:T(8,128)(2,1)} async-done(((bf16[768,3072]{1,0:T(8,128)(2,1)}), bf16[96,3072]{1,0:T(8,128)(2,1)}) %reduce-scatter.9.cloned.1.call-update) | async-done | bytes 589840 | tf_op jit(solution)/shard_map/reduce_scatter | solution.py:851
  639.6 98.6 %reduce-scatter.11.cloned.1.call-done = bf16[384,768]{1,0:T(8,128)(2,1)} async-done(((bf16[3072,768]{1,0:T(8,128)(2,1)}), bf16[384,768]{1,0:T(8,128)(2,1)}) %reduce-scatter.11.cloned.1.call-update) | async-done | bytes 589840 | tf_op jit(solution)/shard_map/reduce_scatter | solution.py:851
  738.2 41.3 %psum.35 = f32[9984]{0:T(1024)S(1)} all-reduce(f32[9984]{0:T(1024)S(1)} %constant_dynamic-update-slice_fusion), channel_id=1, replica_groups=mesh['dp'=8,'bal'=4] {'dp','bal'}, use_global_device_ids=true, to_apply=%region_12.13 | all-reduce | flops 9984 | bytes 79872 | tf_op jit(solution)/shard_map/psum | solution.py:865
  779.5 0.6 slice.75
  780.1 0.6 fusion.15
  780.8 5.9 copy.71
  786.6 11.5 %shard_map.310 = bf16[16,225,768]{2,1,0:T(8,128)(2,1)} custom-call(s32[16]{0:T(128)} %reshape.169.table, bf16[16,225,768]{2,1,0:T(8,128)(2,1)} %bitcast.21), custom_call_target="tpu_custom_call" | custom-call | tf_op jit(solution)/shard_map/pallas_call | solution.py:491
  798.1 7.2 copy.73
  805.3 1.6 convert_element_type.30
  807.0 2.0 convert_element_type.29
  808.9 2.2 convert_element_type.31
  811.1 2.2 convert_element_type.32
  (71 shorter events, 2.5 us)
Async XLA Ops:
  38.7 5.4 copy-start.3
  38.7 5.5 copy-start.4
  38.7 9.6 %copy-start.2 = (s32[4,4]{1,0:T(4,128)S(1)}, s32[4,4]{1,0:T(4,128)}, u32[]{:S(2)}) copy-start(s32[4,4]{1,0:T(4,128)} %param.26) | copy-start | bytes 196
  38.7 9.7 %copy-start.6 = (f32[768]{0:T(1024)S(1)}, f32[768]{0:T(1024)}, u32[]{:S(2)}) copy-start(f32[768]{0:T(1024)} %param.27) | copy-start | bytes 9220
  38.7 10.3 %copy-start.7 = (f32[768]{0:T(1024)S(1)}, f32[768]{0:T(1024)}, u32[]{:S(2)}) copy-start(f32[768]{0:T(1024)} %param.28) | copy-start | bytes 9220
  38.7 10.9 %copy-start.8 = (f32[768]{0:T(1024)S(1)}, f32[768]{0:T(1024)}, u32[]{:S(2)}) copy-start(f32[768]{0:T(1024)} %param.33) | copy-start | bytes 9220
  38.7 11.5 %copy-start.9 = (f32[768]{0:T(1024)S(1)}, f32[768]{0:T(1024)}, u32[]{:S(2)}) copy-start(f32[768]{0:T(1024)} %param.34) | copy-start | bytes 9220
  38.7 12.0 %copy-start.10 = (f32[768]{0:T(1024)S(1)}, f32[768]{0:T(1024)}, u32[]{:S(2)}) copy-start(f32[768]{0:T(1024)} %param.35) | copy-start | bytes 9220
  38.7 12.6 %copy-start.11 = (f32[768]{0:T(1024)S(1)}, f32[768]{0:T(1024)}, u32[]{:S(2)}) copy-start(f32[768]{0:T(1024)} %param.39) | copy-start | bytes 9220
  38.7 13.7 %copy-start.12 = (f32[768]{0:T(1024)S(1)}, f32[768]{0:T(1024)}, u32[]{:S(2)}) copy-start(f32[768]{0:T(1024)} %param.31) | copy-start | bytes 9220
  38.7 13.7 %copy-start.13 = (f32[768]{0:T(1024)S(1)}, f32[768]{0:T(1024)}, u32[]{:S(2)}) copy-start(f32[768]{0:T(1024)} %param.30) | copy-start | bytes 9220
  38.8 14.3 %copy-start = (s32[4,4,225]{2,1,0:T(4,128)S(1)}, s32[4,4,225]{2,1,0:T(4,128)}, u32[]{:S(2)}) copy-start(s32[4,4,225]{2,1,0:T(4,128)} %param.23) | copy-start | bytes 43204
  38.8 14.3 %copy-start.1 = (s32[4,4,225]{2,1,0:T(4,128)S(1)}, s32[4,4,225]{2,1,0:T(4,128)}, u32[]{:S(2)}) copy-start(s32[4,4,225]{2,1,0:T(4,128)} %param.24) | copy-start | bytes 43204
  38.8 133.4 %all-to-all-start = ((bf16[4,4,225,768]{3,1,2,0:T(4,128)(2,1)}), bf16[4,4,225,768]{3,1,2,0:T(4,128)(2,1)}, u32[]{:S(2)}, u32[]{:S(2)}) async-start(bf16[4,4,225,768]{3,1,2,0:T(4,128)(2,1)} %copy.65), calls=%async_computation | async-start | bytes 11059200 | tf_op jit(solution)/shard_map/all_to_all | solution.py:835
  44.0 454.7 %reduce-scatter.7.cloned.1.call-start = ((), (), s32[]{:S(2)}) async-start(), calls=%async_computation.7 | async-start | bytes 1327104 | tf_op jit(solution)/shard_map/reduce_scatter | solution.py:851
  344.4 196.8 %reduce-scatter.5.cloned.1.call-start = ((), (), s32[]{:S(2)}) async-start(), calls=%async_computation.6 | async-start | bytes 3981312 | tf_op jit(solution)/shard_map/reduce_scatter | solution.py:851
  431.5 208.1 %reduce-scatter.9.cloned.1.call-start = ((), (), s32[]{:S(2)}) async-start(), calls=%async_computation.8 | async-start | bytes 5308416 | tf_op jit(solution)/shard_map/reduce_scatter | solution.py:851
  432.2 305.9 %reduce-scatter.11.cloned.1.call-start = ((), (), s32[]{:S(2)}) async-start(), calls=%async_computation.9 | async-start | bytes 5308416 | tf_op jit(solution)/shard_map/reduce_scatter | solution.py:851
  440.0 340.8 %all-to-all-start.1 = ((bf16[4,4,225,768]{3,1,2,0:T(4,128)(2,1)}), bf16[4,4,225,768]{3,1,2,0:T(4,128)(2,1)}, u32[]{:S(2)}, u32[]{:S(2)}) async-start(bf16[4,4,225,768]{3,1,2,0:T(4,128)(2,1)} %copy.70), calls=%async_computation.1 | async-start | bytes 11059200 | tf_op jit(solution)/shard_map/all_to_all | solution.py:835
  457.9 347.4 %all-reduce.7.cloned.1.call-start = ((), (), s32[]{:S(2)}) async-start(), calls=%async_computation.10 | async-start | bytes 3538944 | tf_op jit(solution)/shard_map/psum | solution.py:863
  483.6 14.1 %copy-start.5 = (f32[8,768]{1,0:T(8,128)S(1)}, f32[8,768]{1,0:T(8,128)}, u32[]{:S(2)}) copy-start(f32[8,768]{1,0:T(8,128)} %get-tuple-element.43) | copy-start | bytes 73732
Sparse Core Ops, SparseCore 0:
  344.5 78.1 reduce-scatter.6
  431.6 109.5 reduce-scatter.4
  544.8 94.7 reduce-scatter.8
  643.1 95.0 reduce-scatter.10
  740.6 47.3 all-reduce.6

commit v2 on v1

v2 whole, which is shorter than its diff:
```python
import functools
import math

import jax
import jax.numpy as jnp
from jax import lax
from jax.experimental import pallas as pl
from jax.experimental.pallas import tpu as pltpu
from jax.sharding import PartitionSpec as P

HEADS = 12
TILE = 256
WINDOW = 256
FAR = 1e12
EPS = 1e-06
VMEM_LIMIT = 60 * 1024 * 1024

F32 = jnp.float32
BF16 = jnp.bfloat16

OFF, CNT, IMG, LIVE, PEER, SPOT, MISC = 0, 16, 32, 48, 64, 80, 96
N_FWD, N_BWD, ROWS_FWD, ROWS_BWD, N_LIVE = MISC, MISC + 1, MISC + 2, MISC + 3, MISC + 4
PLACES = 128

GAIN_ONE, SHIFT_ONE, QKV_B, OUT_B, GAIN_TWO, SHIFT_TWO, DOWN_B, UP_B = 0, 1, 2, 5, 6, 7, 8, 9


def dot(a, b):
    return jnp.dot(a, b, preferred_element_type=F32)


def dot_bt(a, b):
    return lax.dot_general(a, b, (((1,), (1,)), ((), ())), preferred_element_type=F32)


def turned(block):
    size = 256 if block.shape[1] % 256 == 0 else 128
    row = lax.broadcasted_iota(jnp.int32, (size, size), 0)
    col = lax.broadcasted_iota(jnp.int32, (size, size), 1)
    eye = jnp.where(row == col, 1.0, 0.0).astype(BF16)
    parts = [
        dot_bt(eye, block[:, start : start + size]).astype(BF16)
        for start in range(0, block.shape[1], size)
    ]
    return parts[0] if len(parts) == 1 else jnp.concatenate(parts, axis=0)


def layer_norm(values):
    average = jnp.mean(values, axis=-1, keepdims=True)
    centred = values - average
    spread = jnp.mean(centred * centred, axis=-1, keepdims=True)
    inverse = lax.rsqrt(spread + EPS)
    return centred * inverse, inverse


def norm_back(out_grad, gain, unit, inverse):
    e = out_grad * gain
    mean_e = jnp.mean(e, axis=-1, keepdims=True)
    mean_eu = jnp.mean(e * unit, axis=-1, keepdims=True)
    return inverse * (e - mean_e - unit * mean_eu)


def gelu_parts(u):
    size = jnp.abs(u)
    t = 1.0 / (1.0 + (0.3275911 * math.sqrt(0.5)) * size)
    bell = jnp.exp(-0.5 * (u * u))
    poly = t * (
        0.5 * 0.254829592
        + t
        * (
            0.5 * -0.284496736
            + t * (0.5 * 1.421413741 + t * (0.5 * -1.453152027 + t * (0.5 * 1.061405429)))
        )
    )
    tail = poly * bell
    phi_sum = jnp.where(u >= 0, 1.0 - tail, tail)
    return phi_sum, u * bell * (1.0 / math.sqrt(2.0 * math.pi))


def row_ids(start, rows):
    return start + lax.broadcasted_iota(jnp.int32, (rows, 1), 0)


def aligned(value, step=16):
    return pl.multiple_of(value, step)


def by_count(count, run):
    @pl.when(count <= 128)
    def _():
        run(128, 128)

    @pl.when(jnp.logical_and(count > 128, count <= 192))
    def _():
        run(192, 256)

    @pl.when(count > 192)
    def _():
        run(256, 256)


def distances(rows, cols, which, count, keys, queries):
    mine = lax.broadcasted_iota(jnp.int32, rows.shape, 0) == which
    row = jnp.sum(jnp.where(mine, rows, 0).astype(F32), axis=0, keepdims=True)
    col = jnp.sum(jnp.where(mine, cols, 0).astype(F32), axis=0, keepdims=True)
    spots = jnp.concatenate([row, col, jnp.zeros((6, row.shape[1]), F32)], axis=0)
    spots = jnp.concatenate([spots, jnp.zeros((8, WINDOW - row.shape[1]), F32)], axis=1)
    eye = jnp.where(
        lax.broadcasted_iota(jnp.int32, (keys, WINDOW), 0)
        == lax.broadcasted_iota(jnp.int32, (keys, WINDOW), 1),
        1.0,
        0.0,
    ).astype(BF16)
    turned_spots = dot_bt(eye, spots.astype(BF16))
    down = turned_spots[:, 0:1] - spots[0:1, :queries]
    across = turned_spots[:, 1:2] - spots[1:2, :queries]
    far = row_ids(0, keys) >= count
    return jnp.where(far, FAR, jnp.sqrt(down * down + across * across))


def prepare_kernel(every, counts, present, slots, me, cot, meta, take, send):
    step = pl.program_id(0)
    steps, length, images, width = pl.num_programs(0), cot.shape[1], cot.shape[2], cot.shape[3]
    group = every.shape[0]

    @pl.when(step == 0)
    def _():
        def fill(live):
            def body(img, carry):
                spot, off = carry
                m, i = img // images, img % images
                count = counts[m, i]
                mine = present[m, i] == live

                @pl.when(mine)
                def _():
                    meta[OFF + spot] = off
                    meta[CNT + spot] = count
                    meta[IMG + spot] = img
                    meta[LIVE + spot] = live
                    meta[PEER + spot] = slots[m, i] // images * steps + m
                    meta[SPOT + img] = spot

                padded = (count + 15) // 16 * 16
                return spot + mine.astype(jnp.int32), off + jnp.where(mine, padded, 0)

            return body

        zero = jnp.int32(0)
        total = counts.shape[0] * images
        spot, off = lax.fori_loop(0, total, fill(1), (zero, zero))
        meta[N_LIVE] = spot
        meta[ROWS_BWD] = off
        meta[N_BWD] = (off + TILE - 1) // TILE
        spot, off = lax.fori_loop(0, total, fill(0), (spot, off))
        meta[ROWS_FWD] = off
        meta[N_FWD] = (off + TILE - 1) // TILE

        def land(n, carry):
            a, m, i = n // total, n % total // images, n % images
            slot = every[a, m, i]

            @pl.when(slot // images == me[0])
            def _():
                take[m * images + slot % images] = a * steps + m

            return carry

        lax.fori_loop(0, group * total, land, 0)

    block = jnp.swapaxes(cot[0].astype(F32), 0, 1).astype(BF16)
    for place in range(images):
        peer = take[step * images + place] // steps
        send[peer, 0, :length, :] = block[place]


def place_kernel(take, got, out):
    step = pl.program_id(0)
    length, images = out.shape[1], out.shape[2]
    steps = pl.num_programs(0)
    parts = [
        got[take[step * images + place] // steps, 0, :length, :].astype(F32)
        for place in range(images)
    ]
    out[0] = jnp.swapaxes(jnp.stack(parts, axis=0), 0, 1).astype(out.dtype)


def attend_kernel(
    meta, slopes, tokens, rows_in, cols_in, vecs, weight,
    packed_out, qkv_out, att_out, total_out,
    held, packed, qkv, att, gaps, sem_packed, sem_qkv, sem_att,
):
    length, per, width = tokens.shape[1], tokens.shape[2], tokens.shape[3]
    images = held.shape[0]
    steps = images // per
    now = pl.program_id(0)

    def tile_copy(which, t):
        src, dst, sem = (
            (packed, packed_out, sem_packed),
            (qkv, qkv_out, sem_qkv),
            (att, att_out, sem_att),
        )[which]
        rows = pl.ds(aligned(t * TILE, TILE), TILE)
        return pltpu.make_async_copy(src.at[rows], dst.at[rows], sem.at[t])

    @pl.when(now == 0)
    def _():
        packed[...] = jnp.zeros_like(packed)

    @pl.when(now < steps)
    def _():
        block = jnp.swapaxes(tokens[0].astype(F32), 0, 1).astype(BF16)
        for i in range(per):
            held[now * per + i, :length, :] = block[i]

    step = now - steps

    @pl.when(jnp.logical_and(step >= 0, step < images))
    def _():
        off = aligned(meta[OFF + step])
        packed[pl.ds(off, length), :] = held[meta[IMG + step], :length, :]
        begin = off // TILE
        after = aligned(meta[OFF + jnp.minimum(step + 1, images - 1)])
        end = jnp.where(step == images - 1, meta[N_FWD], after // TILE)

        def project(t, carry):
            rows = pl.ds(aligned(t * TILE, TILE), TILE)
            unit, _ = layer_norm(packed[rows, :].astype(F32))
            hidden = (
                unit * vecs[GAIN_ONE : GAIN_ONE + 1] + vecs[SHIFT_ONE : SHIFT_ONE + 1]
            ).astype(BF16)
            for part in range(3):
                cols = slice(part * width, (part + 1) * width)
                bias = vecs[QKV_B + part : QKV_B + part + 1]
                qkv[rows, cols] = (dot(hidden, weight[:, cols]) + bias).astype(BF16)
            tile_copy(0, t).start()
            tile_copy(1, t).start()
            return carry

        lax.fori_loop(begin, end, project, 0)

    @pl.when(step >= images)
    def _():
        spot = step - images
        off = aligned(meta[OFF + spot])
        count = meta[CNT + spot]

        def run(keys, queries):
            which = meta[IMG + spot] % per
            gaps[:keys, :queries] = distances(rows_in[0], cols_in[0], which, count, keys, queries)
            key_seen = row_ids(0, keys) < count
            query_seen = row_ids(0, queries) < count
            left = lax.broadcasted_iota(jnp.int32, (queries, 128), 1) < 64

            def pair(p, carry):
                lanes = aligned(p * 128, 128)
                q2 = qkv[pl.ds(off, queries), pl.ds(lanes, 128)] * 0.125
                k2 = qkv[pl.ds(off, keys), pl.ds(width + lanes, 128)]
                v2 = qkv[pl.ds(off, keys), pl.ds(2 * width + lanes, 128)]
                q2 = jnp.where(query_seen, q2, jnp.zeros_like(q2))
                k2 = jnp.where(key_seen, k2, jnp.zeros_like(k2))
                v2 = jnp.where(key_seen, v2, jnp.zeros_like(v2))
                v2t = turned(v2)
                outs = []
                for half in range(2):
                    head = 2 * p + half
                    mine = left if half == 0 else jnp.logical_not(left)
                    qh = jnp.where(mine, q2, jnp.zeros_like(q2))
                    scores = dot_bt(k2, qh) - slopes[head] * gaps[:keys, :queries]
                    top = jnp.max(scores, axis=0, keepdims=True)
                    terms = jnp.exp(scores - top)
                    total = jnp.sum(terms, axis=0, keepdims=True)
                    heads_out = dot(v2t[half * 64 : half * 64 + 64], terms.astype(BF16))
                    outs.append((heads_out * (1.0 / total)).astype(BF16))
                    total_out[0, p, half : half + 1, :queries] = top + jnp.log(total)
                both = jnp.concatenate(outs, axis=0)
                att[pl.ds(off, queries), pl.ds(lanes, 128)] = turned_back(both)
                return carry

            lax.fori_loop(0, HEADS // 2, pair, 0)

        by_count(count, run)
        after = meta[OFF + jnp.minimum(spot + 1, images - 1)]
        end = jnp.where(spot == images - 1, meta[N_FWD], after // TILE)

        def send(t, carry):
            tile_copy(2, t).start()
            return carry

        lax.fori_loop(off // TILE, end, send, 0)

    @pl.when(now == pl.num_programs(0) - 1)
    def _():
        def finish(t, carry):
            for which in range(3):
                tile_copy(which, t).wait()
            return carry

        lax.fori_loop(0, meta[N_FWD], finish, 0)


def turned_back(block):
    size = block.shape[1]
    parts = []
    for start in range(0, size, 128):
        row = lax.broadcasted_iota(jnp.int32, (128, size), 0)
        col = lax.broadcasted_iota(jnp.int32, (128, size), 1)
        eye = jnp.where(row + start == col, 1.0, 0.0).astype(BF16)
        parts.append(dot_bt(eye, block).astype(BF16))
    return parts[0] if len(parts) == 1 else jnp.concatenate(parts, axis=0)


def mlp_kernel(
    chunk, length, meta, cot_in, att_in, tokens_in,
    vecs, out_w, up_w, down_w,
    y_send, mid_grad, att_grad, up_g, down_g, out_g, vec_g, upb_g,
    up_b, cot, y_all, up_acc, down_acc, out_acc, h2_s, h2t_s, dzt_s, z_s, g_s, stage, sem,
):
    step = pl.program_id(0)
    tiles = cot.shape[0] // TILE - WINDOW // TILE
    images = (pl.num_programs(0) - tiles) // 2
    width = cot_in.shape[2]
    hidden = up_w.shape[1]
    out_b, gain, shift, down_b = [
        vecs.at[pl.ds(n, 1)] for n in (OUT_B, GAIN_TWO, SHIFT_TWO, DOWN_B)
    ]

    @pl.when(step == 0)
    def _():
        up_acc[...] = jnp.zeros_like(up_acc)
        down_acc[...] = jnp.zeros_like(down_acc)
        out_acc[...] = jnp.zeros_like(out_acc)
        vec_g[...] = jnp.zeros_like(vec_g)
        upb_g[...] = jnp.zeros_like(upb_g)
        for n in range(hidden // width):
            up_b[0:1, n * width : (n + 1) * width] = vecs[UP_B + n : UP_B + n + 1, :]

    @pl.when(jnp.logical_and(step < images, step < meta[N_LIVE]))
    def _():
        spot = step
        off = aligned(meta[OFF + spot])
        seen = row_ids(0, length) < meta[CNT + spot]
        block = cot_in[0, :length, :]
        edge = (length - 1) // 16 * 16
        cot[pl.ds(aligned(off + edge), 16), :] = jnp.zeros((16, width), BF16)
        cot[pl.ds(off, length), :] = jnp.where(seen, block, jnp.zeros_like(block))

    def run_tile(t, both):
        rows = aligned(t * TILE, TILE)
        ids = row_ids(rows, TILE)
        att = att_in[...]
        att = jnp.where(ids < meta[ROWS_FWD], att, jnp.zeros_like(att))
        mid = tokens_in[...].astype(F32) + (dot(att, out_w[...]) + out_b[...])
        unit, inverse = layer_norm(mid)
        h2 = (unit * gain[...] + shift[...]).astype(BF16)
        h2_s[...] = h2
        z_s[...] = mid + down_b[...]
        if both:
            dz = cot[pl.ds(rows, TILE), :]
            dz = jnp.where(ids < meta[ROWS_BWD], dz, jnp.zeros_like(dz))
            h2t_s[...] = turned(h2)
            dzt_s[...] = turned(dz)
            g_s[...] = jnp.zeros_like(g_s)

        def part(c, carry):
            cols = pl.ds(aligned(c * chunk, chunk), chunk)
            pre = dot(h2_s[...], up_w[:, cols]) + up_b[0:1, cols]
            share, slope = gelu_parts(pre)
            act = (pre * share).astype(BF16)
            z_s[...] += dot(act, down_w[cols, :])
            if both:
                pre_g = (dot_bt(dz, down_w[cols, :]) * (share + slope)).astype(BF16)
                up_acc[:, cols] += dot(h2t_s[...], pre_g)
                down_acc[:, cols] += dot(dzt_s[...], act)
                upb_g[0:1, cols] += jnp.sum(pre_g.astype(F32), axis=0, keepdims=True)
                g_s[...] += dot_bt(pre_g, up_w[:, cols])
            return carry

        lax.fori_loop(0, hidden // chunk, part, 0)
        y_all[pl.ds(rows, TILE), :] = z_s[...].astype(BF16)
        if both:
            dzf = dz.astype(F32)
            g2 = g_s[...]
            dmid = dzf + norm_back(g2, gain[...], unit, inverse)
            branch = dmid.astype(BF16)
            mid_grad[...] = dmid
            att_grad[...] = dot_bt(branch, out_w[...]).astype(BF16)
            out_acc[...] += dot(turned(att), branch)
            vec_g[0:1, :] += jnp.sum(g2 * unit, axis=0, keepdims=True)
            vec_g[1:2, :] += jnp.sum(g2, axis=0, keepdims=True)
            vec_g[2:3, :] += jnp.sum(branch.astype(F32), axis=0, keepdims=True)
            vec_g[3:4, :] += jnp.sum(dzf, axis=0, keepdims=True)

    tile = step - images

    @pl.when(jnp.logical_and(tile >= 0, tile < meta[N_BWD]))
    def _():
        run_tile(tile, True)

    @pl.when(
        jnp.logical_and(
            jnp.logical_and(tile >= meta[N_BWD], tile >= 0),
            jnp.logical_and(tile < meta[N_FWD], tile < tiles),
        )
    )
    def _():
        run_tile(tile, False)

    @pl.when(step == images + tiles)
    def _():
        size = stage.shape[1]
        jobs = []
        for start in range(0, width, size):
            jobs.append((up_acc, start, up_g, False))
            jobs.append((out_acc, start, out_g, False))
        for start in range(0, hidden, size):
            jobs.append((down_acc, start, down_g, True))

        def copy(n):
            source, start, target, _ = jobs[n]
            columns = target.shape[1]
            return pltpu.make_async_copy(
                stage.at[n % 2, :, pl.ds(0, columns)], target.at[pl.ds(start, size)], sem.at[n % 2]
            )

        for n, (source, start, target, flip) in enumerate(jobs):
            if n >= 2:
                copy(n - 2).wait()
            if flip:
                for low in range(0, width, 256):
                    block = source[pl.ds(low, 256), pl.ds(start, size)].astype(BF16)
                    stage[n % 2, :, pl.ds(low, 256)] = turned(block)
            else:
                columns = target.shape[1]
                stage[n % 2, :, pl.ds(0, columns)] = source[pl.ds(start, size), :].astype(BF16)
            copy(n).start()
        copy(len(jobs) - 2).wait()
        copy(len(jobs) - 1).wait()

    spot = step - images - tiles

    @pl.when(spot >= 0)
    def _():
        off = aligned(meta[OFF + spot])
        seen = row_ids(0, length) < meta[CNT + spot]
        block = y_all[pl.ds(off, length), :]
        y_send[0, :length, :] = jnp.where(seen, block, jnp.zeros_like(block))


def attend_back_kernel(
    first, per, meta, slopes, qkv, att_grad, totals, rows_in, cols_in, *rest
):
    grads_out, grads, gaps, sem = rest[-4:]
    step = pl.program_id(0)
    width = att_grad.shape[1]
    spot = first + step
    live = spot < meta[N_LIVE]
    slot = step % 2

    def copy(at):
        rows = pl.ds(aligned(meta[OFF + first + at]), WINDOW)
        return pltpu.make_async_copy(grads.at[at % 2], grads_out.at[rows], sem.at[at % 2])

    @pl.when(live)
    def _():
        count = meta[CNT + spot]

        def run(keys, queries):
            which = meta[IMG + spot] % per
            gaps[:keys, :queries] = distances(rows_in[0], cols_in[0], which, count, keys, queries)
            key_seen = row_ids(0, keys) < count
            query_seen = row_ids(0, queries) < count
            left = lax.broadcasted_iota(jnp.int32, (queries, 128), 1) < 64

            def pair(p, carry):
                lanes = aligned(p * 128, 128)
                q2 = qkv[:queries, pl.ds(lanes, 128)] * 0.125
                k2 = qkv[:keys, pl.ds(width + lanes, 128)]
                v2 = qkv[:keys, pl.ds(2 * width + lanes, 128)]
                o2 = att_grad[:queries, pl.ds(lanes, 128)]
                q2 = jnp.where(query_seen, q2, jnp.zeros_like(q2))
                o2 = jnp.where(query_seen, o2, jnp.zeros_like(o2))
                k2 = jnp.where(key_seen, k2, jnp.zeros_like(k2))
                v2 = jnp.where(key_seen, v2, jnp.zeros_like(v2))
                k2t = turned(k2)
                dq_parts = []
                dk = dv = None
                for half in range(2):
                    head = 2 * p + half
                    mine = left if half == 0 else jnp.logical_not(left)
                    qh = jnp.where(mine, q2, jnp.zeros_like(q2))
                    oh = jnp.where(mine, o2, jnp.zeros_like(o2))
                    scores = dot_bt(k2, qh) - slopes[head] * gaps[:keys, :queries]
                    probs = jnp.exp(scores - totals[0, p, half : half + 1, :queries])
                    prob_g = dot_bt(v2, oh)
                    inner = jnp.sum(probs * prob_g, axis=0, keepdims=True)
                    score_g = (probs * (prob_g - inner)).astype(BF16)
                    dv_part = dot(probs.astype(BF16), oh)
                    dk_part = dot(score_g, qh)
                    dq_parts.append(
                        (dot(k2t[half * 64 : half * 64 + 64], score_g) * 0.125).astype(BF16)
                    )
                    dk = dk_part if dk is None else dk + dk_part
                    dv = dv_part if dv is None else dv + dv_part
                dq = turned_back(jnp.concatenate(dq_parts, axis=0))
                grads[slot, :queries, pl.ds(lanes, 128)] = dq
                grads[slot, :keys, pl.ds(width + lanes, 128)] = dk.astype(BF16)
                grads[slot, :keys, pl.ds(2 * width + lanes, 128)] = dv.astype(BF16)
                return carry

            lax.fori_loop(0, HEADS // 2, pair, 0)

        by_count(count, run)

        @pl.when(step > 0)
        def _():
            copy(step - 1).wait()

        copy(step).start()

        @pl.when(jnp.logical_or(step == pl.num_programs(0) - 1, spot == meta[N_LIVE] - 1))
        def _():
            copy(step).wait()


def qkv_grad_kernel(meta, packed_grad, tokens, vecs, weight_g, bias_g, acc, stage, sem):
    tile = pl.program_id(0)
    width = tokens.shape[1]

    @pl.when(tile == 0)
    def _():
        acc[...] = jnp.zeros_like(acc)
        bias_g[...] = jnp.zeros_like(bias_g)

    @pl.when(tile < meta[N_BWD])
    def _():
        ids = row_ids(tile * TILE, TILE)
        unit, _ = layer_norm(tokens[...].astype(F32))
        hidden = (
            unit * vecs[GAIN_ONE : GAIN_ONE + 1] + vecs[SHIFT_ONE : SHIFT_ONE + 1]
        ).astype(BF16)
        hidden_t = turned(hidden)
        for part in range(3):
            cols = slice(part * width, (part + 1) * width)
            block = packed_grad[:, cols]
            block = jnp.where(ids < meta[ROWS_BWD], block, jnp.zeros_like(block))
            acc[:, cols] += dot(hidden_t, block)
            bias_g[0:1, cols] += jnp.sum(block.astype(F32), axis=0, keepdims=True)

    @pl.when(tile == pl.num_programs(0) - 1)
    def _():
        size = stage.shape[1]
        count = width // size

        def copy(n):
            return pltpu.make_async_copy(
                stage.at[n % 2], weight_g.at[pl.ds(n * size, size)], sem.at[n % 2]
            )

        for n in range(count):
            if n >= 2:
                copy(n - 2).wait()
            stage[n % 2] = acc[pl.ds(n * size, size), :].astype(BF16)
            copy(n).start()
        copy(count - 2).wait()
        copy(count - 1).wait()


def token_grad_kernel(meta, packed_grad, tokens, mid_grad, vecs, weight, out, vec_g, held):
    step = pl.program_id(0)
    tiles = held.shape[0] // TILE - WINDOW // TILE
    length, images = out.shape[1], out.shape[2]

    @pl.when(step == 0)
    def _():
        vec_g[...] = jnp.zeros_like(vec_g)

    @pl.when(jnp.logical_and(step < tiles, step < meta[N_BWD]))
    def _():
        rows = aligned(step * TILE, TILE)
        ids = row_ids(rows, TILE)
        unit, inverse = layer_norm(tokens[...].astype(F32))
        block = packed_grad[...]
        block = jnp.where(ids < meta[ROWS_BWD], block, jnp.zeros_like(block))
        g1 = dot_bt(block, weight[...])
        back = norm_back(g1, vecs[GAIN_ONE : GAIN_ONE + 1], unit, inverse)
        held[pl.ds(rows, TILE), :] = mid_grad[...] + back
        vec_g[0:1, :] += jnp.sum(g1 * unit, axis=0, keepdims=True)
        vec_g[1:2, :] += jnp.sum(g1, axis=0, keepdims=True)

    @pl.when(step >= tiles)
    def _():
        parts = []
        for i in range(images):
            spot = meta[SPOT + (step - tiles) * images + i]
            off = aligned(meta[OFF + spot])
            limit = meta[CNT + spot] * meta[LIVE + spot]
            block = held[pl.ds(off, length), :]
            parts.append(jnp.where(row_ids(0, length) < limit, block, 0.0))
        out[0] = jnp.swapaxes(jnp.stack(parts, axis=0), 0, 1)


def whole(*shape):
    return pl.BlockSpec(shape, lambda *_: (0,) * len(shape), pipeline_mode=pl.Buffered(1))


def params():
    return pltpu.CompilerParams(vmem_limit_bytes=VMEM_LIMIT)


def small():
    return pl.BlockSpec(memory_space=pltpu.SMEM)


def prepare(every, counts, present, slots, me, cotangent):
    steps, length, images, width = cotangent.shape
    group = every.shape[0]
    padded = (length + 7) // 8 * 8
    return pl.pallas_call(
        prepare_kernel,
        out_shape=(
            jax.ShapeDtypeStruct((PLACES,), jnp.int32),
            jax.ShapeDtypeStruct((steps * images,), jnp.int32),
            jax.ShapeDtypeStruct((group, steps, padded, width), BF16),
        ),
        grid=(steps,),
        in_specs=[small()] * 5 + [pl.BlockSpec((1, length, images, width), lambda m: (m, 0, 0, 0))],
        out_specs=[
            small(),
            small(),
            pl.BlockSpec((group, 1, padded, width), lambda m: (0, m, 0, 0)),
        ],
        compiler_params=params(),
    )(every, counts, present, slots, me, cotangent)


def place(take, got, length):
    group, steps, padded, width = got.shape
    return pl.pallas_call(
        place_kernel,
        out_shape=jax.ShapeDtypeStruct((steps, length, group, width), BF16),
        grid=(steps,),
        in_specs=[small(), pl.BlockSpec((group, 1, padded, width), lambda m: (0, m, 0, 0))],
        out_specs=pl.BlockSpec((1, length, group, width), lambda m: (m, 0, 0, 0)),
        compiler_params=params(),
    )(take, got)


def first_half(meta, slopes, tokens, rows, cols, vecs, weight):
    steps, length, per, width = tokens.shape
    images = steps * per
    tiles = -(-images * ((length + 15) // 16 * 16) // TILE)
    total = tiles * TILE + WINDOW
    spots = pl.BlockSpec(
        (1, per, length),
        lambda s, meta, slopes: (meta[IMG + jnp.maximum(s - steps - images, 0)] // per, 0, 0),
    )
    return pl.pallas_call(
        attend_kernel,
        out_shape=(
            jax.ShapeDtypeStruct((total, width), BF16),
            jax.ShapeDtypeStruct((total, 3 * width), BF16),
            jax.ShapeDtypeStruct((total, width), BF16),
            jax.ShapeDtypeStruct((images, HEADS // 2, 8, WINDOW), F32),
        ),
        grid_spec=pltpu.PrefetchScalarGridSpec(
            num_scalar_prefetch=2,
            grid=(steps + 2 * images,),
            in_specs=[
                pl.BlockSpec(
                    (1, length, per, width),
                    lambda s, meta, slopes: (jnp.minimum(s, steps - 1), 0, 0, 0),
                ),
                spots,
                spots,
                whole(*vecs.shape),
                whole(width, 3 * width),
            ],
            out_specs=[
                pl.BlockSpec(memory_space=pl.ANY),
                pl.BlockSpec(memory_space=pl.ANY),
                pl.BlockSpec(memory_space=pl.ANY),
                pl.BlockSpec(
                    (1, HEADS // 2, 8, WINDOW),
                    lambda s, meta, slopes: (jnp.maximum(s - steps - images, 0), 0, 0, 0),
                ),
            ],
            scratch_shapes=[
                pltpu.VMEM((images, (length + 15) // 16 * 16, width), BF16),
                pltpu.VMEM((total, width), BF16),
                pltpu.VMEM((total, 3 * width), BF16),
                pltpu.VMEM((total, width), BF16),
                pltpu.VMEM((WINDOW, WINDOW), F32),
                pltpu.SemaphoreType.DMA((tiles,)),
                pltpu.SemaphoreType.DMA((tiles,)),
                pltpu.SemaphoreType.DMA((tiles,)),
            ],
        ),
        compiler_params=params(),
        cost_estimate=cost(40),
    )(meta, slopes, tokens, rows, cols, vecs, weight)


def mlp(meta, cot, att, packed, vecs, out_w, up_w, down_w, length):
    images, padded, width = cot.shape
    rows = packed.shape[0]
    tiles = (rows - WINDOW) // TILE
    hidden = up_w.shape[1]
    last = images - 1

    def fwd_tile(s, meta):
        return (jnp.clip(s - images, 0, meta[N_FWD] - 1), 0)

    def bwd_tile(s, meta):
        return (jnp.clip(s - images, 0, jnp.maximum(meta[N_BWD] - 1, 0)), 0)

    return pl.pallas_call(
        functools.partial(mlp_kernel, 512, length),
        out_shape=(
            jax.ShapeDtypeStruct((images, padded, width), BF16),
            jax.ShapeDtypeStruct((rows, width), F32),
            jax.ShapeDtypeStruct((rows, width), BF16),
            jax.ShapeDtypeStruct((width, hidden), BF16),
            jax.ShapeDtypeStruct((hidden, width), BF16),
            jax.ShapeDtypeStruct((width, width), BF16),
            jax.ShapeDtypeStruct((8, width), F32),
            jax.ShapeDtypeStruct((8, hidden), F32),
        ),
        grid_spec=pltpu.PrefetchScalarGridSpec(
            num_scalar_prefetch=1,
            grid=(2 * images + tiles,),
            in_specs=[
                pl.BlockSpec(
                    (1, padded, width), lambda s, meta: (meta[PEER + jnp.minimum(s, last)], 0, 0)
                ),
                pl.BlockSpec((TILE, width), fwd_tile),
                pl.BlockSpec((TILE, width), fwd_tile),
                whole(*vecs.shape),
                whole(width, width),
                whole(width, hidden),
                whole(hidden, width),
            ],
            out_specs=[
                pl.BlockSpec(
                    (1, padded, width),
                    lambda s, meta: (meta[PEER + jnp.clip(s - images - tiles, 0, last)], 0, 0),
                ),
                pl.BlockSpec((TILE, width), bwd_tile),
                pl.BlockSpec((TILE, width), bwd_tile),
                pl.BlockSpec(memory_space=pl.ANY),
                pl.BlockSpec(memory_space=pl.ANY),
                pl.BlockSpec(memory_space=pl.ANY),
                whole(8, width),
                whole(8, hidden),
            ],
            scratch_shapes=[
                pltpu.VMEM((8, hidden), F32),
                pltpu.VMEM((rows, width), BF16),
                pltpu.VMEM((rows, width), BF16),
                pltpu.VMEM((width, hidden), F32),
                pltpu.VMEM((width, hidden), F32),
                pltpu.VMEM((width, width), F32),
                pltpu.VMEM((TILE, width), BF16),
                pltpu.VMEM((width, TILE), BF16),
                pltpu.VMEM((width, TILE), BF16),
                pltpu.VMEM((TILE, width), F32),
                pltpu.VMEM((TILE, width), F32),
                pltpu.VMEM((2, 256, hidden), BF16),
                pltpu.SemaphoreType.DMA((2,)),
            ],
        ),
        compiler_params=params(),
        cost_estimate=cost(110),
    )(meta, cot, att, packed, vecs, out_w, up_w, down_w)


def attend_back(first, count, meta, slopes, qkv, att_grad, totals, rows_in, cols_in, earlier):
    total, wide = qkv.shape
    width = wide // 3
    per, length = rows_in.shape[1:]

    def spot_of(s, meta):
        return jnp.clip(first + s, 0, jnp.maximum(meta[N_LIVE] - 1, 0))

    def by_offset(s, meta, slopes):
        return (aligned(meta[OFF + spot_of(s, meta)]), 0)

    spots = pl.BlockSpec(
        (1, per, length),
        lambda s, meta, slopes: (meta[IMG + spot_of(s, meta)] // per, 0, 0),
    )
    anywhere = pl.BlockSpec(memory_space=pl.ANY)
    return pl.pallas_call(
        functools.partial(attend_back_kernel, first, per),
        out_shape=jax.ShapeDtypeStruct((total, wide), BF16),
        grid_spec=pltpu.PrefetchScalarGridSpec(
            num_scalar_prefetch=2,
            grid=(count,),
            in_specs=[
                pl.BlockSpec((pl.Element(WINDOW), pl.Element(wide)), by_offset),
                pl.BlockSpec((pl.Element(WINDOW), pl.Element(width)), by_offset),
                pl.BlockSpec(
                    (1, HEADS // 2, 8, WINDOW),
                    lambda s, meta, slopes: (spot_of(s, meta), 0, 0, 0),
                ),
                spots,
                spots,
            ]
            + [anywhere] * len(earlier),
            out_specs=anywhere,
            scratch_shapes=[
                pltpu.VMEM((2, WINDOW, wide), BF16),
                pltpu.VMEM((WINDOW, WINDOW), F32),
                pltpu.SemaphoreType.DMA((2,)),
            ],
        ),
        input_output_aliases={7: 0} if earlier else {},
        compiler_params=params(),
        cost_estimate=cost(15),
    )(meta, slopes, qkv, att_grad, totals, rows_in, cols_in, *earlier)


def bwd_tile(s, meta):
    return (jnp.clip(s, 0, jnp.maximum(meta[N_BWD] - 1, 0)), 0)


def qkv_grad(meta, packed_grad, packed, vecs):
    rows, width = packed.shape
    tiles = (rows - WINDOW) // TILE
    return pl.pallas_call(
        qkv_grad_kernel,
        out_shape=(
            jax.ShapeDtypeStruct((width, 3 * width), BF16),
            jax.ShapeDtypeStruct((8, 3 * width), F32),
        ),
        grid_spec=pltpu.PrefetchScalarGridSpec(
            num_scalar_prefetch=1,
            grid=(tiles,),
            in_specs=[
                pl.BlockSpec((TILE, 3 * width), bwd_tile),
                pl.BlockSpec((TILE, width), bwd_tile),
                whole(*vecs.shape),
            ],
            out_specs=[pl.BlockSpec(memory_space=pl.ANY), whole(8, 3 * width)],
            scratch_shapes=[
                pltpu.VMEM((width, 3 * width), F32),
                pltpu.VMEM((2, 256, 3 * width), BF16),
                pltpu.SemaphoreType.DMA((2,)),
            ],
        ),
        compiler_params=params(),
        cost_estimate=cost(15),
    )(meta, packed_grad, packed, vecs)


def token_grad(meta, packed_grad, packed, mid_grad, vecs, weight, steps, length, images):
    rows, width = packed.shape
    tiles = (rows - WINDOW) // TILE
    return pl.pallas_call(
        token_grad_kernel,
        out_shape=(
            jax.ShapeDtypeStruct((steps, length, images, width), F32),
            jax.ShapeDtypeStruct((8, width), F32),
        ),
        grid_spec=pltpu.PrefetchScalarGridSpec(
            num_scalar_prefetch=1,
            grid=(tiles + steps,),
            in_specs=[
                pl.BlockSpec((TILE, 3 * width), bwd_tile),
                pl.BlockSpec((TILE, width), bwd_tile),
                pl.BlockSpec((TILE, width), bwd_tile),
                whole(*vecs.shape),
                whole(width, 3 * width),
            ],
            out_specs=[
                pl.BlockSpec(
                    (1, length, images, width),
                    lambda s, meta: (jnp.clip(s - tiles, 0, steps - 1), 0, 0, 0),
                ),
                whole(8, width),
            ],
            scratch_shapes=[pltpu.VMEM((rows, width), F32)],
        ),
        compiler_params=params(),
        cost_estimate=cost(20),
    )(meta, packed_grad, packed, mid_grad, vecs, weight)


def cost(microseconds):
    return pl.CostEstimate(
        flops=int(microseconds * 1e9), bytes_accessed=int(microseconds * 1e5), transcendentals=0
    )


def swap(block, axis, bit):
    size = lax.axis_size(axis)
    return lax.ppermute(block, axis, [(n, n ^ bit) for n in range(size)])


def bit_of(axis, bit):
    return lax.axis_index(axis) // bit % 2


def added(a, b):
    return (a.astype(F32) + b.astype(F32)).astype(BF16)


def half_sums(block, axis, bit, dim):
    mine = bit_of(axis, bit)
    keep = lax.dynamic_index_in_dim(block, mine, dim, keepdims=False)
    send = lax.dynamic_index_in_dim(block, 1 - mine, dim, keepdims=False)
    return added(keep, swap(send, axis, bit))


def summed_rows(matrix):
    size = lax.axis_size("dp")
    rows, columns = matrix.shape
    mine = bit_of("bal", 1)
    half = columns // 2
    keep = lax.dynamic_slice(matrix, (0, mine * half), (rows, half))
    send = lax.dynamic_slice(matrix, (0, (1 - mine) * half), (rows, half))
    block = added(keep, swap(send, "bal", 1))
    bit = 1
    while bit < size:
        left = size // bit
        block = half_sums(block.reshape(left // 2, 2, rows // size, half), "dp", bit, 1)
        bit *= 2
    block = block.reshape(rows // size, half)
    block = added(block, swap(block, "bal", 2))
    other = swap(block, "bal", 1)
    first = jnp.where(mine == 0, block, other)
    second = jnp.where(mine == 0, other, block)
    return jnp.concatenate([first, second], axis=1).astype(F32)


def summed(block):
    for axis in ("bal", "dp"):
        bit = 1
        while bit < lax.axis_size(axis):
            block = block + swap(block, axis, bit)
            bit *= 2
    return block


def per_device(
    tokens,
    cotangent,
    counts,
    rows,
    cols,
    present,
    slots,
    first_gain,
    first_shift,
    qkv_weight,
    query_bias,
    value_bias,
    out_weight,
    out_bias,
    second_gain,
    second_shift,
    up_weight,
    up_bias,
    down_weight,
    down_bias,
):
    steps, images, length, width = tokens.shape
    hidden = up_weight.shape[1]
    group = lax.axis_size("bal")
    total = steps * images
    vecs = jnp.concatenate(
        [
            first_gain, first_shift, query_bias, jnp.zeros_like(query_bias), value_bias,
            out_bias, second_gain, second_shift, down_bias, up_bias,
            jnp.zeros((7 * width - hidden,), F32),
        ]
    ).reshape(16, width)
    slopes = jnp.exp2(-8.0 * (jnp.arange(16, dtype=F32) + 1.0) / HEADS)

    def exchange(blocks):
        flat = blocks.reshape(group, -1, width)
        return lax.all_to_all(flat, "bal", split_axis=0, concat_axis=0, tiled=True)

    def turn(array):
        return jnp.transpose(array, (0, 2, 1, 3))

    meta, take, cot_send = prepare(
        lax.all_gather(slots, "bal"), counts, present, slots,
        lax.axis_index("bal").astype(jnp.int32).reshape(1), turn(cotangent),
    )
    cot_home = exchange(cot_send).reshape(total, -1, width)
    packed, qkv, att, totals = first_half(meta, slopes, turn(tokens), rows, cols, vecs, qkv_weight)
    y_send, mid_grad, att_grad, up_g, down_g, out_g, vec_two, upb_g = mlp(
        meta, cot_home, att, packed, vecs, out_weight, up_weight, down_weight, length
    )
    y_got = exchange(y_send).reshape(group, steps, -1, width)
    up_rows, down_rows, out_rows = summed_rows(up_g), summed_rows(down_g), summed_rows(out_g)
    vec_two = summed(jnp.concatenate([vec_two[:4].reshape(-1), upb_g[0]]))

    quarter = images
    earlier = ()
    for first in range(0, total, quarter):
        packed_grad = attend_back(
            first, quarter, meta, slopes, qkv, att_grad, totals, rows, cols, earlier
        )
        earlier = (packed_grad,)
    qkv_g, bias_g = qkv_grad(meta, packed_grad, packed, vecs)
    qkv_rows = summed_rows(qkv_g)
    input_grad, vec_one = token_grad(
        meta, packed_grad, packed, mid_grad, vecs, qkv_weight, steps, length, images
    )
    vec_one = summed(
        jnp.concatenate([vec_one[:2].reshape(-1), bias_g[0, :width], bias_g[0, 2 * width :]])
    )

    def vector(array, n):
        return array[n * width : (n + 1) * width]

    return (
        turn(place(take, y_got, length)),
        turn(input_grad),
        vector(vec_one, 0),
        vector(vec_one, 1),
        qkv_rows,
        vector(vec_one, 2),
        vector(vec_one, 3),
        out_rows,
        vector(vec_two, 2),
        vector(vec_two, 0),
        vector(vec_two, 1),
        up_rows,
        vec_two[4 * width :],
        down_rows,
        vector(vec_two, 3),
    )


def solution(mesh):
    images = P(None, ("dp", "bal"), None, None)
    spots = P(None, ("dp", "bal"), None)
    flags = P(None, ("dp", "bal"))
    matrix = P("dp", None)
    return jax.shard_map(
        per_device,
        mesh=mesh,
        in_specs=(images, images, flags, spots, spots, flags, flags) + (P(),) * 13,
        out_specs=(
            images, images, P(), P(), matrix, P(), P(), matrix, P(), P(), P(), matrix, P(), matrix, P(),
        ),
        check_vma=False,
    )
```

time: 831 us -> 640 us (0.77)
  waiting for transfers between devices: 241 us -> 126 us
  starting transfers between devices: 23.3 us -> 102 us
  local copies, waits for them, and re-layouts: 77.4 us -> 17.7 us
  Pallas kernels: 403 us -> 360 us
  blocking collectives: 47.6 us -> 7.97 us
  between operations: 15.4 us -> 1.9 us
    reduce_scatter x4 -> x0, waiting for transfers between devices: 239 us -> none  [over_dp(): return lax.psum_scatter(matrix, 'dp', scatter_dimension=0, tiled=True)]
    ppermute x0 -> x34, waiting for transfers between devices: none -> 126 us  [swap(): return lax.ppermute(block, axis, [(n, n ^ bit) for n in range(size)])]
    ppermute x0 -> x34, starting transfers between devices: none -> 91.8 us  [swap(): return lax.ppermute(block, axis, [(n, n ^ bit) for n in range(size)])]
    pallas_call x6 -> x10, Pallas kernels: 403 us -> 360 us  [the longest x1 144 us: mlp(): pl.pallas_call(functools.partial(mlp_kernel, 512, length), out_shape=(jax...]
    psum x1 -> x0, blocking collectives: 41.3 us -> none  [per_device(): lax.psum(jnp.concatenate([vec_one[0], vec_one[1], bias_g[0], vec_two[0],...]
    unnamed x40 -> x48, local copies, waits for them, and re-layouts: 34.4 us -> 1.55 us
    reshape x12 -> x3, local copies, waits for them, and re-layouts: 19.3 us -> 1.92 us  [the longest x1 1.29 us: per_device(): vec_one[:2].reshape(-1)]
    all_to_all x2, starting transfers between devices: 23.2 us -> 10.4 us  [exchange(): return lax.all_to_all(flat, 'bal', split_axis=0, concat_axis=0, tiled=True)]
  transfers between devices with their start and end apart: 7 -> 36, of which waited for: 3 -> 11; matrix products, arithmetic and copies ran while one was open for 8% -> 5% of each run, Pallas kernels for 27% -> 33%
where the time goes in v2:
time: 640 us; the launch traced here: 632 us
  Pallas kernels  360 us (56%)
  waiting for transfers between devices  126 us (20%)
  starting transfers between devices  102 us (16%)
  local copies, waits for them, and re-layouts  17.7 us (3%)
  other arithmetic  16.2 us (3%)
  blocking collectives  7.97 us (1%)
    pallas_call x1, Pallas kernels, mlp(): pl.pallas_call(functools.partial(mlp_kernel, 512, length), out_shape=(jax...  144 us
    ppermute x34, waiting for transfers between devices, swap(): return lax.ppermute(block, axis, [(n, n ^ bit) for n in range(size)])  126 us
    pallas_call x1, Pallas kernels, first_half(): pl.pallas_call(attend_kernel, out_shape=(jax.ShapeDtypeStruct((total, wid...  97.7 us
    ppermute x34, starting transfers between devices, swap(): return lax.ppermute(block, axis, [(n, n ^ bit) for n in range(size)])  91.8 us
    pallas_call x4, Pallas kernels, attend_back(): pl.pallas_call(functools.partial(attend_back_kernel, first, per), out_sha...  67.4 us
    pallas_call x1, Pallas kernels, token_grad(): pl.pallas_call(token_grad_kernel, out_shape=(jax.ShapeDtypeStruct((steps,...  18.9 us
    pallas_call x1, Pallas kernels, qkv_grad(): pl.pallas_call(qkv_grad_kernel, out_shape=(jax.ShapeDtypeStruct((width, 3...  15.7 us
  transfers between devices with their start and end apart: 36, of which 11 were waited for; matrix products, arithmetic and copies ran while one was open for 5% of the time, Pallas kernels for 33%

profile of v2, /device:TPU:0, one launch (start us, length us, event | category | flops | bytes accessed | tf_op | source)
XLA Modules:
  0.0 631.9 jit_solution(16953074343179209703)
XLA Ops:
  0.6 8.0 %all-gather.1.every = s32[4,4,4]{2,1,0:T(4,128)} all-gather(s32[1,4,4]{2,1,0:T(4,128)} %bitcast.101), channel_id=2, replica_groups=mesh['dp'=8,'bal'=4] {'bal'}, dimensions={0}, use_global_device_ids=true | all-gather | bytes 320 | tf_op jit(solution)/shard_map/all_gather | solution.py:989
  8.6 9.8 %shard_map.307 = (s32[128]{0:T(128)}, s32[16]{0:T(128)}, bf16[4,4,232,768]{3,2,1,0:T(8,128)(2,1)}) custom-call(s32[4,4,4]{2,1,0:T(4,128)} %all-gather.1.every, s32[4,4]{1,0:T(4,128)} %counts.1, s32[4,4]{1,0:T(4,128)} %present.1, s32[4,4]{1,0:T(4,128)} %slots.1, s32[1]{0:T(128)} %bitcast.1.me, bf16[4,225,4,768]{3,2,1,0:T(4,128)(2,1)} %bitcast.83), custom_call_target="tpu_custom_call" | custom-call | tf_op jit(solution)/shard_map/pallas_call | solution.py:620
  18.5 5.3 all-to-all-start
  25.2 97.7 %shard_map.308 = (bf16[4096,768]{1,0:T(8,128)(2,1)}, bf16[4096,2304]{1,0:T(8,128)(2,1)}, bf16[4096,768]{1,0:T(8,128)(2,1)}, f32[16,6,8,256]{3,2,1,0:T(8,128)}) custom-call(s32[128]{0:T(128)} %get-tuple-element.35.meta, f32[16]{0:T(128)} %multiply_exponential_fusion.slopes, bf16[4,225,4,768]{3,2,1,0:T(4,128)(2,1)} %bitcast.102, s32[4,4,225]{2,1,0:T(4,128)} %rows_in.9, ...), custom_call_target="tpu_custom_call" | custom-call | flops 40000000000 | bytes 4000000 | tf_op jit(solution)/shard_map/pallas_call | solution.py:659
  123.0 143.8 %shard_map.309 = (bf16[16,232,768]{2,1,0:T(8,128)(2,1)}, f32[4096,768]{1,0:T(8,128)}, bf16[4096,768]{1,0:T(8,128)(2,1)}, bf16[768,3072]{1,0:T(8,128)(2,1)}, bf16...) custom-call(s32[128]{0:T(128)} %get-tuple-element.35.meta, ...), custom_call_target="tpu_custom_call" | custom-call | flops 109999996928 | bytes 11000000 | tf_op jit(solution)/shard_map/pallas_call | solution.py:718
  267.5 0.9 slice.50
  270.4 1.9 constant_dynamic-slice_fusion.5
  272.4 27.1 %shard_map.311.rest_0_ = bf16[4096,2304]{1,0:T(8,128)(2,1)} custom-call(s32[128]{0:T(128)} %get-tuple-element.35.meta, f32[16]{0:T(128)} %multiply_exponential_fusion.slopes, bf16[4096,2304]{1,0:T(8,128)(2,1)} %get-tuple-element.40.qkv, bf16[4096,768]{1,0:T(8,128)(2,1)} %get-tuple-element.41.att_grad, f32[16,6,8,256]{3,2,1,0:T(8,128)} %get-tuple-element.42.totals, ...), custom_call_target="tpu_custom_call" | custom-call | flops 15000000512 | bytes 1500000 | tf_op jit(solution)/shard_map/pallas_call | solution.py:794
  299.5 23.1 %shard_map.312.rest_0_ = bf16[4096,2304]{1,0:T(8,128)(2,1)} custom-call(s32[128]{0:T(128)} %get-tuple-element.35.meta, f32[16]{0:T(128)} %multiply_exponential_fusion.slopes, bf16[4096,2304]{1,0:T(8,128)(2,1)} %get-tuple-element.40.qkv, bf16[4096,768]{1,0:T(8,128)(2,1)} %get-tuple-element.41.att_grad, ...), custom_call_target="tpu_custom_call", output_to_operand_aliasing={{}: (7, {})} | custom-call | flops 15000000512 | bytes 1500000 | tf_op jit(solution)/shard_map/pallas_call | solution.py:794
  322.6 15.0 %shard_map.313.rest_0_ = bf16[4096,2304]{1,0:T(8,128)(2,1)} custom-call(s32[128]{0:T(128)} %get-tuple-element.35.meta, f32[16]{0:T(128)} %multiply_exponential_fusion.slopes, bf16[4096,2304]{1,0:T(8,128)(2,1)} %get-tuple-element.40.qkv, bf16[4096,768]{1,0:T(8,128)(2,1)} %get-tuple-element.41.att_grad, ...), custom_call_target="tpu_custom_call", output_to_operand_aliasing={{}: (7, {})} | custom-call | flops 15000000512 | bytes 1500000 | tf_op jit(solution)/shard_map/pallas_call | solution.py:794
  337.6 2.2 shard_map.314.packed_grad
  339.8 15.7 %shard_map.316 = (bf16[768,2304]{1,0:T(8,128)(2,1)}, f32[8,2304]{1,0:T(8,128)}) custom-call(s32[128]{0:T(128)} %get-tuple-element.35.meta, bf16[4096,2304]{1,0:T(8,128)(2,1)} %shard_map.314.packed_grad, bf16[4096,768]{1,0:T(8,128)(2,1)} %get-tuple-element.38.tokens_in.tokens, f32[16,768]{1,0:T(8,128)} %reshape.137.vecs), custom_call_target="tpu_custom_call" | custom-call | flops 15000000512 | bytes 1500000 | tf_op jit(solution)/shard_map/pallas_call | solution.py:831
  355.5 18.9 %shard_map.315 = (f32[4,225,4,768]{3,2,1,0:T(4,128)}, f32[8,768]{1,0:T(8,128)}) custom-call(s32[128]{0:T(128)} %get-tuple-element.35.meta, bf16[4096,2304]{1,0:T(8,128)(2,1)} %shard_map.314.packed_grad, bf16[4096,768]{1,0:T(8,128)(2,1)} %get-tuple-element.38.tokens_in.tokens, f32[4096,768]{1,0:T(8,128)} %get-tuple-element.43.mid_grad, ...), custom_call_target="tpu_custom_call" | custom-call | flops 20000000000 | bytes 2000000 | tf_op jit(solution)/shard_map/pallas_call | solution.py:860
  374.4 1.3 slice.42
  375.7 1.3 reshape.140
  377.0 0.9 slice_reduce_fusion.1
  378.6 8.4 %collective-permute-start = (f32[3072]{0:T(1024)S(1)}, f32[3072]{0:T(1024)S(1)}, u32[]{:S(2)}, u32[]{:S(2)}) collective-permute-start(f32[3072]{0:T(1024)S(1)} %pad_maximum_fusion.1), channel_id=1, source_target_pairs={{0,1},{1,0},{2,3},{3,2},{4,5},{5,4},{6,7},{7,6},{8,9},{9,8},{10,11... | collective-permute-start | bytes 36872 | tf_op jit(solution)/shard_map/ppermute | solution.py:898
  387.0 1.4 constant_dynamic-slice_fusion.7
  388.4 1.2 add_convert_fusion.3
  391.2 12.4 %collective-permute-start.12 = (bf16[4,96,384]{2,1,0:T(8,128)(2,1)}, bf16[4,96,384]{2,1,0:T(8,128)(2,1)}, u32[]{:S(2)}, u32[]{:S(2)}) collective-permute-start(bf16[4,96,384]{2,1,0:T(8,128)(2,1)} %dynamic-slice_bitcast_fusion.6), channel_id=1, source_target_pairs={{0,4},{4,0},{8,12},{12,8},{16,20},{20,16},{24,28},{28,24},{1,5},{5... | collective-permute-start | bytes 884744 | tf_op jit(solution)/shard_map/ppermute | solution.py:898
  403.6 46.7 %collective-permute-start.1 = (f32[3072]{0:T(1024)S(1)}, f32[3072]{0:T(1024)S(1)}, u32[]{:S(2)}, u32[]{:S(2)}) collective-permute-start(f32[3072]{0:T(1024)S(1)} %fusion.15), channel_id=1, source_target_pairs={{0,2},{1,3},{2,0},{3,1},{4,6},{5,7},{6,4},{7,5},{8,10},{9,11},{10,... | collective-permute-start | bytes 36872 | tf_op jit(solution)/shard_map/ppermute | solution.py:898
  450.3 1.4 fusion.12
  452.0 5.1 all-to-all-start.1
  457.9 3.5 collective-permute-start.3
  462.1 2.0 collective-permute-start.19
  464.1 1.1 fusion.6
  465.3 2.0 constant_dynamic-slice_fusion.1
  467.4 2.1 collective-permute-start.20
  469.5 1.9 collective-permute-done.13
  471.5 1.1 collective-permute-start.14
  472.5 2.0 constant_dynamic-slice_fusion.3
  475.1 2.0 collective-permute-start.21
  477.1 1.7 collective-permute-start.15
  478.9 1.9 add_convert_fusion.2
  481.8 41.2 %collective-permute-done.15 = bf16[96,384]{1,0:T(8,128)(2,1)S(1)} collective-permute-done((bf16[96,384]{1,0:T(8,128)(2,1)S(1)}, bf16[96,384]{1,0:T(8,128)(2,1)S(1)}, u32[]{:S(2)}, u32[]{:S(2)}) %collective-permute-start.15) | collective-permute-done | bytes 73760 | tf_op jit(solution)/shard_map/ppermute | solution.py:898
  525.4 3.5 collective-permute-start.7
  529.8 2.1 collective-permute-start.23
  531.9 7.8 %collective-permute-done.7 = bf16[2,96,1152]{2,1,0:T(8,128)(2,1)S(1)} collective-permute-done((bf16[2,96,1152]{2,1,0:T(8,128)(2,1)S(1)}, bf16[2,96,1152]{2,1,0:T(8,128)(2,1)S(1)}, u32[]{:S(2)}, u32[]{:S(2)}) %collective-permute-start.7) | collective-permute-done | bytes 442400 | tf_op jit(solution)/shard_map/ppermute | solution.py:898
  540.8 2.1 collective-permute-start.29
  542.9 10.0 %collective-permute-done.8 = bf16[1,96,1152]{2,1,0:T(8,128)(2,1)S(1)} collective-permute-done((bf16[1,96,1152]{2,1,0:T(8,128)(2,1)S(1)}, bf16[1,96,1152]{2,1,0:T(8,128)(2,1)S(1)}, u32[]{:S(2)}, u32[]{:S(2)}) %collective-permute-start.8) | collective-permute-done | bytes 221216 | tf_op jit(solution)/shard_map/ppermute | solution.py:898
  553.3 5.4 collective-permute-done.23
  559.2 24.4 %collective-permute-done.29 = bf16[4,384,384]{2,1,0:T(8,128)(2,1)S(1)} collective-permute-done((bf16[4,384,384]{2,1,0:T(8,128)(2,1)S(1)}, bf16[4,384,384]{2,1,0:T(8,128)(2,1)S(1)}, u32[]{:S(2)}, u32[]{:S(2)}) %collective-permute-start.29) | collective-permute-done | bytes 1179680 | tf_op jit(solution)/shard_map/ppermute | solution.py:898
  584.8 20.5 %collective-permute-done.30 = bf16[2,384,384]{2,1,0:T(8,128)(2,1)S(1)} collective-permute-done((bf16[2,384,384]{2,1,0:T(8,128)(2,1)S(1)}, bf16[2,384,384]{2,1,0:T(8,128)(2,1)S(1)}, u32[]{:S(2)}, u32[]{:S(2)}) %collective-permute-start.30) | collective-permute-done | bytes 589856 | tf_op jit(solution)/shard_map/ppermute | solution.py:898
  606.1 13.4 %collective-permute-done.31 = bf16[1,384,384]{2,1,0:T(8,128)(2,1)S(1)} collective-permute-done((bf16[1,384,384]{2,1,0:T(8,128)(2,1)S(1)}, bf16[1,384,384]{2,1,0:T(8,128)(2,1)S(1)}, u32[]{:S(2)}, u32[]{:S(2)}) %collective-permute-start.31) | collective-permute-done | bytes 294944 | tf_op jit(solution)/shard_map/ppermute | solution.py:898
  620.2 1.0 maximum_convert_fusion.2
  621.2 7.0 %shard_map.310 = bf16[4,225,4,768]{3,2,1,0:T(4,128)(2,1)} custom-call(s32[16]{0:T(128)} %get-tuple-element.34.take, bf16[4,4,232,768]{3,2,1,0:T(8,128)(2,1)} %bitcast.7.got), custom_call_target="tpu_custom_call" | custom-call | tf_op jit(solution)/shard_map/pallas_call | solution.py:640
  628.9 1.1 maximum_convert_fusion
  630.4 1.1 maximum_convert_fusion.1
  (154 shorter events, 19.0 us)
Async XLA Ops:
  18.5 5.5 copy-start.12
  18.5 5.5 copy-start.13
  18.5 5.5 copy-start.14
  18.5 5.5 copy-start.6
  18.5 104.4 %all-to-all-start = ((bf16[4,928,768]{2,1,0:T(8,128)(2,1)}), bf16[4,928,768]{2,1,0:T(8,128)(2,1)}, u32[]{:S(2)}, u32[]{:S(2)}) async-start(bf16[4,928,768]{2,1,0:T(8,128)(2,1)} %bitcast.82), calls=%async_computation | async-start | bytes 11403264 | tf_op jit(solution)/shard_map/all_to_all | solution.py:983
  269.7 180.6 %collective-permute-start.17 = (f32[6144]{0:T(1024)}, f32[6144]{0:T(1024)}, u32[]{:S(2)}, u32[]{:S(2)}) collective-permute-start(f32[6144]{0:T(1024)} %pad_maximum_fusion), channel_id=1, source_target_pairs={{0,1},{1,0},{2,3},{3,2},{4,5},{5,4},{6,7},{7,6},{8,9},{9,8},{10,11... | collective-permute-start | bytes 73736 | tf_op jit(solution)/shard_map/ppermute | solution.py:898
  272.4 116.0 %collective-permute-start.11 = (bf16[768,384]{1,0:T(8,128)(2,1)}, bf16[768,384]{1,0:T(8,128)(2,1)}, u32[]{:S(2)}, u32[]{:S(2)}) collective-permute-start(bf16[768,384]{1,0:T(8,128)(2,1)} %constant_dynamic-slice_fusion.5), channel_id=1, source_target_pairs={{0,1},{1,0},{2,3},{3,2},{4,5},{5,4},{6,7},{7,6},{8,9},{9,8},{10,11... | collective-permute-start | bytes 1769480 | tf_op jit(solution)/shard_map/ppermute | solution.py:898
  355.5 31.4 %copy-start = (bf16[768,2304]{1,0:T(8,128)(2,1)S(1)}, bf16[768,2304]{1,0:T(8,128)(2,1)}, u32[]{:S(2)}) copy-start(bf16[768,2304]{1,0:T(8,128)(2,1)} %get-tuple-element.47) | copy-start | bytes 10616836
  377.0 11.4 %copy-start.2 = (bf16[768,768]{1,0:T(8,128)(2,1)S(1)}, bf16[768,768]{1,0:T(8,128)(2,1)}, u32[]{:S(2)}) copy-start(bf16[768,768]{1,0:T(8,128)(2,1)} %get-tuple-element.48) | copy-start | bytes 3538948
  378.6 25.0 %collective-permute-start = (f32[3072]{0:T(1024)S(1)}, f32[3072]{0:T(1024)S(1)}, u32[]{:S(2)}, u32[]{:S(2)}) collective-permute-start(f32[3072]{0:T(1024)S(1)} %pad_maximum_fusion.1), channel_id=1, source_target_pairs={{0,1},{1,0},{2,3},{3,2},{4,5},{5,4},{6,7},{7,6},{8,9},{9,8},{10,11... | collective-permute-start | bytes 36872 | tf_op jit(solution)/shard_map/ppermute | solution.py:898
  387.0 16.6 %copy-start.5 = (f32[1536]{0:T(1024)S(1)}, f32[1536]{0:T(1024)}, u32[]{:S(2)}) copy-start(f32[1536]{0:T(1024)} %reshape.140) | copy-start | bytes 18436
  387.0 63.3 %copy-start.4 = (f32[1,3072]{1,0:T(1,128)S(1)}, f32[1,3072]{1,0:T(1,128)}, u32[]{:S(2)}) copy-start(f32[1,3072]{1,0:T(1,128)} %copy-done.3) | copy-start | bytes 36868
  388.3 90.5 %collective-permute-start.5 = (bf16[768,1152]{1,0:T(8,128)(2,1)}, bf16[768,1152]{1,0:T(8,128)(2,1)}, u32[]{:S(2)}, u32[]{:S(2)}) collective-permute-start(bf16[768,1152]{1,0:T(8,128)(2,1)} %constant_dynamic-slice_fusion.7), channel_id=1, source_target_pairs={{0,1},{1,0},{2,3},{3,2},{4,5},{5,4},{6,7},{7,6},{8,9},{9,8},{10,11... | collective-permute-start | bytes 5308424 | tf_op jit(solution)/shard_map/ppermute | solution.py:898
  391.2 72.9 %collective-permute-start.12 = (bf16[4,96,384]{2,1,0:T(8,128)(2,1)}, bf16[4,96,384]{2,1,0:T(8,128)(2,1)}, u32[]{:S(2)}, u32[]{:S(2)}) collective-permute-start(bf16[4,96,384]{2,1,0:T(8,128)(2,1)} %dynamic-slice_bitcast_fusion.6), channel_id=1, source_target_pairs={{0,4},{4,0},{8,12},{12,8},{16,20},{20,16},{24,28},{28,24},{1,5},{5... | collective-permute-start | bytes 884744 | tf_op jit(solution)/shard_map/ppermute | solution.py:898
  403.6 48.4 %collective-permute-start.1 = (f32[3072]{0:T(1024)S(1)}, f32[3072]{0:T(1024)S(1)}, u32[]{:S(2)}, u32[]{:S(2)}) collective-permute-start(f32[3072]{0:T(1024)S(1)} %fusion.15), channel_id=1, source_target_pairs={{0,2},{1,3},{2,0},{3,1},{4,6},{5,7},{6,4},{7,5},{8,10},{9,11},{10,... | collective-permute-start | bytes 36872 | tf_op jit(solution)/shard_map/ppermute | solution.py:898
  451.7 9.7 %collective-permute-start.18 = (f32[6144]{0:T(1024)}, f32[6144]{0:T(1024)}, u32[]{:S(2)}, u32[]{:S(2)}) collective-permute-start(f32[6144]{0:T(1024)} %fusion.12), channel_id=1, source_target_pairs={{0,2},{1,3},{2,0},{3,1},{4,6},{5,7},{6,4},{7,5},{8,10},{9,11},{10,... | collective-permute-start | bytes 73736 | tf_op jit(solution)/shard_map/ppermute | solution.py:898
  452.0 5.2 collective-permute-start.2
  452.0 169.2 %all-to-all-start.1 = ((bf16[4,928,768]{2,1,0:T(8,128)(2,1)}), bf16[4,928,768]{2,1,0:T(8,128)(2,1)}, u32[]{:S(2)}, u32[]{:S(2)}) async-start(bf16[4,928,768]{2,1,0:T(8,128)(2,1)} %bitcast.81), calls=%async_computation.1 | async-start | bytes 11403264 | tf_op jit(solution)/shard_map/all_to_all | solution.py:983
  457.9 9.4 %collective-permute-start.3 = (f32[3072]{0:T(1024)S(1)}, f32[3072]{0:T(1024)S(1)}, u32[]{:S(2)}, u32[]{:S(2)}) collective-permute-start(f32[3072]{0:T(1024)S(1)} %add.204), channel_id=1, source_target_pairs={{0,8},{4,12},{8,0},{12,4},{16,24},{20,28},{24,16},{28,20},{1,9},{5... | collective-permute-start | bytes 36872 | tf_op jit(solution)/shard_map/ppermute | solution.py:898
  462.1 5.3 collective-permute-start.19
  465.3 6.1 collective-permute-start.13
  467.3 7.3 %collective-permute-start.4 = (f32[3072]{0:T(1024)S(1)}, f32[3072]{0:T(1024)S(1)}, u32[]{:S(2)}, u32[]{:S(2)}) collective-permute-start(f32[3072]{0:T(1024)S(1)} %add.205), channel_id=1, source_target_pairs={{0,16},{4,20},{8,24},{12,28},{16,0},{20,4},{24,8},{28,12},{1,17},{... | collective-permute-start | bytes 36872 | tf_op jit(solution)/shard_map/ppermute | solution.py:898
  467.4 7.7 %collective-permute-start.20 = (f32[6144]{0:T(1024)S(1)}, f32[6144]{0:T(1024)S(1)}, u32[]{:S(2)}, u32[]{:S(2)}) collective-permute-start(f32[6144]{0:T(1024)S(1)} %add.233), channel_id=1, source_target_pairs={{0,8},{4,12},{8,0},{12,4},{16,24},{20,28},{24,16},{28,20},{1,9},{5... | collective-permute-start | bytes 73736 | tf_op jit(solution)/shard_map/ppermute | solution.py:898
  471.5 5.6 collective-permute-start.14
  472.5 56.4 %slice-start.2 = ((s8[4718592]{0:T(1024)(128)(4,1)}), s8[4194304]{0:T(1024)(128)(4,1)S(1)}, s32[]{:S(2)}) async-start(s8[4718592]{0:T(1024)(128)(4,1)} %bitcast.87), calls=%async_computation.4 | async-start | bytes 8388608
  474.5 54.4 %collective-permute-start.22 = (bf16[768,1536]{1,0:T(8,128)(2,1)S(1)}, bf16[768,1536]{1,0:T(8,128)(2,1)S(1)}, u32[]{:S(2)}, u32[]{:S(2)}) collective-permute-start(bf16[768,1536]{1,0:T(8,128)(2,1)S(1)} %constant_dynamic-slice_fusion.3), channel_id=1, source_target_pairs={{0,1},{1,0},{2,3},{3,2},{4,5},{5,4},{6,7},{7,6},{8,9},{9,8},{10,11... | collective-permute-start | bytes 7077896 | tf_op jit(solution)/shard_map/ppermute | solution.py:898
  474.6 65.4 %collective-permute-start.28 = (bf16[3072,384]{1,0:T(8,128)(2,1)S(1)}, bf16[3072,384]{1,0:T(8,128)(2,1)S(1)}, u32[]{:S(2)}, u32[]{:S(2)}) collective-permute-start(bf16[3072,384]{1,0:T(8,128)(2,1)S(1)} %constant_dynamic-slice_fusion.1), channel_id=1, source_target_pairs={{0,1},{1,0},{2,3},{3,2},{4,5},{5,4},{6,7},{7,6},{8,9},{9,8},{10,11... | collective-permute-start | bytes 7077896 | tf_op jit(solution)/shard_map/ppermute | solution.py:898
  475.1 6.7 %collective-permute-start.21 = (f32[6144]{0:T(1024)S(1)}, f32[6144]{0:T(1024)S(1)}, u32[]{:S(2)}, u32[]{:S(2)}) collective-permute-start(f32[6144]{0:T(1024)S(1)} %add.234), channel_id=1, source_target_pairs={{0,16},{4,20},{8,24},{12,28},{16,0},{20,4},{24,8},{28,12},{1,17},{... | collective-permute-start | bytes 73736 | tf_op jit(solution)/shard_map/ppermute | solution.py:898
  477.1 51.9 %slice-start.3 = ((s8[4718592]{0:T(1024)(128)(4,1)}), s8[524288]{0:T(1024)(128)(4,1)S(1)}, s32[]{:S(2)}) async-start(s8[4718592]{0:T(1024)(128)(4,1)} %bitcast.87), calls=%async_computation.5 | async-start | bytes 1048576
  477.1 45.9 %collective-permute-start.15 = (bf16[96,384]{1,0:T(8,128)(2,1)S(1)}, bf16[96,384]{1,0:T(8,128)(2,1)S(1)}, u32[]{:S(2)}, u32[]{:S(2)}) collective-permute-start(bf16[96,384]{1,0:T(8,128)(2,1)S(1)} %fusion.11), channel_id=1, source_target_pairs={{0,2},{1,3},{2,0},{3,1},{4,6},{5,7},{6,4},{7,5},{8,10},{9,11},{10,... | collective-permute-start | bytes 221192 | tf_op jit(solution)/shard_map/ppermute | solution.py:898
  480.8 44.3 %collective-permute-start.6 = (bf16[4,96,1152]{2,1,0:T(8,128)(2,1)S(1)}, bf16[4,96,1152]{2,1,0:T(8,128)(2,1)S(1)}, u32[]{:S(2)}, u32[]{:S(2)}) collective-permute-start(bf16[4,96,1152]{2,1,0:T(8,128)(2,1)S(1)} %dynamic-slice_bitcast_fusion.2), channel_id=1, source_target_pairs={{0,4},{4,0},{8,12},{12,8},{16,20},{20,16},{24,28},{28,24},{1,5},{5... | collective-permute-start | bytes 2654216 | tf_op jit(solution)/shard_map/ppermute | solution.py:898
  523.0 1.3 collective-permute-start.16
  525.4 14.6 %slice-start = ((s8[4718592]{0:T(1024)(128)(4,1)}), s8[4194304]{0:T(1024)(128)(4,1)S(1)}, s32[]{:S(2)}) async-start(s8[4718592]{0:T(1024)(128)(4,1)} %bitcast.85), calls=%async_computation.2 | async-start | bytes 8388608
  525.4 14.6 %slice-start.1 = ((s8[4718592]{0:T(1024)(128)(4,1)}), s8[524288]{0:T(1024)(128)(4,1)S(1)}, s32[]{:S(2)}) async-start(s8[4718592]{0:T(1024)(128)(4,1)} %bitcast.85), calls=%async_computation.3 | async-start | bytes 1048576
  525.4 14.3 %collective-permute-start.7 = (bf16[2,96,1152]{2,1,0:T(8,128)(2,1)S(1)}, bf16[2,96,1152]{2,1,0:T(8,128)(2,1)S(1)}, u32[]{:S(2)}, u32[]{:S(2)}) collective-permute-start(bf16[2,96,1152]{2,1,0:T(8,128)(2,1)S(1)} %dynamic-slice_bitcast_fusion.5), channel_id=1, source_target_pairs={{0,8},{4,12},{8,0},{12,4},{16,24},{20,28},{24,16},{28,20},{1,9},{5... | collective-permute-start | bytes 1327112 | tf_op jit(solution)/shard_map/ppermute | solution.py:898
  529.8 28.8 %collective-permute-start.23 = (bf16[4,96,1536]{2,1,0:T(8,128)(2,1)S(1)}, bf16[4,96,1536]{2,1,0:T(8,128)(2,1)S(1)}, u32[]{:S(2)}, u32[]{:S(2)}) collective-permute-start(bf16[4,96,1536]{2,1,0:T(8,128)(2,1)S(1)} %dynamic-slice_bitcast_fusion.1), channel_id=1, source_target_pairs={{0,4},{4,0},{8,12},{12,8},{16,20},{20,16},{24,28},{28,24},{1,5},{5... | collective-permute-start | bytes 3538952 | tf_op jit(solution)/shard_map/ppermute | solution.py:898
  539.9 12.9 %collective-permute-start.8 = (bf16[1,96,1152]{2,1,0:T(8,128)(2,1)S(1)}, bf16[1,96,1152]{2,1,0:T(8,128)(2,1)S(1)}, u32[]{:S(2)}, u32[]{:S(2)}) collective-permute-start(bf16[1,96,1152]{2,1,0:T(8,128)(2,1)S(1)} %constant_dynamic-slice_fusion.6), channel_id=1, source_target_pairs={{0,16},{4,20},{8,24},{12,28},{16,0},{20,4},{24,8},{28,12},{1,17},{... | collective-permute-start | bytes 663560 | tf_op jit(solution)/shard_map/ppermute | solution.py:898
  540.8 42.8 %collective-permute-start.29 = (bf16[4,384,384]{2,1,0:T(8,128)(2,1)S(1)}, bf16[4,384,384]{2,1,0:T(8,128)(2,1)S(1)}, u32[]{:S(2)}, u32[]{:S(2)}) collective-permute-start(bf16[4,384,384]{2,1,0:T(8,128)(2,1)S(1)} %dynamic-slice_bitcast_fusion), channel_id=1, source_target_pairs={{0,4},{4,0},{8,12},{12,8},{16,20},{20,16},{24,28},{28,24},{1,5},{5... | collective-permute-start | bytes 3538952 | tf_op jit(solution)/shard_map/ppermute | solution.py:898
  552.9 31.5 %collective-permute-start.9 = (bf16[96,1152]{1,0:T(8,128)(2,1)S(1)}, bf16[96,1152]{1,0:T(8,128)(2,1)S(1)}, u32[]{:S(2)}, u32[]{:S(2)}) collective-permute-start(bf16[96,1152]{1,0:T(8,128)(2,1)S(1)} %fusion.10), channel_id=1, source_target_pairs={{0,2},{1,3},{2,0},{3,1},{4,6},{5,7},{6,4},{7,5},{8,10},{9,11},{10,... | collective-permute-start | bytes 663560 | tf_op jit(solution)/shard_map/ppermute | solution.py:898
  559.0 25.5 %collective-permute-start.24 = (bf16[2,96,1536]{2,1,0:T(8,128)(2,1)S(1)}, bf16[2,96,1536]{2,1,0:T(8,128)(2,1)S(1)}, u32[]{:S(2)}, u32[]{:S(2)}) collective-permute-start(bf16[2,96,1536]{2,1,0:T(8,128)(2,1)S(1)} %dynamic-slice_bitcast_fusion.4), channel_id=1, source_target_pairs={{0,8},{4,12},{8,0},{12,4},{16,24},{20,28},{24,16},{28,20},{1,9},{5... | collective-permute-start | bytes 1769480 | tf_op jit(solution)/shard_map/ppermute | solution.py:898
  583.9 21.3 %collective-permute-start.30 = (bf16[2,384,384]{2,1,0:T(8,128)(2,1)S(1)}, bf16[2,384,384]{2,1,0:T(8,128)(2,1)S(1)}, u32[]{:S(2)}, u32[]{:S(2)}) collective-permute-start(bf16[2,384,384]{2,1,0:T(8,128)(2,1)S(1)} %dynamic-slice_bitcast_fusion.3), channel_id=1, source_target_pairs={{0,8},{4,12},{8,0},{12,4},{16,24},{20,28},{24,16},{28,20},{1,9},{5... | collective-permute-start | bytes 1769480 | tf_op jit(solution)/shard_map/ppermute | solution.py:898
  584.4 21.7 %collective-permute-start.10 = (bf16[96,1152]{1,0:T(8,128)(2,1)S(1)}, bf16[96,1152]{1,0:T(8,128)(2,1)S(1)}, u32[]{:S(2)}, u32[]{:S(2)}) collective-permute-start(bf16[96,1152]{1,0:T(8,128)(2,1)S(1)} %add_convert_fusion.8), channel_id=1, source_target_pairs={{0,1},{1,0},{2,3},{3,2},{4,5},{5,4},{6,7},{7,6},{8,9},{9,8},{10,11... | collective-permute-start | bytes 663560 | tf_op jit(solution)/shard_map/ppermute | solution.py:898
  584.7 20.9 %collective-permute-start.25 = (bf16[1,96,1536]{2,1,0:T(8,128)(2,1)S(1)}, bf16[1,96,1536]{2,1,0:T(8,128)(2,1)S(1)}, u32[]{:S(2)}, u32[]{:S(2)}) collective-permute-start(bf16[1,96,1536]{2,1,0:T(8,128)(2,1)S(1)} %constant_dynamic-slice_fusion.2), channel_id=1, source_target_pairs={{0,16},{4,20},{8,24},{12,28},{16,0},{20,4},{24,8},{28,12},{1,17},{... | collective-permute-start | bytes 884744 | tf_op jit(solution)/shard_map/ppermute | solution.py:898
  605.5 14.0 %collective-permute-start.31 = (bf16[1,384,384]{2,1,0:T(8,128)(2,1)S(1)}, bf16[1,384,384]{2,1,0:T(8,128)(2,1)S(1)}, u32[]{:S(2)}, u32[]{:S(2)}) collective-permute-start(bf16[1,384,384]{2,1,0:T(8,128)(2,1)S(1)} %constant_dynamic-slice_fusion), channel_id=1, source_target_pairs={{0,16},{4,20},{8,24},{12,28},{16,0},{20,4},{24,8},{28,12},{1,17},{... | collective-permute-start | bytes 884744 | tf_op jit(solution)/shard_map/ppermute | solution.py:898
  605.7 14.4 %collective-permute-start.26 = (bf16[96,1536]{1,0:T(8,128)(2,1)S(1)}, bf16[96,1536]{1,0:T(8,128)(2,1)S(1)}, u32[]{:S(2)}, u32[]{:S(2)}) collective-permute-start(bf16[96,1536]{1,0:T(8,128)(2,1)S(1)} %fusion.7), channel_id=1, source_target_pairs={{0,2},{1,3},{2,0},{3,1},{4,6},{5,7},{6,4},{7,5},{8,10},{9,11},{10,... | collective-permute-start | bytes 884744 | tf_op jit(solution)/shard_map/ppermute | solution.py:898
  619.6 9.0 %collective-permute-start.32 = (bf16[384,384]{1,0:T(8,128)(2,1)S(1)}, bf16[384,384]{1,0:T(8,128)(2,1)S(1)}, u32[]{:S(2)}, u32[]{:S(2)}) collective-permute-start(bf16[384,384]{1,0:T(8,128)(2,1)S(1)} %fusion.8), channel_id=1, source_target_pairs={{0,2},{1,3},{2,0},{3,1},{4,6},{5,7},{6,4},{7,5},{8,10},{9,11},{10,... | collective-permute-start | bytes 884744 | tf_op jit(solution)/shard_map/ppermute | solution.py:898
  620.1 8.7 %collective-permute-start.27 = (bf16[96,1536]{1,0:T(8,128)(2,1)S(1)}, bf16[96,1536]{1,0:T(8,128)(2,1)S(1)}, u32[]{:S(2)}, u32[]{:S(2)}) collective-permute-start(bf16[96,1536]{1,0:T(8,128)(2,1)S(1)} %add_convert_fusion.6), channel_id=1, source_target_pairs={{0,1},{1,0},{2,3},{3,2},{4,5},{5,4},{6,7},{7,6},{8,9},{9,8},{10,11... | collective-permute-start | bytes 884744 | tf_op jit(solution)/shard_map/ppermute | solution.py:898
  628.7 1.6 collective-permute-start.33
  (7 other events, 28.7 us)

commit v3 on v2

--- a/solution.py
+++ b/solution.py
@@ -13,16 +13,18 @@
 WINDOW = 256
 FAR = 1e12
 EPS = 1e-06
+BLOCKS = 8
 VMEM_LIMIT = 60 * 1024 * 1024
 
 F32 = jnp.float32
 BF16 = jnp.bfloat16
 
 OFF, CNT, IMG, LIVE, PEER, SPOT, MISC = 0, 16, 32, 48, 64, 80, 96
-N_FWD, N_BWD, ROWS_FWD, ROWS_BWD, N_LIVE = MISC, MISC + 1, MISC + 2, MISC + 3, MISC + 4
+N_FWD, N_BWD, ROWS_FWD, ROWS_BWD, N_LIVE, CORE = range(MISC, MISC + 6)
 PLACES = 128
 
 GAIN_ONE, SHIFT_ONE, QKV_B, OUT_B, GAIN_TWO, SHIFT_TWO, DOWN_B, UP_B = 0, 1, 2, 5, 6, 7, 8, 9
+VECTORS = (GAIN_ONE, SHIFT_ONE, QKV_B, QKV_B + 2, OUT_B, GAIN_TWO, SHIFT_TWO, DOWN_B, UP_B)
 
 
 def dot(a, b):
@@ -118,7 +120,8 @@
     return jnp.where(far, FAR, jnp.sqrt(down * down + across * across))
 
 
-def prepare_kernel(every, counts, present, slots, me, cot, meta, take, send):
+def prepare_kernel(every, counts, present, slots, me, cot, *rest):
+    *lines, meta, take, vecs, send = rest
     step = pl.program_id(0)
     steps, length, images, width = pl.num_programs(0), cot.shape[1], cot.shape[2], cot.shape[3]
     group = every.shape[0]
@@ -146,6 +149,12 @@
 
             return body
 
+        meta[CORE] = me[0] % 2
+        vecs[...] = jnp.zeros_like(vecs)
+        for row, values in zip(VECTORS, lines):
+            for n in range(values.shape[0] // width):
+                piece = values[n * width : (n + 1) * width]
+                vecs[row + n : row + n + 1, :] = piece.reshape(1, width)
         zero = jnp.int32(0)
         total = counts.shape[0] * images
         spot, off = lax.fori_loop(0, total, fill(1), (zero, zero))
@@ -314,8 +323,8 @@
 def mlp_kernel(
     chunk, length, meta, cot_in, att_in, tokens_in,
     vecs, out_w, up_w, down_w,
-    y_send, mid_grad, att_grad, up_g, down_g, out_g, vec_g, upb_g,
-    up_b, cot, y_all, up_acc, down_acc, out_acc, h2_s, h2t_s, dzt_s, z_s, g_s, stage, sem,
+    y_send, mid_grad, att_grad, keep_g, send_g, vec_g, upb_g,
+    up_b, cot, y_all, up_acc, down_acc, out_acc, h2_s, h2t_s, dzt_s, z_s, g_s, stage, spare, sem,
 ):
     step = pl.program_id(0)
     tiles = cot.shape[0] // TILE - WINDOW // TILE
@@ -409,34 +418,54 @@
 
     @pl.when(step == images + tiles)
     def _():
-        size = stage.shape[1]
+        share = width // BLOCKS
+        long = hidden // BLOCKS
+        half = long // 2
         jobs = []
-        for start in range(0, width, size):
-            jobs.append((up_acc, start, up_g, False))
-            jobs.append((out_acc, start, out_g, False))
-        for start in range(0, hidden, size):
-            jobs.append((down_acc, start, down_g, True))
-
-        def copy(n):
-            source, start, target, _ = jobs[n]
-            columns = target.shape[1]
-            return pltpu.make_async_copy(
-                stage.at[n % 2, :, pl.ds(0, columns)], target.at[pl.ds(start, size)], sem.at[n % 2]
-            )
-
-        for n, (source, start, target, flip) in enumerate(jobs):
+        for n in range(BLOCKS):
+            for c in range(hidden // width):
+                jobs.append(("up", n, c // 2, c % 2 * share, share, c))
+            for h in range(2):
+                jobs.append(("down", n, h, 2 * share, half, 0))
+                jobs.append(("out", n, h, 2 * share + half, share // 2, 0))
+
+        def copy(n, target):
+            _, block, _, at, rows, _ = jobs[n]
+            src = stage.at[n % 2, pl.ds(0, rows)]
+            return pltpu.make_async_copy(src, target.at[block, pl.ds(at, rows)], sem.at[n % 2])
+
+        def start(n):
+            h = jobs[n][2]
+
+            @pl.when(meta[CORE] == h)
+            def _():
+                copy(n, keep_g).start()
+
+            @pl.when(meta[CORE] != h)
+            def _():
+                copy(n, send_g).start()
+
+        for n, (kind, block, h, _, rows, c) in enumerate(jobs):
             if n >= 2:
-                copy(n - 2).wait()
-            if flip:
+                copy(n - 2, keep_g).wait()
+            if kind == "up":
+                piece = up_acc[block * share : (block + 1) * share, c * width : (c + 1) * width]
+                stage[n % 2, :rows, :] = piece.astype(BF16)
+            elif kind == "out":
+                first = block * share + h * rows
+                stage[n % 2, :rows, :] = out_acc[first : first + rows, :].astype(BF16)
+            elif h == 0:
                 for low in range(0, width, 256):
-                    block = source[pl.ds(low, 256), pl.ds(start, size)].astype(BF16)
-                    stage[n % 2, :, pl.ds(low, 256)] = turned(block)
+                    cols = slice(low, low + 256)
+                    piece = down_acc[cols, block * long : (block + 1) * long].astype(BF16)
+                    flipped = turned(piece)
+                    stage[n % 2, :half, cols] = flipped[:half]
+                    spare[:, cols] = flipped[half:]
             else:
-                columns = target.shape[1]
-                stage[n % 2, :, pl.ds(0, columns)] = source[pl.ds(start, size), :].astype(BF16)
-            copy(n).start()
-        copy(len(jobs) - 2).wait()
-        copy(len(jobs) - 1).wait()
+                stage[n % 2, :half, :] = spare[...]
+            start(n)
+        copy(len(jobs) - 2, keep_g).wait()
+        copy(len(jobs) - 1, keep_g).wait()
 
     spot = step - images - tiles
 
@@ -524,7 +553,7 @@
             copy(step).wait()
 
 
-def qkv_grad_kernel(meta, packed_grad, tokens, vecs, weight_g, bias_g, acc, stage, sem):
+def qkv_grad_kernel(meta, packed_grad, tokens, vecs, keep_g, send_g, bias_g, acc, stage, sem):
     tile = pl.program_id(0)
     width = tokens.shape[1]
 
@@ -550,21 +579,35 @@
 
     @pl.when(tile == pl.num_programs(0) - 1)
     def _():
-        size = stage.shape[1]
-        count = width // size
-
-        def copy(n):
+        rows = width // BLOCKS // 2
+        jobs = [(n, h, c) for n in range(BLOCKS) for h in range(2) for c in range(3)]
+
+        def copy(n, target):
+            block, _, c = jobs[n]
             return pltpu.make_async_copy(
-                stage.at[n % 2], weight_g.at[pl.ds(n * size, size)], sem.at[n % 2]
+                stage.at[n % 2], target.at[block, pl.ds(c * rows, rows)], sem.at[n % 2]
             )
 
-        for n in range(count):
+        def start(n):
+            h = jobs[n][1]
+
+            @pl.when(meta[CORE] == h)
+            def _():
+                copy(n, keep_g).start()
+
+            @pl.when(meta[CORE] != h)
+            def _():
+                copy(n, send_g).start()
+
+        for n, (block, h, c) in enumerate(jobs):
             if n >= 2:
-                copy(n - 2).wait()
-            stage[n % 2] = acc[pl.ds(n * size, size), :].astype(BF16)
-            copy(n).start()
-        copy(count - 2).wait()
-        copy(count - 1).wait()
+                copy(n - 2, keep_g).wait()
+            first = (2 * block + h) * rows
+            piece = acc[first : first + rows, c * width : (c + 1) * width]
+            stage[n % 2] = piece.astype(BF16)
+            start(n)
+        copy(len(jobs) - 2, keep_g).wait()
+        copy(len(jobs) - 1, keep_g).wait()
 
 
 def token_grad_kernel(meta, packed_grad, tokens, mid_grad, vecs, weight, out, vec_g, held):
@@ -613,7 +656,7 @@
     return pl.BlockSpec(memory_space=pltpu.SMEM)
 
 
-def prepare(every, counts, present, slots, me, cotangent):
+def prepare(every, counts, present, slots, me, cotangent, *vectors):
     steps, length, images, width = cotangent.shape
     group = every.shape[0]
     padded = (length + 7) // 8 * 8
@@ -622,17 +665,21 @@
         out_shape=(
             jax.ShapeDtypeStruct((PLACES,), jnp.int32),
             jax.ShapeDtypeStruct((steps * images,), jnp.int32),
+            jax.ShapeDtypeStruct((16, width), F32),
             jax.ShapeDtypeStruct((group, steps, padded, width), BF16),
         ),
         grid=(steps,),
-        in_specs=[small()] * 5 + [pl.BlockSpec((1, length, images, width), lambda m: (m, 0, 0, 0))],
+        in_specs=[small()] * 5
+        + [pl.BlockSpec((1, length, images, width), lambda m: (m, 0, 0, 0))]
+        + [whole(*vector.shape) for vector in vectors],
         out_specs=[
             small(),
             small(),
+            whole(16, width),
             pl.BlockSpec((group, 1, padded, width), lambda m: (0, m, 0, 0)),
         ],
         compiler_params=params(),
-    )(every, counts, present, slots, me, cotangent)
+    )(every, counts, present, slots, me, cotangent, *vectors)
 
 
 def place(take, got, length):
@@ -707,6 +754,7 @@
     rows = packed.shape[0]
     tiles = (rows - WINDOW) // TILE
     hidden = up_w.shape[1]
+    parcel = (2 * width + hidden // 2 + width // 2) // BLOCKS
     last = images - 1
 
     def fwd_tile(s, meta):
@@ -721,9 +769,8 @@
             jax.ShapeDtypeStruct((images, padded, width), BF16),
             jax.ShapeDtypeStruct((rows, width), F32),
             jax.ShapeDtypeStruct((rows, width), BF16),
-            jax.ShapeDtypeStruct((width, hidden), BF16),
-            jax.ShapeDtypeStruct((hidden, width), BF16),
-            jax.ShapeDtypeStruct((width, width), BF16),
+            jax.ShapeDtypeStruct((BLOCKS, parcel, width), BF16),
+            jax.ShapeDtypeStruct((BLOCKS, parcel, width), BF16),
             jax.ShapeDtypeStruct((8, width), F32),
             jax.ShapeDtypeStruct((8, hidden), F32),
         ),
@@ -750,7 +797,6 @@
                 pl.BlockSpec((TILE, width), bwd_tile),
                 pl.BlockSpec(memory_space=pl.ANY),
                 pl.BlockSpec(memory_space=pl.ANY),
-                pl.BlockSpec(memory_space=pl.ANY),
                 whole(8, width),
                 whole(8, hidden),
             ],
@@ -766,7 +812,8 @@
                 pltpu.VMEM((width, TILE), BF16),
                 pltpu.VMEM((TILE, width), F32),
                 pltpu.VMEM((TILE, width), F32),
-                pltpu.VMEM((2, 256, hidden), BF16),
+                pltpu.VMEM((2, hidden // BLOCKS // 2, width), BF16),
+                pltpu.VMEM((hidden // BLOCKS // 2, width), BF16),
                 pltpu.SemaphoreType.DMA((2,)),
             ],
         ),
@@ -775,7 +822,7 @@
     )(meta, cot, att, packed, vecs, out_w, up_w, down_w)
 
 
-def attend_back(first, count, meta, slopes, qkv, att_grad, totals, rows_in, cols_in, earlier):
+def attend_back(first, count, expected, meta, slopes, qkv, att_grad, totals, rows_in, cols_in, earlier):
     total, wide = qkv.shape
     width = wide // 3
     per, length = rows_in.shape[1:]
@@ -817,7 +864,7 @@
         ),
         input_output_aliases={7: 0} if earlier else {},
         compiler_params=params(),
-        cost_estimate=cost(15),
+        cost_estimate=cost(expected),
     )(meta, slopes, qkv, att_grad, totals, rows_in, cols_in, *earlier)
 
 
@@ -827,11 +874,13 @@
 
 def qkv_grad(meta, packed_grad, packed, vecs):
     rows, width = packed.shape
+    parcel = 3 * width // 2 // BLOCKS
     tiles = (rows - WINDOW) // TILE
     return pl.pallas_call(
         qkv_grad_kernel,
         out_shape=(
-            jax.ShapeDtypeStruct((width, 3 * width), BF16),
+            jax.ShapeDtypeStruct((BLOCKS, parcel, width), BF16),
+            jax.ShapeDtypeStruct((BLOCKS, parcel, width), BF16),
             jax.ShapeDtypeStruct((8, 3 * width), F32),
         ),
         grid_spec=pltpu.PrefetchScalarGridSpec(
@@ -842,10 +891,14 @@
                 pl.BlockSpec((TILE, width), bwd_tile),
                 whole(*vecs.shape),
             ],
-            out_specs=[pl.BlockSpec(memory_space=pl.ANY), whole(8, 3 * width)],
+            out_specs=[
+                pl.BlockSpec(memory_space=pl.ANY),
+                pl.BlockSpec(memory_space=pl.ANY),
+                whole(8, 3 * width),
+            ],
             scratch_shapes=[
                 pltpu.VMEM((width, 3 * width), F32),
-                pltpu.VMEM((2, 256, 3 * width), BF16),
+                pltpu.VMEM((2, width // BLOCKS // 2, width), BF16),
                 pltpu.SemaphoreType.DMA((2,)),
             ],
         ),
@@ -913,25 +966,57 @@
     return added(keep, swap(send, axis, bit))
 
 
-def summed_rows(matrix):
-    size = lax.axis_size("dp")
-    rows, columns = matrix.shape
-    mine = bit_of("bal", 1)
-    half = columns // 2
-    keep = lax.dynamic_slice(matrix, (0, mine * half), (rows, half))
-    send = lax.dynamic_slice(matrix, (0, (1 - mine) * half), (rows, half))
-    block = added(keep, swap(send, "bal", 1))
+def unpacked(mine, other, shapes):
+    swapped = bit_of("bal", 1) == 1
+    first = jnp.where(swapped, other, mine)
+    second = jnp.where(swapped, mine, other)
+    lead, width = mine.shape[:-2], mine.shape[-1]
+    out, at = [], 0
+    for rows, columns, by_rows in shapes:
+        wide = columns // width
+        part = rows * wide // 2
+        if by_rows:
+            parts = [
+                jnp.concatenate(
+                    [half[..., at + c * (rows // 2) : at + (c + 1) * (rows // 2), :] for c in range(wide)],
+                    axis=-1,
+                )
+                for half in (first, second)
+            ]
+            out.append(jnp.concatenate(parts, axis=-2))
+        else:
+            parts = [
+                half[..., at + c * rows : at + (c + 1) * rows, :]
+                for half in (first, second)
+                for c in range(wide // 2)
+            ]
+            out.append(jnp.concatenate(parts, axis=-1))
+        at += part
+    return [matrix.reshape(lead[:-1] + (-1, matrix.shape[-1])) if lead else matrix for matrix in out]
+
+
+def spread_sum(keep, send, shapes):
+    return [
+        lax.psum(lax.psum_scatter(matrix, "dp", scatter_dimension=0, tiled=True), "bal").astype(F32)
+        for matrix in unpacked(keep, send, shapes)
+    ]
+
+
+def joined(block, shapes):
+    block = added(block, swap(block, "bal", 2))
+    return [matrix.astype(F32) for matrix in unpacked(block, swap(block, "bal", 1), shapes)]
+
+
+def halved(block):
     bit = 1
-    while bit < size:
-        left = size // bit
-        block = half_sums(block.reshape(left // 2, 2, rows // size, half), "dp", bit, 1)
+    while bit < lax.axis_size("dp"):
+        block = half_sums(block.reshape((-1, 2) + block.shape[-2:]), "dp", bit, 1)
         bit *= 2
-    block = block.reshape(rows // size, half)
-    block = added(block, swap(block, "bal", 2))
-    other = swap(block, "bal", 1)
-    first = jnp.where(mine == 0, block, other)
-    second = jnp.where(mine == 0, other, block)
-    return jnp.concatenate([first, second], axis=1).astype(F32)
+    return block.reshape(block.shape[-2:])
+
+
+def after(value, *others):
+    return lax.optimization_barrier((value,) + others)[0]
 
 
 def summed(block):
@@ -969,13 +1054,6 @@
     hidden = up_weight.shape[1]
     group = lax.axis_size("bal")
     total = steps * images
-    vecs = jnp.concatenate(
-        [
-            first_gain, first_shift, query_bias, jnp.zeros_like(query_bias), value_bias,
-            out_bias, second_gain, second_shift, down_bias, up_bias,
-            jnp.zeros((7 * width - hidden,), F32),
-        ]
-    ).reshape(16, width)
     slopes = jnp.exp2(-8.0 * (jnp.arange(16, dtype=F32) + 1.0) / HEADS)
 
     def exchange(blocks):
@@ -985,54 +1063,80 @@
     def turn(array):
         return jnp.transpose(array, (0, 2, 1, 3))
 
-    meta, take, cot_send = prepare(
+    meta, take, vecs, cot_send = prepare(
         lax.all_gather(slots, "bal"), counts, present, slots,
         lax.axis_index("bal").astype(jnp.int32).reshape(1), turn(cotangent),
+        first_gain, first_shift, query_bias, value_bias, out_bias, second_gain, second_shift,
+        down_bias, up_bias,
     )
     cot_home = exchange(cot_send).reshape(total, -1, width)
     packed, qkv, att, totals = first_half(meta, slopes, turn(tokens), rows, cols, vecs, qkv_weight)
-    y_send, mid_grad, att_grad, up_g, down_g, out_g, vec_two, upb_g = mlp(
+    y_send, mid_grad, att_grad, keep_two, send_two, vec_two, upb_g = mlp(
         meta, cot_home, att, packed, vecs, out_weight, up_weight, down_weight, length
     )
-    y_got = exchange(y_send).reshape(group, steps, -1, width)
-    up_rows, down_rows, out_rows = summed_rows(up_g), summed_rows(down_g), summed_rows(out_g)
-    vec_two = summed(jnp.concatenate([vec_two[:4].reshape(-1), upb_g[0]]))
-
-    quarter = images
-    earlier = ()
-    for first in range(0, total, quarter):
-        packed_grad = attend_back(
-            first, quarter, meta, slopes, qkv, att_grad, totals, rows, cols, earlier
+    y_got = exchange(y_send)
+
+    share, long = width // BLOCKS, hidden // BLOCKS
+    shapes_two = ((share, hidden, False), (long, width, True), (share, width, True))
+    shapes_one = ((share, 3 * width, True),)
+    direct = lax.axis_size("dp") == BLOCKS
+
+    def back(first, count, expected, table, earlier):
+        return attend_back(
+            first, count, expected, table, slopes, qkv, att_grad, totals, rows, cols, earlier
         )
-        earlier = (packed_grad,)
-    qkv_g, bias_g = qkv_grad(meta, packed_grad, packed, vecs)
-    qkv_rows = summed_rows(qkv_g)
+
+    lead = max(images // 2, 1)
+    packed_grad = back(0, lead, 15, meta, ())
+    table = meta
+    if direct:
+        sum_two = added(after(keep_two, packed_grad), swap(send_two, "bal", 1))
+        share_two = lax.psum_scatter(sum_two, "dp", scatter_dimension=0, tiled=True)[0]
+        table = after(meta, sum_two)
+    packed_grad = back(lead, total - lead, 500, table, (packed_grad,))
+    keep_one, send_one, bias_g = qkv_grad(after(table, y_got), packed_grad, packed, vecs)
+    output = place(after(take, keep_one), y_got.reshape(group, steps, -1, width), length)
+    table = after(table, output)
+    if direct:
+        sum_one = added(keep_one, swap(send_one, "bal", 1))
+        table = after(table, sum_one)
     input_grad, vec_one = token_grad(
-        meta, packed_grad, packed, mid_grad, vecs, qkv_weight, steps, length, images
+        table, packed_grad, packed, mid_grad, vecs, qkv_weight, steps, length, images
     )
-    vec_one = summed(
-        jnp.concatenate([vec_one[:2].reshape(-1), bias_g[0, :width], bias_g[0, 2 * width :]])
+    if direct:
+        (qkv_rows,) = joined(halved(sum_one), shapes_one)
+        up_rows, down_rows, out_rows = joined(share_two, shapes_two)
+    else:
+        (qkv_rows,) = spread_sum(keep_one, send_one, shapes_one)
+        up_rows, down_rows, out_rows = spread_sum(keep_two, send_two, shapes_two)
+    vectors = summed(
+        jnp.concatenate(
+            [
+                vec_one[:2].reshape(-1), bias_g[0, :width], bias_g[0, 2 * width :],
+                vec_two[:4].reshape(-1), upb_g[0],
+            ]
+        )
     )
 
-    def vector(array, n):
-        return array[n * width : (n + 1) * width]
+    def vector(n):
+        return vectors[n * width : (n + 1) * width]
 
     return (
-        turn(place(take, y_got, length)),
+        turn(output),
         turn(input_grad),
-        vector(vec_one, 0),
-        vector(vec_one, 1),
+        vector(0),
+        vector(1),
         qkv_rows,
-        vector(vec_one, 2),
-        vector(vec_one, 3),
+        vector(2),
+        vector(3),
         out_rows,
-        vector(vec_two, 2),
-        vector(vec_two, 0),
-        vector(vec_two, 1),
+        vector(6),
+        vector(4),
+        vector(5),
         up_rows,
-        vec_two[4 * width :],
+        vectors[8 * width :],
         down_rows,
-        vector(vec_two, 3),
+        vector(7),
     )
 
 

time: 640 us -> 568 us (0.89)
  waiting for transfers between devices: 126 us -> 51.9 us
  Pallas kernels: 360 us -> 393 us
  starting transfers between devices: 102 us -> 75.2 us
  between operations: 1.9 us -> 14.4 us
  local copies, waits for them, and re-layouts: 17.7 us -> 7.04 us
    ppermute x34 -> x14, waiting for transfers between devices: 126 us -> 42 us  [swap(): return lax.ppermute(block, axis, [(n, n ^ bit) for n in range(size)])]
    ppermute x34 -> x14, starting transfers between devices: 91.8 us -> 61.7 us  [swap(): return lax.ppermute(block, axis, [(n, n ^ bit) for n in range(size)])]
    pallas_call x1, Pallas kernels: 144 us -> 165 us  [mlp(): pl.pallas_call(functools.partial(mlp_kernel, 512, length), out_shape=(jax...]
    pallas_call x1, Pallas kernels: 15.7 us -> 30.3 us  [qkv_grad(): pl.pallas_call(qkv_grad_kernel, out_shape=(jax.ShapeDtypeStruct((BLOCKS,...]
    all_to_all x2, waiting for transfers between devices: 0.01 us -> 9.95 us  [exchange(): return lax.all_to_all(flat, 'bal', split_axis=0, concat_axis=0, tiled=True)]
    dynamic_slice x4 -> x0, local copies, waits for them, and re-layouts: 7.22 us -> none  [summed_rows(): send = lax.dynamic_slice(matrix, (0, (1 - mine) * half), (rows, half))]
    pallas_call x4 -> x2, Pallas kernels: 67.4 us -> 62.1 us  [attend_back(): pl.pallas_call(functools.partial(attend_back_kernel, first, per), out_sha...]
  transfers between devices with their start and end apart: 36 -> 17, of which waited for: 11 -> 10; matrix products, arithmetic and copies ran while one was open for 5% -> 4% of each run, Pallas kernels for 33% -> 38%
where the time goes in v3:
time: 568 us; the launch traced here: 565 us
  Pallas kernels  393 us (69%)
  starting transfers between devices  75.2 us (13%)
  waiting for transfers between devices  51.9 us (9%)
  other arithmetic  16 us (3%)
  between operations  14.4 us (3%)
  blocking collectives  7.93 us (1%)
  local copies, waits for them, and re-layouts  7.04 us (1%)
    pallas_call x1, Pallas kernels, mlp(): pl.pallas_call(functools.partial(mlp_kernel, 512, length), out_shape=(jax...  165 us
    pallas_call x1, Pallas kernels, first_half(): pl.pallas_call(attend_kernel, out_shape=(jax.ShapeDtypeStruct((total, wid...  98.2 us
    pallas_call x2, Pallas kernels, attend_back(): pl.pallas_call(functools.partial(attend_back_kernel, first, per), out_sha...  62.1 us
    ppermute x14, starting transfers between devices, swap(): return lax.ppermute(block, axis, [(n, n ^ bit) for n in range(size)])  61.7 us
    ppermute x14, waiting for transfers between devices, swap(): return lax.ppermute(block, axis, [(n, n ^ bit) for n in range(size)])  42 us
    pallas_call x1, Pallas kernels, qkv_grad(): pl.pallas_call(qkv_grad_kernel, out_shape=(jax.ShapeDtypeStruct((BLOCKS,...  30.3 us
    pallas_call x1, Pallas kernels, token_grad(): pl.pallas_call(token_grad_kernel, out_shape=(jax.ShapeDtypeStruct((steps,...  20 us
    all_to_all x2, starting transfers between devices, exchange(): return lax.all_to_all(flat, 'bal', split_axis=0, concat_axis=0, tiled=True)  13.5 us
  transfers between devices with their start and end apart: 17, of which 10 were waited for; matrix products, arithmetic and copies ran while one was open for 4% of the time, Pallas kernels for 38%

profile of v3, /device:TPU:0, one launch (start us, length us, event | category | flops | bytes accessed | tf_op | source)
XLA Modules:
  0.0 565.5 jit_solution(5297227564233319227)
XLA Ops:
  7.2 7.9 %all-gather.1.every = s32[4,4,4]{2,1,0:T(4,128)} all-gather(s32[1,4,4]{2,1,0:T(4,128)} %bitcast.39), channel_id=2, replica_groups=mesh['dp'=8,'bal'=4] {'bal'}, dimensions={0}, use_global_device_ids=true | all-gather | bytes 320 | tf_op jit(solution)/shard_map/all_gather | solution.py:1067
  15.1 9.8 %shard_map.307 = (s32[128]{0:T(128)}, s32[16]{0:T(128)}, f32[16,768]{1,0:T(8,128)}, bf16[4,4,232,768]{3,2,1,0:T(8,128)(2,1)}) custom-call(s32[4,4,4]{2,1,0:T(4,128)} %all-gather.1.every, s32[4,4]{1,0:T(4,128)} %counts.1, s32[4,4]{1,0:T(4,128)} %present.1, s32[4,4]{1,0:T(4,128)} %slots.1, s32[1]{0:T(128)} %bitcast.1.me, bf16[4,225,4,768]{3,2,1,0:T(4,128)(2,1)} %bitcast.34, ...), custom_call_target="tpu_custom_call" | custom-call | tf_op jit(solution)/shard_map/pallas_call | solution.py:663
  25.0 5.1 all-to-all-start
  30.1 0.5 multiply_exponential_fusion.slopes
  30.6 98.2 %shard_map.308 = (bf16[4096,768]{1,0:T(8,128)(2,1)}, bf16[4096,2304]{1,0:T(8,128)(2,1)}, bf16[4096,768]{1,0:T(8,128)(2,1)}, f32[16,6,8,256]{3,2,1,0:T(8,128)}) custom-call(s32[128]{0:T(128)} %get-tuple-element.60.meta, f32[16]{0:T(128)} %multiply_exponential_fusion.slopes, bf16[4,225,4,768]{3,2,1,0:T(4,128)(2,1)} %bitcast.40, s32[4,4,225]{2,1,0:T(4,128)} %rows_in.5, ...), custom_call_target="tpu_custom_call" | custom-call | flops 40000000000 | bytes 4000000 | tf_op jit(solution)/shard_map/pallas_call | solution.py:706
  128.8 165.3 %shard_map.309 = (bf16[16,232,768]{2,1,0:T(8,128)(2,1)}, f32[4096,768]{1,0:T(8,128)}, bf16[4096,768]{1,0:T(8,128)(2,1)}, bf16[8,432,768]{2,1,0:T(8,128)(2,1)}, b...) custom-call(s32[128]{0:T(128)} %get-tuple-element.60.meta, bf16[16,232,768]{2,1,0:T(8,128)(2,1)} %bitcast.4.cot_in, ...), custom_call_target="tpu_custom_call" | custom-call | flops 109999996928 | bytes 11000000 | tf_op jit(solution)/shard_map/pallas_call | solution.py:766
  294.2 0.1 collective-permute-start
  294.3 14.1 %shard_map.310.rest_0_ = bf16[4096,2304]{1,0:T(8,128)(2,1)} custom-call(s32[128]{0:T(128)} %get-tuple-element.60.meta, f32[16]{0:T(128)} %multiply_exponential_fusion.slopes, bf16[4096,2304]{1,0:T(8,128)(2,1)} %get-tuple-element.48.qkv, bf16[4096,768]{1,0:T(8,128)(2,1)} %get-tuple-element.49.att_grad, f32[16,6,8,256]{3,2,1,0:T(8,128)} %get-tuple-element.50.totals, ...), custom_call_target="tpu_custom_call" | custom-call | flops 15000000512 | bytes 1500000 | tf_op jit(solution)/shard_map/pallas_call | solution.py:841
  308.3 8.4 %all-to-all-start.1 = ((bf16[4,928,768]{2,1,0:T(8,128)(2,1)}), bf16[4,928,768]{2,1,0:T(8,128)(2,1)}, u32[]{:S(2)}, u32[]{:S(2)}) async-start(bf16[4,928,768]{2,1,0:T(8,128)(2,1)} %bitcast.31), calls=%async_computation.1 | async-start | bytes 11403264 | tf_op jit(solution)/shard_map/all_to_all | solution.py:1061
  316.7 7.8 %add_convert_fusion = bf16[8,432,768]{2,1,0:T(8,128)(2,1)} fusion(bf16[8,432,768]{2,1,0:T(8,128)(2,1)} %collective-permute-done, bf16[8,432,768]{2,1,0:T(8,128)(2,1)} %get-tuple-element.51), kind=kLoop, calls=%fused_computation | loop fusion | flops 10616832 | bytes 15925248 | tf_op jit(solution)/shard_map/convert_element_type | solution.py:959
  324.5 48.0 %shard_map.311.packed_grad = bf16[4096,2304]{1,0:T(8,128)(2,1)} custom-call(s32[128]{0:T(128)} %get-tuple-element.60.meta, f32[16]{0:T(128)} %multiply_exponential_fusion.slopes, bf16[4096,2304]{1,0:T(8,128)(2,1)} %get-tuple-element.48.qkv, bf16[4096,768]{1,0:T(8,128)(2,1)} %get-tuple-element.49.att_grad, ...), custom_call_target="tpu_custom_call", output_to_operand_aliasing={{}: (7, {})} | custom-call | flops 499999997952 | bytes 50000000 | tf_op jit(solution)/shard_map/pallas_call | solution.py:841
  372.6 10.0 %all-to-all-done.1 = bf16[4,928,768]{2,1,0:T(8,128)(2,1)} async-done(((bf16[4,928,768]{2,1,0:T(8,128)(2,1)}), bf16[4,928,768]{2,1,0:T(8,128)(2,1)}, u32[]{:S(2)}, u32[]{:S(2)}) %all-to-all-start.1) | async-done | bytes 5701664 | tf_op jit(solution)/shard_map/all_to_all | solution.py:1061
  382.5 30.3 %shard_map.312 = (bf16[8,144,768]{2,1,0:T(8,128)(2,1)}, bf16[8,144,768]{2,1,0:T(8,128)(2,1)}, f32[8,2304]{1,0:T(8,128)}) custom-call(s32[128]{0:T(128)} %get-tuple-element.60.meta, bf16[4096,2304]{1,0:T(8,128)(2,1)} %shard_map.311.packed_grad, bf16[4096,768]{1,0:T(8,128)(2,1)} %get-tuple-element.46.tokens_in.tokens, f32[16,768]{1,0:T(8,128)} %get-tuple-element.44.vecs), custom_call_target="tpu_custom_call" | custom-call | flops 15000000512 | bytes 1500000 | tf_op jit(solution)/shard_map/pallas_call | solution.py:879
  413.0 0.6 reshape.77
  413.6 0.9 slice.88
  414.5 7.2 %shard_map.313 = bf16[4,225,4,768]{3,2,1,0:T(4,128)(2,1)} custom-call(s32[16]{0:T(128)} %get-tuple-element.57.take, bf16[4,4,232,768]{3,2,1,0:T(8,128)(2,1)} %bitcast.7.got), custom_call_target="tpu_custom_call" | custom-call | tf_op jit(solution)/shard_map/pallas_call | solution.py:687
  421.7 1.4 slice_reduce_fusion
  423.1 1.9 add_convert_fusion.1
  425.1 5.2 collective-permute-start.7
  430.2 20.0 %shard_map.314 = (f32[4,225,4,768]{3,2,1,0:T(4,128)}, f32[8,768]{1,0:T(8,128)}) custom-call(s32[128]{0:T(128)} %get-tuple-element.60.meta, bf16[4096,2304]{1,0:T(8,128)(2,1)} %shard_map.311.packed_grad, bf16[4096,768]{1,0:T(8,128)(2,1)} %get-tuple-element.46.tokens_in.tokens, f32[4096,768]{1,0:T(8,128)} %get-tuple-element.61.mid_grad, ...), custom_call_target="tpu_custom_call" | custom-call | flops 20000000000 | bytes 2000000 | tf_op jit(solution)/shard_map/pallas_call | solution.py:913
  450.2 1.3 slice.84
  451.5 1.3 reshape.76
  452.8 3.7 collective-permute-done.7
  456.5 0.2 fusion
  456.8 26.2 %collective-permute-start.8 = (bf16[2,144,768]{2,1,0:T(8,128)(2,1)S(1)}, bf16[2,144,768]{2,1,0:T(8,128)(2,1)S(1)}, u32[]{:S(2)}, u32[]{:S(2)}) collective-permute-start(bf16[2,144,768]{2,1,0:T(8,128)(2,1)S(1)} %dynamic-slice_bitcast_fusion.1), channel_id=1, source_target_pairs={{0,8},{4,12},{8,0},{12,4},{16,24},{20,28},{24,16},{28,20},{1,9},{5... | collective-permute-start | bytes 1327112 | tf_op jit(solution)/shard_map/ppermute | solution.py:951
  483.1 7.8 %collective-permute-done.8 = bf16[2,144,768]{2,1,0:T(8,128)(2,1)S(1)} collective-permute-done((bf16[2,144,768]{2,1,0:T(8,128)(2,1)S(1)}, bf16[2,144,768]{2,1,0:T(8,128)(2,1)S(1)}, u32[]{:S(2)}, u32[]{:S(2)}) %collective-permute-start.8) | collective-permute-done | bytes 442400 | tf_op jit(solution)/shard_map/ppermute | solution.py:951
  490.9 0.1 fusion.1
  491.1 24.5 %collective-permute-start.9 = (bf16[1,144,768]{2,1,0:T(8,128)(2,1)S(1)}, bf16[1,144,768]{2,1,0:T(8,128)(2,1)S(1)}, u32[]{:S(2)}, u32[]{:S(2)}) collective-permute-start(bf16[1,144,768]{2,1,0:T(8,128)(2,1)S(1)} %constant_dynamic-slice_fusion), channel_id=1, source_target_pairs={{0,16},{4,20},{8,24},{12,28},{16,0},{20,4},{24,8},{28,12},{1,17},{... | collective-permute-start | bytes 663560 | tf_op jit(solution)/shard_map/ppermute | solution.py:951
  515.5 1.2 collective-permute-done.2
  516.8 3.9 collective-permute-done.3
  520.7 1.2 collective-permute-start.4
  521.9 2.8 collective-permute-done.4
  524.7 1.7 collective-permute-start.5
  526.4 2.2 collective-permute-done.5
  528.7 0.1 collective-permute-start.6
  528.7 4.8 collective-permute-done.6
  533.5 0.6 slice.131
  534.2 2.1 collective-permute-start.10
  536.3 0.6 fusion.7
  536.9 14.8 %collective-permute-done.10 = bf16[144,768]{1,0:T(8,128)(2,1)S(1)} collective-permute-done((bf16[144,768]{1,0:T(8,128)(2,1)S(1)}, bf16[144,768]{1,0:T(8,128)(2,1)S(1)}, u32[]{:S(2)}, u32[]{:S(2)}) %collective-permute-start.10) | collective-permute-done | bytes 221216 | tf_op jit(solution)/shard_map/ppermute | solution.py:951
  551.9 1.3 add_convert_fusion.2
  553.2 0.6 collective-permute-start.13
  553.8 1.0 maximum_convert_fusion.2
  554.8 0.7 collective-permute-done.13
  555.5 0.1 broadcast_select_fusion.1
  555.7 1.1 maximum_convert_fusion.1
  556.8 0.7 maximum_convert_fusion.3
  557.5 1.1 maximum_convert_fusion
  (50 shorter events, 0.7 us)
Async XLA Ops:
  25.0 103.9 %all-to-all-start = ((bf16[4,928,768]{2,1,0:T(8,128)(2,1)}), bf16[4,928,768]{2,1,0:T(8,128)(2,1)}, u32[]{:S(2)}, u32[]{:S(2)}) async-start(bf16[4,928,768]{2,1,0:T(8,128)(2,1)} %bitcast.32), calls=%async_computation | async-start | bytes 11403264 | tf_op jit(solution)/shard_map/all_to_all | solution.py:1061
  294.2 22.5 %collective-permute-start = (bf16[8,432,768]{2,1,0:T(8,128)(2,1)}, bf16[8,432,768]{2,1,0:T(8,128)(2,1)}, u32[]{:S(2)}, u32[]{:S(2)}) collective-permute-start(bf16[8,432,768]{2,1,0:T(8,128)(2,1)} %get-tuple-element.52), channel_id=1, source_target_pairs={{0,1},{1,0},{2,3},{3,2},{4,5},{5,4},{6,7},{7,6},{8,9},{9,8},{10,11... | collective-permute-start | bytes 15925256 | tf_op jit(solution)/shard_map/ppermute | solution.py:951
  308.3 74.2 %all-to-all-start.1 = ((bf16[4,928,768]{2,1,0:T(8,128)(2,1)}), bf16[4,928,768]{2,1,0:T(8,128)(2,1)}, u32[]{:S(2)}, u32[]{:S(2)}) async-start(bf16[4,928,768]{2,1,0:T(8,128)(2,1)} %bitcast.31), calls=%async_computation.1 | async-start | bytes 11403264 | tf_op jit(solution)/shard_map/all_to_all | solution.py:1061
  316.7 217.4 %reduce-scatter.2.cloned.1.call-start = ((), (), s32[]{:S(2)}) async-start(), calls=%async_computation.3 | async-start | bytes 5971968 | tf_op jit(solution)/shard_map/reduce_scatter | solution.py:1094
  372.6 40.5 %copy-start.5 = (f32[8,768]{1,0:T(8,128)S(1)}, f32[8,768]{1,0:T(8,128)}, u32[]{:S(2)}) copy-start(f32[8,768]{1,0:T(8,128)} %get-tuple-element.65) | copy-start | bytes 73732
  412.8 10.2 %collective-permute-start.1 = (bf16[8,144,768]{2,1,0:T(8,128)(2,1)}, bf16[8,144,768]{2,1,0:T(8,128)(2,1)}, u32[]{:S(2)}, u32[]{:S(2)}) collective-permute-start(bf16[8,144,768]{2,1,0:T(8,128)(2,1)} %get-tuple-element.59), channel_id=1, source_target_pairs={{0,1},{1,0},{2,3},{3,2},{4,5},{5,4},{6,7},{7,6},{8,9},{9,8},{10,11... | collective-permute-start | bytes 5308424 | tf_op jit(solution)/shard_map/ppermute | solution.py:951
  414.5 8.5 %copy-start = (bf16[8,144,768]{2,1,0:T(8,128)(2,1)S(1)}, bf16[8,144,768]{2,1,0:T(8,128)(2,1)}, u32[]{:S(2)}) copy-start(bf16[8,144,768]{2,1,0:T(8,128)(2,1)} %get-tuple-element.56) | copy-start | bytes 5308420
  425.1 31.5 %collective-permute-start.7 = (bf16[4,144,768]{2,1,0:T(8,128)(2,1)S(1)}, bf16[4,144,768]{2,1,0:T(8,128)(2,1)S(1)}, u32[]{:S(2)}, u32[]{:S(2)}) collective-permute-start(bf16[4,144,768]{2,1,0:T(8,128)(2,1)S(1)} %dynamic-slice_bitcast_fusion), channel_id=1, source_target_pairs={{0,4},{4,0},{8,12},{12,8},{16,20},{20,16},{24,28},{28,24},{1,5},{5... | collective-permute-start | bytes 2654216 | tf_op jit(solution)/shard_map/ppermute | solution.py:951
  452.8 30.2 %copy-start.2 = (f32[9216]{0:T(1024)S(1)}, f32[9216]{0:T(1024)}, u32[]{:S(2)}) copy-start(f32[9216]{0:T(1024)} %custom-call) | copy-start | bytes 110596
  452.8 30.2 %copy-start.3 = (f32[1536]{0:T(1024)S(1)}, f32[1536]{0:T(1024)}, u32[]{:S(2)}) copy-start(f32[1536]{0:T(1024)} %reshape.76) | copy-start | bytes 18436
  452.8 30.2 %copy-start.4 = (f32[768]{0:T(1024)S(1)}, f32[768]{0:T(1024)}, u32[]{:S(2)}) copy-start(f32[768]{0:T(1024)} %get-tuple-element.68) | copy-start | bytes 9220
  452.8 30.3 %copy-start.1 = (f32[3072]{0:T(1024)S(1)}, f32[3072]{0:T(1024)}, u32[]{:S(2)}) copy-start(f32[3072]{0:T(1024)} %reshape.77) | copy-start | bytes 36868
  456.8 34.1 %collective-permute-start.8 = (bf16[2,144,768]{2,1,0:T(8,128)(2,1)S(1)}, bf16[2,144,768]{2,1,0:T(8,128)(2,1)S(1)}, u32[]{:S(2)}, u32[]{:S(2)}) collective-permute-start(bf16[2,144,768]{2,1,0:T(8,128)(2,1)S(1)} %dynamic-slice_bitcast_fusion.1), channel_id=1, source_target_pairs={{0,8},{4,12},{8,0},{12,4},{16,24},{20,28},{24,16},{28,20},{1,9},{5... | collective-permute-start | bytes 1327112 | tf_op jit(solution)/shard_map/ppermute | solution.py:951
  491.1 43.1 %collective-permute-start.9 = (bf16[1,144,768]{2,1,0:T(8,128)(2,1)S(1)}, bf16[1,144,768]{2,1,0:T(8,128)(2,1)S(1)}, u32[]{:S(2)}, u32[]{:S(2)}) collective-permute-start(bf16[1,144,768]{2,1,0:T(8,128)(2,1)S(1)} %constant_dynamic-slice_fusion), channel_id=1, source_target_pairs={{0,16},{4,20},{8,24},{12,28},{16,0},{20,4},{24,8},{28,12},{1,17},{... | collective-permute-start | bytes 663560 | tf_op jit(solution)/shard_map/ppermute | solution.py:951
  515.5 1.2 collective-permute-start.2
  516.8 4.0 collective-permute-start.3
  520.7 4.0 collective-permute-start.4
  524.7 4.0 collective-permute-start.5
  528.7 4.9 collective-permute-start.6
  534.1 17.8 %collective-permute-start.12 = (bf16[432,768]{1,0:T(8,128)(2,1)}, bf16[432,768]{1,0:T(8,128)(2,1)S(1)}, u32[]{:S(2)}, u32[]{:S(2)}) collective-permute-start(bf16[432,768]{1,0:T(8,128)(2,1)} %bitcast.37), channel_id=1, source_target_pairs={{0,2},{1,3},{2,0},{3,1},{4,6},{5,7},{6,4},{7,5},{8,10},{9,11},{10,... | collective-permute-start | bytes 1990664 | tf_op jit(solution)/shard_map/ppermute | solution.py:951
  534.2 17.5 %collective-permute-start.10 = (bf16[144,768]{1,0:T(8,128)(2,1)S(1)}, bf16[144,768]{1,0:T(8,128)(2,1)S(1)}, u32[]{:S(2)}, u32[]{:S(2)}) collective-permute-start(bf16[144,768]{1,0:T(8,128)(2,1)S(1)} %fusion.2), channel_id=1, source_target_pairs={{0,2},{1,3},{2,0},{3,1},{4,6},{5,7},{6,4},{7,5},{8,10},{9,11},{10,... | collective-permute-start | bytes 663560 | tf_op jit(solution)/shard_map/ppermute | solution.py:951
  551.8 1.9 collective-permute-start.11
  553.2 2.3 collective-permute-start.13
Sparse Core Ops, SparseCore 0:
  324.6 130.1 reduce-scatter.1
